TPU v7x, 1024 devices: a whole 4x4x32 slice. The times are simulated.
1024 devices in a mesh: dp: 16 (over z_lo), ctx: 4 (over x), ep: 16 (over z_hi, y, core).
Axes of the slice: x: 4, y: 4, z: 32 (z_hi: 2, z_lo: 16; z = z_hi * 16 + z_lo), core: 2. Of those that a mesh axis runs over, the one named last changes fastest.
Arguments:
- tokens: bfloat16 [32768, 4096], P(('dp', 'ep'), 'ctx'), may hold values from -24 to 24
- routes: int32 [32768, 1], P(('dp', 'ep')), may hold values from 0 to 15; in each aligned block of 128 rows (0 to 127, 128 to 255, ...) at most 10 rows name the same one
- router_weight: float32 [4096, 16], replicated, may hold values from -0.09375 to 0.09375
- gate_weight: bfloat16 [16, 4096, 1024], P('ep', 'ctx'), may hold values from -0.09375 to 0.09375
- up_weight: bfloat16 [16, 4096, 1024], P('ep', 'ctx'), may hold values from -0.09375 to 0.09375
- down_weight: bfloat16 [16, 1024, 4096], P('ep', None, 'ctx'), may hold values from -0.1875 to 0.1875
- cotangent: bfloat16 [32768, 4096], P(('dp', 'ep'), 'ctx'), may hold values from -0.03125 to 0.03125
Outputs:
- block_out: bfloat16 [32768, 4096], P(('dp', 'ep'), 'ctx')
- router_grad: float32 [4096, 16], P('ctx')
Inputs may be any that keep to these rules, and one draw needn't show every extreme that they name: `routes`: within each aligned block of 128 rows no expert is named by more than 10 rows, a bound that some block reaches.
All inputs are finite; a program needn't handle non-finite values.
Results may differ from a plain program's by a relative error of at most 0.023.
Values may be sent and summed in bfloat16 or wider, within the bound.
No kernel may reach another device: no remote copies, remote signals or barrier semaphores. Data moves between devices by JAX's collectives and lax.ppermute only.
A program may use at most 32 MiB of HBM per device.

v0:
```python
import jax
import jax.numpy as jnp
from jax import lax
from jax.sharding import PartitionSpec as P


def shards(tokens, routes, router_weight, gate_weight, up_weight, down_weight, cotangent):
    n_experts = lax.axis_size("ep")
    tok_count = tokens.shape[0]
    slice_width = tokens.shape[1]
    capacity = 5 * tok_count // (4 * n_experts)
    route = routes[:, 0]
    expert_ids = jnp.arange(n_experts, dtype=jnp.int32)
    onehot_int = (route[:, None] == expert_ids[None, :]).astype(jnp.int32)
    earlier = jnp.cumsum(onehot_int, axis=0) - onehot_int
    position = jnp.sum(earlier * onehot_int, axis=1)
    slot = route * capacity + position
    slot_ids = jnp.arange(n_experts * capacity, dtype=jnp.int32)
    placement = (slot[None, :] == slot_ids[:, None]).astype(jnp.bfloat16)
    outgoing = jnp.dot(placement, tokens, preferred_element_type=jnp.float32).astype(jnp.bfloat16)
    received = lax.all_to_all(outgoing, "ep", split_axis=0, concat_axis=0, tiled=True)
    gate_sum = jnp.dot(received, gate_weight[0], preferred_element_type=jnp.float32)
    up_sum = jnp.dot(received, up_weight[0], preferred_element_type=jnp.float32)
    gate_share, up_share = (
        lax.psum_scatter(
            gate_sum.astype(jnp.bfloat16), "ctx", scatter_dimension=1, tiled=True
        ).astype(jnp.float32),
        lax.psum_scatter(
            up_sum.astype(jnp.bfloat16), "ctx", scatter_dimension=1, tiled=True
        ).astype(jnp.float32),
    )
    hidden_share = (jax.nn.silu(gate_share) * up_share).astype(jnp.bfloat16)
    weight_rows = down_weight[0]
    down_sum = jnp.dot(
        lax.all_gather(hidden_share, "ctx", axis=1, tiled=True),
        weight_rows,
        preferred_element_type=jnp.float32,
    )
    expert_out = down_sum.astype(jnp.bfloat16)
    returned = lax.all_to_all(expert_out, "ep", split_axis=0, concat_axis=0, tiled=True)
    values = jnp.take(returned, slot, axis=0).astype(jnp.float32)
    tok_float = tokens.astype(jnp.float32)
    router_rows = lax.dynamic_slice_in_dim(
        router_weight, lax.axis_index("ctx") * slice_width, slice_width, 0
    )
    logit_part = jnp.dot(tok_float, router_rows, precision=lax.Precision.HIGHEST)
    inner_part = jnp.sum(cotangent.astype(jnp.float32) * values, axis=1)
    logits, inner = lax.psum((logit_part, inner_part), "ctx")
    onehot = onehot_int.astype(jnp.float32)
    score = jax.nn.sigmoid(jnp.sum(logits * onehot, axis=1))
    block_out = (score[:, None] * values).astype(jnp.bfloat16)
    slope = inner * score * (1.0 - score)
    coefs = onehot * slope[:, None]
    router_term = jnp.dot(tok_float.T, coefs, precision=lax.Precision.HIGHEST)
    router_grad = lax.psum(router_term, ("dp", "ep"))
    return (block_out, router_grad)


def solution(mesh):
    return jax.shard_map(
        shards,
        mesh=mesh,
        in_specs=(
            P(("dp", "ep"), "ctx"),
            P(("dp", "ep"), None),
            P(),
            P("ep", "ctx", None),
            P("ep", "ctx", None),
            P("ep", None, "ctx"),
            P(("dp", "ep"), "ctx"),
        ),
        out_specs=(P(("dp", "ep"), "ctx"), P("ctx", None)),
        check_vma=False,
    )
```

profile of v0, /device:TPU:1, one launch (start us, length us, event | category | flops | bytes accessed | tf_op | source)
XLA Modules:
  0.0 882.5 jit_solution(8072480952910424190)
XLA Ops:
  7.2 0.0 reduce-scatter.3.cloned.1.call-start
  7.2 0.8 fusion.27
  8.0 0.1 copy.11
  8.1 0.2 reduce_window_sum.11
  8.3 0.1 copy.12
  8.4 0.7 select_reduce_fusion
  9.1 0.7 multiply_add_fusion
  9.7 1.2 convolution_convert_fusion
  10.9 0.1 all_to_all.16
  11.0 62.0 %all_to_all.24 = bf16[16,10,1024]{2,1,0:T(8,128)(2,1)S(1)} all-to-all(bf16[16,10,1024]{2,1,0:T(8,128)(2,1)S(1)} %all_to_all.16), channel_id=1, replica_groups=mesh['dp'=16,'ctx'=4,'ep'=16] {'ep'}, dimensions={0} | all-to-all | bytes 655360 | tf_op jit(solution)/shard_map/all_to_all | solution.py:21
  73.0 0.1 all_to_all.18
  73.2 1.2 fusion.6
  74.4 0.0 reduce-scatter.5.cloned.1.call-start
  74.5 2.8 fusion.9
  77.3 57.3 %reduce-scatter.3.cloned.1.call-done = bf16[160,256]{1,0:T(8,128)(2,1)} async-done(((bf16[160,1024]{1,0:T(8,128)(2,1)}), bf16[160,256]{1,0:T(8,128)(2,1)}) %reduce-scatter.3.cloned.1.call-update) | async-done | bytes 81936 | tf_op jit(solution)/shard_map/reduce_scatter | solution.py:25
  134.7 42.0 %reduce-scatter.5.cloned.1.call-done = bf16[160,256]{1,0:T(8,128)(2,1)} async-done(((bf16[160,1024]{1,0:T(8,128)(2,1)}), bf16[160,256]{1,0:T(8,128)(2,1)}) %reduce-scatter.5.cloned.1.call-update) | async-done | bytes 81936 | tf_op jit(solution)/shard_map/reduce_scatter | solution.py:28
  176.7 1.0 fusion.21
  177.7 9.5 %all_gather.3 = bf16[160,1024]{1,0:T(8,128)(2,1)S(1)} all-gather(bf16[160,256]{1,0:T(8,128)(2,1)S(1)} %fusion.21), channel_id=1, replica_groups=mesh['dp'=16,'ctx'=4,'ep'=16] {'ctx'}, dimensions={1}, use_global_device_ids=true | all-gather | bytes 409600 | tf_op jit(solution)/shard_map/all_gather | solution.py:35
  187.2 2.1 fusion.12
  189.3 0.9 all_to_all.19
  190.2 30.5 %all-to-all-start.1 = ((bf16[16,10,1024]{2,1,0:T(8,128)(2,1)}), bf16[16,10,1024]{2,1,0:T(8,128)(2,1)S(1)}, u32[]{:S(2)}, u32[]{:S(2)}) async-start(bf16[16,10,1024]{2,1,0:T(8,128)(2,1)} %all_to_all.19), calls=%async_computation.3 | async-start | bytes 1048576 | tf_op jit(solution)/shard_map/all_to_all | solution.py:40
  220.8 0.0 all-reduce.3.cloned.1.call-start
  220.9 1.1 convolution_bitcast_fusion.1
  222.0 44.1 %all-to-all-done.1 = bf16[16,10,1024]{2,1,0:T(8,128)(2,1)S(1)} async-done(((bf16[16,10,1024]{2,1,0:T(8,128)(2,1)}), bf16[16,10,1024]{2,1,0:T(8,128)(2,1)S(1)}, u32[]{:S(2)}, u32[]{:S(2)}) %all-to-all-start.1) | async-done | bytes 327712 | tf_op jit(solution)/shard_map/all_to_all | solution.py:40
  266.1 0.1 all_to_all.21
  266.3 0.9 gather_fusion
  267.1 0.2 fusion.16
  267.4 7.1 all-reduce
  274.5 0.9 convolution_bitcast_fusion
  275.4 0.9 fusion.15
  276.3 598.2 %all-reduce.3.cloned.1.call-done = f32[1024,16]{0,1:T(8,128)} async-done(((f32[1024,16]{0,1:T(8,128)}), f32[1024,16]{0,1:T(8,128)}) %all-reduce.3.cloned.1.call-update) | async-done | bytes 65552 | tf_op jit(solution)/shard_map/psum | solution.py:55
  874.5 1.5 copy.14
  (15 shorter events, 0.1 us)
Async XLA Ops:
  7.2 66.0 %copy-start = (bf16[1,1024,1024]{2,1,0:T(8,128)(2,1)S(1)}, bf16[1,1024,1024]{2,1,0:T(8,128)(2,1)}, u32[]{:S(2)}) copy-start(bf16[1,1024,1024]{2,1,0:T(8,128)(2,1)} %param.10) | copy-start | bytes 6291460
  7.2 127.5 %reduce-scatter.3.cloned.1.call-start = ((), (), s32[]{:S(2)}) async-start(), calls=%async_computation.4 | async-start | bytes 409600 | tf_op jit(solution)/shard_map/reduce_scatter | solution.py:25
  74.4 102.2 %reduce-scatter.5.cloned.1.call-start = ((), (), s32[]{:S(2)}) async-start(), calls=%async_computation.5 | async-start | bytes 409600 | tf_op jit(solution)/shard_map/reduce_scatter | solution.py:28
  187.2 33.7 %copy-start.3 = (s32[128,1]{0,1:T(1,128)S(1)}, s32[128,1]{0,1:T(1,128)}, u32[]{:S(2)}) copy-start(s32[128,1]{0,1:T(1,128)} %param.8) | copy-start | bytes 1540
  187.2 33.7 %copy-start.1 = (bf16[128,1024]{1,0:T(8,128)(2,1)S(1)}, bf16[128,1024]{1,0:T(8,128)(2,1)}, u32[]{:S(2)}) copy-start(bf16[128,1024]{1,0:T(8,128)(2,1)} %param.7) | copy-start | bytes 786436
  190.2 76.9 %copy-start.2 = (bf16[128,1024]{1,0:T(8,128)(2,1)S(1)}, bf16[128,1024]{1,0:T(8,128)(2,1)}, u32[]{:S(2)}) copy-start(bf16[128,1024]{1,0:T(8,128)(2,1)} %param.13) | copy-start | bytes 786436
  190.2 75.9 %all-to-all-start.1 = ((bf16[16,10,1024]{2,1,0:T(8,128)(2,1)}), bf16[16,10,1024]{2,1,0:T(8,128)(2,1)S(1)}, u32[]{:S(2)}, u32[]{:S(2)}) async-start(bf16[16,10,1024]{2,1,0:T(8,128)(2,1)} %all_to_all.19), calls=%async_computation.3 | async-start | bytes 1048576 | tf_op jit(solution)/shard_map/all_to_all | solution.py:40
  220.8 653.7 %all-reduce.3.cloned.1.call-start = ((), (), s32[]{:S(2)}) async-start(), calls=%async_computation.6 | async-start | bytes 131072 | tf_op jit(solution)/shard_map/psum | solution.py:55
Sparse Core Ops, SparseCore 0:
  74.5 60.0 reduce-scatter.2
  138.1 38.5 reduce-scatter.4
  275.6 598.8 all-reduce.2
where the time goes:
time: 883 us; the launch traced here: 882 us
  waiting for transfers between devices  742 us (84%)
  blocking collectives  78.7 us (9%)
  starting transfers between devices  30.7 us (3%)
  between operations  13.8 us (2%)
  matrix products  9.39 us (1%)
    psum x1, waiting for transfers between devices, shards(): router_grad = lax.psum(router_term, ('dp', 'ep'))  598 us
    all_to_all x1, blocking collectives, shards(): lax.all_to_all(outgoing, 'ep', split_axis=0, concat_axis=0, tiled=True)  62 us
    reduce_scatter x1, waiting for transfers between devices, shards(): lax.psum_scatter(gate_sum.astype(jnp.bfloat16), 'ctx', scatter_dimension=...  57.3 us
    all_to_all x1, waiting for transfers between devices, shards(): lax.all_to_all(expert_out, 'ep', split_axis=0, concat_axis=0, tiled=True)  44.1 us
    reduce_scatter x1, waiting for transfers between devices, shards(): lax.psum_scatter(up_sum.astype(jnp.bfloat16), 'ctx', scatter_dimension=1,...  42 us
    all_to_all x1, starting transfers between devices, shards(): lax.all_to_all(expert_out, 'ep', split_axis=0, concat_axis=0, tiled=True)  30.5 us
  transfers between devices with their start and end apart: 4, of which 4 were waited for; matrix products, arithmetic and copies ran while one was open for 1% of the time, Pallas kernels for 0%

commit v1 on v0

v1 whole, which is shorter than its diff:
```python
import jax
import jax.numpy as jnp
from jax import lax
from jax.sharding import Mesh, PartitionSpec as P

BF16 = jnp.bfloat16
F32 = jnp.float32
N_EP = 16
N_CTX = 4
ROUTE = ("dh", "zh", "y", "core")
ALL_Z = ("dh", "dl", "zh")
IN_Z = ("y", "core")


def route_groups():
    groups = []
    for flip in (0, 1):
        groups.append([(((e >> 3) ^ flip) * 2 + (e >> 3)) * 8 + (e & 7) for e in range(N_EP)])
    return groups


def split(v, parts):
    out = []
    for _ in range(parts):
        p = v.astype(BF16)
        out.append(p)
        v = v - p.astype(F32)
    return jnp.stack(out, axis=-1)


def dot(a, b, dims=((1,), (0,))):
    return lax.dot_general(a, b, (dims, ((), ())), preferred_element_type=F32)


def shards(tokens, routes, router_weight, gate_weight, up_weight, down_weight, cotangent):
    tok_count, width = tokens.shape
    capacity = 5 * tok_count // (4 * N_EP)
    rows = N_EP * capacity
    groups = route_groups()
    expert = lax.axis_index("zh") * 8 + lax.axis_index("y") * 2 + lax.axis_index("core")
    route = routes[:, 0]
    expert_ids = jnp.arange(N_EP, dtype=jnp.int32)
    onehot = (route[:, None] == expert_ids[None, :]).astype(jnp.int32)
    earlier = jnp.cumsum(onehot, axis=0) - onehot
    position = jnp.sum(earlier * onehot, axis=1)
    slot = route * capacity + position
    slot_ids = jnp.arange(rows, dtype=jnp.int32)
    placement = (slot[None, :] == slot_ids[:, None]).astype(BF16)
    both = jnp.concatenate([tokens, cotangent], axis=1)
    outgoing = dot(placement, both).astype(BF16)
    received = lax.all_to_all(outgoing, ROUTE, 0, 0, axis_index_groups=groups, tiled=True)
    x, cot = received[:, :width], received[:, width:]

    router_rows = lax.dynamic_slice_in_dim(router_weight, lax.axis_index("ctx") * width, width, 0)
    router_col = lax.dynamic_slice_in_dim(router_rows, expert, 1, 1)[:, 0]
    gate_part = dot(x, gate_weight[0]).astype(BF16)
    up_part = dot(x, up_weight[0]).astype(BF16)
    back_part = dot(cot, down_weight[0], ((1,), (1,))).astype(BF16)
    logit_part = jnp.sum(dot(x, split(router_col, 3)), axis=1)
    small = jnp.pad(split(logit_part, 3), ((0, 0), (0, 125)))
    parts = jnp.concatenate([gate_part, up_part, back_part, small], axis=1)
    mine = lax.all_to_all(parts, "ctx", 0, 0, tiled=True)
    sums = jnp.sum(mine.reshape(N_CTX, rows // N_CTX, -1).astype(F32), axis=0)
    h = gate_part.shape[1]
    gate, up, back = sums[:, :h], sums[:, h : 2 * h], sums[:, 2 * h : 3 * h]
    logit = jnp.sum(sums[:, 3 * h :], axis=1)
    hidden = (jax.nn.silu(gate) * up).astype(BF16)
    inner = jnp.sum(hidden.astype(F32) * back, axis=1)
    score = jax.nn.sigmoid(logit)
    slope = inner * score * (1.0 - score)
    small = jnp.pad(jnp.concatenate([split(score, 3), split(slope, 3)], axis=1), ((0, 0), (0, 122)))
    full = lax.all_gather(jnp.concatenate([hidden, small], axis=1), "ctx", axis=0, tiled=True)
    values = dot(full[:, :h], down_weight[0]).astype(BF16).astype(F32)
    score = jnp.sum(full[:, h : h + 3].astype(F32), axis=1)
    block_rows = (score[:, None] * values).astype(BF16)
    grad = jnp.sum(dot(full[:, h + 3 : h + 6], x, ((0,), (0,))), axis=0)
    returned = lax.all_to_all(block_rows, ROUTE, 0, 0, axis_index_groups=groups, tiled=True)
    block_out = dot(placement, returned, ((0,), (0,))).astype(BF16)

    grads = lax.all_to_all(jnp.broadcast_to(grad.reshape(1, 8, -1), (32, 8, width // 8)), ALL_Z, 0, 0, tiled=True)
    grads = jnp.sum(grads.reshape(16, 2, 1, 8, -1), axis=0)
    grads = jnp.broadcast_to(grads.reshape(1, 16, -1), (8, 16, width // 8))
    grads = lax.all_to_all(grads, IN_Z, 0, 0, tiled=True)
    router_grad = grads.reshape(8, 2, width).transpose(2, 1, 0).reshape(width, N_EP)
    return (block_out, router_grad)


def solution(mesh):
    fine = Mesh(mesh.devices.reshape(2, 8, 4, 2, 4, 2), ("dh", "dl", "ctx", "zh", "y", "core"))
    tok = ("dh", "dl", "zh", "y", "core")
    ep = ("zh", "y", "core")
    return jax.shard_map(
        shards,
        mesh=fine,
        in_specs=(
            P(tok, "ctx"),
            P(tok, None),
            P(),
            P(ep, "ctx", None),
            P(ep, "ctx", None),
            P(ep, None, "ctx"),
            P(tok, "ctx"),
        ),
        out_specs=(P(tok, "ctx"), P("ctx", None)),
        check_vma=False,
    )
```

time: 883 us -> 277 us (0.31)
  the two profiles are of different devices: /device:TPU:1 before, /device:TPU:224 now
where the time goes in v1:
time: 277 us; the launch traced here: 276 us
  waiting for transfers between devices  185 us (67%)
  starting transfers between devices  41.3 us (15%)
  blocking collectives  31.2 us (11%)
  matrix products  6.93 us (3%)
  local copies, waits for them, and re-layouts  6.9 us (2%)
  other arithmetic  4.02 us (1%)
    all_to_all x1, waiting for transfers between devices, shards(): lax.all_to_all(outgoing, ROUTE, 0, 0, axis_index_groups=groups, tiled=True)  102 us
    all_to_all x1, waiting for transfers between devices, shards(): lax.all_to_all(block_rows, ROUTE, 0, 0, axis_index_groups=groups, tiled=T...  58.2 us
    all_to_all x1, waiting for transfers between devices, shards(): lax.all_to_all(jnp.broadcast_to(grad.reshape(1, 8, -1), (32, 8, width //...  20.2 us
    all_to_all x1, blocking collectives, shards(): mine = lax.all_to_all(parts, 'ctx', 0, 0, tiled=True)  18.7 us
    all_to_all x1, starting transfers between devices, shards(): lax.all_to_all(outgoing, ROUTE, 0, 0, axis_index_groups=groups, tiled=True)  17.7 us
    all_to_all x1, starting transfers between devices, shards(): lax.all_to_all(jnp.broadcast_to(grad.reshape(1, 8, -1), (32, 8, width //...  12.9 us
    all_gather x1, blocking collectives, shards(): lax.all_gather(jnp.concatenate([hidden, small], axis=1), 'ctx', axis=0, t...  12.5 us
    all_to_all x1, starting transfers between devices, shards(): lax.all_to_all(block_rows, ROUTE, 0, 0, axis_index_groups=groups, tiled=T...  7.13 us
  transfers between devices with their start and end apart: 4, of which 4 were waited for; matrix products, arithmetic and copies ran while one was open for 1% of the time, Pallas kernels for 0%

profile of v1, /device:TPU:224, one launch (start us, length us, event | category | flops | bytes accessed | tf_op | source)
XLA Modules:
  0.0 276.0 jit_solution(10313361472011359737)
XLA Ops:
  0.6 0.9 fusion.44
  1.5 0.2 reduce_window_sum.11
  1.7 0.8 select_reduce_fusion
  2.5 0.7 multiply_add_fusion
  3.2 1.3 convolution_convert_fusion
  4.6 1.2 all_to_all.28
  5.8 17.7 %all-to-all-start = ((bf16[16,10,2048]{2,1,0:T(8,128)(2,1)}), bf16[16,10,2048]{2,1,0:T(8,128)(2,1)}, u32[]{:S(2)}, u32[]{:S(2)}) async-start(bf16[16,10,2048]{2,1,0:T(8,128)(2,1)} %all_to_all.28), calls=%async_computation | async-start | bytes 2097152 | tf_op jit(solution)/shard_map/all_to_all | solution.py:51
  23.5 0.9 dynamic_slice.13
  24.3 0.8 fusion.59
  25.2 102.2 %all-to-all-done = bf16[16,10,2048]{2,1,0:T(8,128)(2,1)} async-done(((bf16[16,10,2048]{2,1,0:T(8,128)(2,1)}), bf16[16,10,2048]{2,1,0:T(8,128)(2,1)}, u32[]{:S(2)}, u32[]{:S(2)}) %all-to-all-start) | async-done | bytes 655392 | tf_op jit(solution)/shard_map/all_to_all | solution.py:51
  127.4 1.4 all_to_all.30
  128.8 0.2 convolution_reduce_fusion.1
  129.2 2.3 fusion.12
  131.5 0.8 fusion.15
  132.3 0.5 fusion.9
  132.9 18.7 %all_to_all.43 = bf16[4,40,3200]{2,1,0:T(8,128)(2,1)S(1)} all-to-all(bf16[4,40,3200]{2,1,0:T(8,128)(2,1)S(1)} %bitcast.60), channel_id=1, replica_groups=mesh['dh'=2,'dl'=8,'ctx'=4,'zh'=2,'y'=4,'core'=2] {'ctx'}, dimensions={0} | all-to-all | bytes 2048000 | tf_op jit(solution)/shard_map/all_to_all | solution.py:62
  151.7 0.1 convert_reduce_fusion
  151.9 0.2 fusion.41
  152.3 12.5 %all_gather.3 = bf16[160,1152]{1,0:T(8,128)(2,1)S(1)} all-gather(bf16[40,1152]{1,0:T(8,128)(2,1)S(1)} %fusion.43), channel_id=1, replica_groups=mesh['dh'=2,'dl'=8,'ctx'=4,'zh'=2,'y'=4,'core'=2] {'ctx'}, dimensions={0}, use_global_device_ids=true | all-gather | bytes 460800 | tf_op jit(solution)/shard_map/all_gather | solution.py:72
  164.8 0.3 convolution_reduce_fusion
  165.1 0.7 broadcast_in_dim.9
  165.7 12.9 %all-to-all-start.3 = ((f32[32,8,128]{2,1,0:T(8,128)}), f32[32,8,128]{2,1,0:T(8,128)S(1)}, u32[]{:S(2)}, u32[]{:S(2)}) async-start(f32[32,8,128]{2,1,0:T(8,128)} %broadcast_in_dim.9), calls=%async_computation.3 | async-start | bytes 262144 | tf_op jit(solution)/shard_map/all_to_all | solution.py:80
  178.7 20.2 %all-to-all-done.3 = f32[32,8,128]{2,1,0:T(8,128)S(1)} async-done(((f32[32,8,128]{2,1,0:T(8,128)}), f32[32,8,128]{2,1,0:T(8,128)S(1)}, u32[]{:S(2)}, u32[]{:S(2)}) %all-to-all-start.3) | async-done | bytes 131104 | tf_op jit(solution)/shard_map/all_to_all | solution.py:80
  199.0 0.6 broadcast_in_dim.21
  199.6 3.6 %all-to-all-start.4 = ((f32[8,16,128]{2,1,0:T(8,128)}), f32[8,16,128]{2,1,0:T(8,128)S(1)}, u32[]{:S(2)}, u32[]{:S(2)}) async-start(f32[8,16,128]{2,1,0:T(8,128)} %broadcast_in_dim.21), calls=%async_computation.4 | async-start | bytes 131072 | tf_op jit(solution)/shard_map/all_to_all | solution.py:83
  203.2 0.5 fusion.27
  203.7 0.9 all_to_all.33
  204.6 4.2 %all-to-all-done.4 = f32[8,16,128]{2,1,0:T(8,128)S(1)} async-done(((f32[8,16,128]{2,1,0:T(8,128)}), f32[8,16,128]{2,1,0:T(8,128)S(1)}, u32[]{:S(2)}, u32[]{:S(2)}) %all-to-all-start.4) | async-done | bytes 65568 | tf_op jit(solution)/shard_map/all_to_all | solution.py:83
  208.8 7.1 %all-to-all-start.2 = ((bf16[16,10,1024]{2,1,0:T(8,128)(2,1)}), bf16[16,10,1024]{2,1,0:T(8,128)(2,1)S(1)}, u32[]{:S(2)}, u32[]{:S(2)}) async-start(bf16[16,10,1024]{2,1,0:T(8,128)(2,1)} %all_to_all.33), calls=%async_computation.2 | async-start | bytes 1048576 | tf_op jit(solution)/shard_map/all_to_all | solution.py:77
  216.0 0.7 copy.35
  216.7 58.2 %all-to-all-done.2 = bf16[16,10,1024]{2,1,0:T(8,128)(2,1)S(1)} async-done(((bf16[16,10,1024]{2,1,0:T(8,128)(2,1)}), bf16[16,10,1024]{2,1,0:T(8,128)(2,1)S(1)}, u32[]{:S(2)}, u32[]{:S(2)}) %all-to-all-start.2) | async-done | bytes 327712 | tf_op jit(solution)/shard_map/all_to_all | solution.py:77
  275.0 1.0 convolution_convert_fusion.1
  (22 shorter events, 0.8 us)
Async XLA Ops:
  0.6 130.8 %copy-start = (bf16[1,1024,1024]{2,1,0:T(8,128)(2,1)S(1)}, bf16[1,1024,1024]{2,1,0:T(8,128)(2,1)}, u32[]{:S(2)}) copy-start(bf16[1,1024,1024]{2,1,0:T(8,128)(2,1)} %param.12) | copy-start | bytes 6291460
  5.8 121.6 %all-to-all-start = ((bf16[16,10,2048]{2,1,0:T(8,128)(2,1)}), bf16[16,10,2048]{2,1,0:T(8,128)(2,1)}, u32[]{:S(2)}, u32[]{:S(2)}) async-start(bf16[16,10,2048]{2,1,0:T(8,128)(2,1)} %all_to_all.28), calls=%async_computation | async-start | bytes 2097152 | tf_op jit(solution)/shard_map/all_to_all | solution.py:51
  129.2 3.1 %copy-start.1 = (bf16[1,1024,1024]{2,1,0:T(8,128)(2,1)S(1)}, bf16[1,1024,1024]{2,1,0:T(8,128)(2,1)}, u32[]{:S(2)}) copy-start(bf16[1,1024,1024]{2,1,0:T(8,128)(2,1)} %param.10) | copy-start | bytes 6291460
  165.7 33.2 %all-to-all-start.3 = ((f32[32,8,128]{2,1,0:T(8,128)}), f32[32,8,128]{2,1,0:T(8,128)S(1)}, u32[]{:S(2)}, u32[]{:S(2)}) async-start(f32[32,8,128]{2,1,0:T(8,128)} %broadcast_in_dim.9), calls=%async_computation.3 | async-start | bytes 262144 | tf_op jit(solution)/shard_map/all_to_all | solution.py:80
  199.6 9.2 %all-to-all-start.4 = ((f32[8,16,128]{2,1,0:T(8,128)}), f32[8,16,128]{2,1,0:T(8,128)S(1)}, u32[]{:S(2)}, u32[]{:S(2)}) async-start(f32[8,16,128]{2,1,0:T(8,128)} %broadcast_in_dim.21), calls=%async_computation.4 | async-start | bytes 131072 | tf_op jit(solution)/shard_map/all_to_all | solution.py:83
  208.8 66.0 %all-to-all-start.2 = ((bf16[16,10,1024]{2,1,0:T(8,128)(2,1)}), bf16[16,10,1024]{2,1,0:T(8,128)(2,1)S(1)}, u32[]{:S(2)}, u32[]{:S(2)}) async-start(bf16[16,10,1024]{2,1,0:T(8,128)(2,1)} %all_to_all.33), calls=%async_computation.2 | async-start | bytes 1048576 | tf_op jit(solution)/shard_map/all_to_all | solution.py:77

commit v2 on v1

v2 whole, which is shorter than its diff:
```python
import functools

import jax
import jax.numpy as jnp
from jax import lax
from jax.experimental import pallas as pl
from jax.experimental.pallas import tpu as pltpu
from jax.sharding import Mesh, PartitionSpec as P

BF16 = jnp.bfloat16
F32 = jnp.float32
I32 = jnp.int32
CAP = 10
N_EXP = 16
N_CTX = 4
HALF = 8
PART = 16
BACK = 8
MESH = (2, 8, 4, 2, 4, 2)
NAMES = ("dh", "dl", "ctx", "zh", "y", "core")
TOK = ("dh", "dl", "zh", "y", "core")
ALL_Z = ("dh", "dl", "zh")
IN_Z = ("y", "core")
PAIR = ("dh", "zh")
PAIR_PERM = ((0, 3), (3, 0), (1, 2), (2, 1))


def dot(a, b, dims=((1,), (0,))):
    return lax.dot_general(a, b, (dims, ((), ())), preferred_element_type=F32)


def iota(shape, dim):
    return lax.broadcasted_iota(I32, shape, dim)


def pick(mask):
    return mask.astype(F32).astype(BF16)


def pieces(v):
    a = v.astype(BF16)
    v = v - a.astype(F32)
    b = v.astype(BF16)
    c = (v - b.astype(F32)).astype(BF16)
    return a, b, c


def spread(lane, first, v):
    a, b, c = pieces(v)
    out = jnp.where(lane == first, a.astype(F32), 0.0)
    out = jnp.where(lane == first + 1, b.astype(F32), out)
    return jnp.where(lane == first + 2, c.astype(F32), out)


def gathered(lane, first, v):
    return jnp.sum(jnp.where((lane >= first) & (lane < first + 3), v, 0.0), axis=1, keepdims=True)


def tenth(r):
    out = jnp.zeros_like(r)
    for k in range(1, HALF):
        out = out + (r >= k * CAP).astype(I32)
    return out


def where_to(zh, route):
    count = route.shape[0]
    ids = iota((count, 128), 1)
    onehot = (route == ids).astype(F32)
    before = pick(iota((count, count), 1) < iota((count, count), 0))
    earlier = dot(before, onehot.astype(BF16))
    position = jnp.sum(earlier * onehot, axis=1, keepdims=True).astype(I32)
    far = jnp.where(route >= HALF, 1, 0)
    far = jnp.where(zh == 1, 1 - far, far)
    place = jnp.where(route >= HALF, route - HALF, route)
    return far, place, position


def pack_kernel(zh_ref, route_ref, tok_ref, cot_ref, near_ref, far_ref):
    far, place, position = where_to(zh_ref[0], route_ref[...])
    count, width = tok_ref.shape
    quarter = width // 4
    first = PART - CAP
    slots = iota((count, 2 * HALF * PART), 1)
    base = far * (HALF * PART) + place * PART
    to_tok = pick(slots == base + position)
    to_cot = pick((slots == base + CAP + position) & (position < first))
    turn = ((0,), (0,))
    main = dot(to_tok, tok_ref[...], turn) + dot(to_cot, cot_ref[...], turn)
    extra = jnp.zeros((2 * HALF * PART, quarter), F32)
    for i in range(4):
        to_extra = pick((slots == base + (position - first) * 4 + i) & (position >= first))
        extra = extra + dot(to_extra, cot_ref[:, i * quarter : (i + 1) * quarter], turn)
    main, extra = main.astype(BF16), extra.astype(BF16)
    n = HALF * PART
    near_ref[:, :width], near_ref[:, width:] = main[:n], extra[:n]
    far_ref[:, :width], far_ref[:, width:] = main[n:], extra[n:]


def up_kernel(near_ref, far_ref, router_ref, gate_ref, up_ref, down_ref, part_ref, x_ref, c_ref):
    width, hid = gate_ref.shape
    quarter = width // 4
    first = PART - CAP
    n = HALF * CAP
    r = iota((n, HALF * PART), 0)
    col = iota((n, HALF * PART), 1)
    src = tenth(r)
    p = r - src * CAP
    base = src * PART
    of_tok = pick(col == base + p)
    of_cot = pick((col == base + CAP + p) & (p < first))
    of_extra = [pick((col == base + (p - first) * 4 + i) & (p >= first)) for i in range(4)]
    for half, ref in enumerate((near_ref, far_ref)):
        main, extra = ref[:, :width], ref[:, width:]
        x_ref[half * n : (half + 1) * n, :] = dot(of_tok, main).astype(BF16)
        for i in range(4):
            cols = slice(i * quarter, (i + 1) * quarter)
            c_ref[half * n : (half + 1) * n, cols] = (dot(of_cot, main[:, cols]) + dot(of_extra[i], extra)).astype(BF16)
    x = x_ref[...]
    rows = 2 * n // N_CTX

    def put(v, at):
        for i in range(N_CTX):
            part_ref[i, :, at : at + v.shape[1]] = v[i * rows : (i + 1) * rows].astype(BF16)

    put(dot(x, gate_ref[...]), 0)
    put(dot(x, up_ref[...]), hid)
    put(dot(c_ref[...], down_ref[...], ((1,), (1,))), 2 * hid)
    logit = jnp.sum(dot(x, router_ref[...]), axis=1, keepdims=True)
    put(spread(iota((2 * n, 128), 1), 0, logit), 3 * hid)


def hidden_kernel(mine_ref, out_ref):
    hid = (mine_ref.shape[2] - 128) // 3

    def total(at, size):
        out = mine_ref[0, :, at : at + size].astype(F32)
        for i in range(1, N_CTX):
            out = out + mine_ref[i, :, at : at + size].astype(F32)
        return out

    gate, up, back = total(0, hid), total(hid, hid), total(2 * hid, hid)
    logit = jnp.sum(total(3 * hid, 128), axis=1, keepdims=True)
    hidden = (gate / (1.0 + jnp.exp(-gate)) * up).astype(BF16)
    inner = jnp.sum(hidden.astype(F32) * back, axis=1, keepdims=True)
    score = 1.0 / (1.0 + jnp.exp(-logit))
    slope = inner * score * (1.0 - score)
    lane = iota((hidden.shape[0], 128), 1)
    small = (spread(lane, 0, score) + spread(lane, 3, slope)).astype(BF16)
    for i in range(N_CTX):
        out_ref[i, :, :hid] = hidden
        out_ref[i, :, hid:] = small


def down_kernel(full_ref, down_ref, near_ref, far_ref, rows_ref):
    hid, width = down_ref.shape
    quarter = width // 4
    rows = full_ref.shape[1]
    full = jnp.concatenate([full_ref[i].astype(F32) for i in range(N_CTX)], axis=0)
    score = gathered(iota((N_CTX * rows, 128), 1), 0, full[:, hid:])
    values = dot(full[:, :hid].astype(BF16), down_ref[...]).astype(BF16)
    rows_ref[...] = (score * values.astype(F32)).astype(BF16)
    n = HALF * CAP
    slot = iota((HALF * BACK, n), 0)
    r = iota((HALF * BACK, n), 1)
    src = tenth(r)
    p = r - src * CAP
    to_main = pick((slot == src * BACK + p) & (p < BACK))
    to_extra = [pick((slot == src * BACK + (p - BACK) * 4 + i) & (p >= BACK)) for i in range(4)]
    for half, ref in enumerate((near_ref, far_ref)):
        mine = rows_ref[half * n : (half + 1) * n, :]
        ref[:, :width] = dot(to_main, mine).astype(BF16)
        extra = jnp.zeros((HALF * BACK, quarter), F32)
        for i in range(4):
            extra = extra + dot(to_extra[i], mine[:, i * quarter : (i + 1) * quarter])
        ref[:, width:] = extra.astype(BF16)


def grad_kernel(full_ref, x_ref, far_ref, out_ref):
    hid = full_ref.shape[2] - 128
    small = jnp.concatenate([full_ref[i, :, hid:].astype(F32) for i in range(N_CTX)], axis=0).astype(BF16)
    every = dot(small, x_ref[...], ((0,), (0,)))
    grad = every[3:4] + every[4:5] + every[5:6]
    copies = out_ref.shape[0]
    for j in range(8):
        out_ref[:, j, :] = jnp.broadcast_to(grad[:, j * 128 : (j + 1) * 128], (copies, 128))


def merge_kernel(near_ref, far_ref, grads_ref, out_ref):
    span = near_ref.shape[1]
    out_ref[:, :span] = near_ref[...]
    out_ref[:, span : 2 * span] = far_ref[...]
    parts = grads_ref.shape[0] // 2
    for zh in range(2):
        total = grads_ref[zh]
        for k in range(1, parts):
            total = total + grads_ref[2 * k + zh]
        high = total.astype(BF16)
        low = (total - high.astype(F32)).astype(BF16)
        for at, v in ((2 * span + zh * 128, high), (2 * span + 256 + zh * 128, low)):
            out_ref[:, at : at + 128] = jnp.concatenate([v.astype(F32)] * HALF, axis=0).astype(BF16)


def out_kernel(zh_ref, route_ref, fin_ref, out_ref, grad_ref):
    far, place, position = where_to(zh_ref[0], route_ref[...])
    count, width = out_ref.shape
    quarter = width // 4
    span = width + quarter
    n = HALF * BACK
    slots = iota((count, n), 1)
    base = place * BACK
    for half in range(2):
        here = far == half
        of_main = pick((slots == base + position) & (position < BACK) & here)
        main = dot(of_main, fin_ref[:, half * span : half * span + width])
        extra = fin_ref[:, half * span + width : (half + 1) * span]
        for i in range(4):
            cols = slice(i * quarter, (i + 1) * quarter)
            of_extra = pick((slots == base + (position - BACK) * 4 + i) & (position >= BACK) & here)
            value = main[:, cols] + dot(of_extra, extra)
            if half:
                value = value + out_ref[:, cols].astype(F32)
            out_ref[:, cols] = value.astype(BF16)
    r = iota((n, 128), 0)
    col = iota((n, 128), 1)
    j, e = col // N_EXP, col % N_EXP
    turned = jnp.zeros((128, 128), F32)
    for zh in range(2):
        take = pick((r == (e % HALF) * BACK + j) & (e // HALF == zh))
        for part in range(2):
            at = 2 * span + part * 256 + zh * 128
            turned = turned + dot(fin_ref[:, at : at + 128], take, ((0,), (0,)))
    for k in range(8):
        grad_ref[k * 128 : (k + 1) * 128, :] = turned[:, k * N_EXP : (k + 1) * N_EXP]


def call(kernel, out, scalars=0, scratch=(), unread=()):
    def run(*args):
        smem = pl.BlockSpec(memory_space=pltpu.SMEM)
        vmem = pl.BlockSpec(memory_space=pltpu.VMEM)
        anywhere = pl.BlockSpec(memory_space=pl.ANY)
        specs = [smem if i < scalars else anywhere if i in unread else vmem for i in range(len(args))]
        return pl.pallas_call(
            kernel,
            in_specs=specs,
            out_specs=jax.tree.map(lambda _: vmem, out),
            out_shape=out,
            scratch_shapes=scratch,
            compiler_params=pltpu.CompilerParams(vmem_limit_bytes=32 * 1024 * 1024),
        )(*args)

    return run


def shards(tokens, routes, router_weight, gate_weight, up_weight, down_weight, cotangent):
    count, width = tokens.shape
    hid = gate_weight.shape[2]
    shape = jax.ShapeDtypeStruct
    zh = lax.axis_index("zh").astype(I32)
    expert = zh * HALF + lax.axis_index("y") * 2 + lax.axis_index("core")
    zh = zh.reshape(1)
    span = width + width // 4
    rows = N_EXP * CAP
    exchange = functools.partial(lax.all_to_all, axis_name=IN_Z, split_axis=0, concat_axis=0, tiled=True)
    over_ctx = functools.partial(lax.all_to_all, axis_name="ctx", split_axis=0, concat_axis=0, tiled=True)

    sent = shape((HALF * PART, span), BF16)
    near, far = call(pack_kernel, (sent, sent), 1)(zh, routes, tokens, cotangent)
    far = lax.ppermute(far, PAIR, PAIR_PERM)
    near = exchange(near)
    far = exchange(far)

    router_col = lax.dynamic_slice(router_weight, (lax.axis_index("ctx") * width, expert), (width, 1))
    router_col = jnp.concatenate([*pieces(router_col), jnp.zeros((width, 125), BF16)], axis=1)
    part, x = call(
        up_kernel,
        (shape((N_CTX, rows // N_CTX, 3 * hid + 128), BF16), shape((rows, width), BF16)),
        scratch=[pltpu.VMEM((rows, width), BF16)],
    )(near, far, router_col, gate_weight[0], up_weight[0], down_weight[0])
    mine = over_ctx(part)
    full = over_ctx(call(hidden_kernel, shape((N_CTX, rows // N_CTX, hid + 128), BF16))(mine))

    back = shape((HALF * BACK, span), BF16)
    near, far = call(down_kernel, (back, back), scratch=[pltpu.VMEM((rows, width), BF16)])(full, down_weight[0])
    grad = call(grad_kernel, shape((lax.axis_size(ALL_Z), 8, width // 8), F32), unread=(2,))(full, x, far)
    far = lax.ppermute(far, PAIR, PAIR_PERM)
    grads = lax.all_to_all(grad, ALL_Z, 0, 0, tiled=True)
    fin = exchange(call(merge_kernel, shape((HALF * BACK, 2 * span + 512), BF16))(near, far, grads))
    return call(out_kernel, (shape((count, width), BF16), shape((width, N_EXP), F32)), 1)(zh, routes, fin)


def solution(mesh):
    fine = Mesh(mesh.devices.reshape(MESH), NAMES)
    ep = ("zh", "y", "core")
    return jax.shard_map(
        shards,
        mesh=fine,
        in_specs=(
            P(TOK, "ctx"),
            P(TOK, None),
            P(),
            P(ep, "ctx", None),
            P(ep, "ctx", None),
            P(ep, None, "ctx"),
            P(TOK, "ctx"),
        ),
        out_specs=(P(TOK, "ctx"), P("ctx", None)),
        check_vma=False,
    )
```

time: 277 us -> 212 us (0.77)
  the two profiles are of different devices: /device:TPU:224 before, /device:TPU:64 now
where the time goes in v2:
time: 212 us
  waiting for transfers between devices  85.6 us (40%)
  starting transfers between devices  70.4 us (33%)
  blocking collectives  39.6 us (19%)
  local copies, waits for them, and re-layouts  7.78 us (4%)
  Pallas kernels  7.16 us (3%)
    ppermute x2, waiting for transfers between devices, shards(): far = lax.ppermute(far, PAIR, PAIR_PERM)  51.1 us
    ppermute x2, starting transfers between devices, shards(): far = lax.ppermute(far, PAIR, PAIR_PERM)  31.5 us
    all_to_all x1, starting transfers between devices, shards(): grads = lax.all_to_all(grad, ALL_Z, 0, 0, tiled=True)  29.8 us
    all_to_all x1, waiting for transfers between devices, shards(): grads = lax.all_to_all(grad, ALL_Z, 0, 0, tiled=True)  19.6 us
    all_to_all x1, blocking collectives, shards(): mine = over_ctx(part)  18.5 us
    all_to_all x1, blocking collectives, shards(): exchange(call(merge_kernel, shape((HALF * BACK, 2 * span + 512), BF16))(n...  11.5 us
    all_to_all x1, blocking collectives, shards(): over_ctx(call(hidden_kernel, shape((N_CTX, rows // N_CTX, hid + 128), BF1...  9.62 us
    all_to_all x1, waiting for transfers between devices, shards(): far = exchange(far)  7.78 us
  transfers between devices with their start and end apart: 5, of which 5 were waited for; matrix products, arithmetic and copies ran while one was open for 1% of the time, Pallas kernels for 0%

profile of v2, /device:TPU:64, one launch (start us, length us, event | category | flops | bytes accessed | tf_op | source)
XLA Modules:
  0.0 211.6 jit_solution(2861921643267141573)
XLA Ops:
  0.6 0.8 copy.15.route_ref
  1.4 0.9 copy-done.3
  2.4 0.9 copy-done.4
  3.3 1.7 shard_map.86
  5.0 21.2 %collective-permute-start = (bf16[128,1280]{1,0:T(8,128)(2,1)S(1)}, bf16[128,1280]{1,0:T(8,128)(2,1)}, u32[]{:S(2)}, u32[]{:S(2)}) collective-permute-start(bf16[128,1280]{1,0:T(8,128)(2,1)S(1)} %get-tuple-element.9), channel_id=1, source_target_pairs={{0,520},{520,0},{8,512},{512,8},{1,521},{521,1},{9,513},{513,9},{2... | collective-permute-start | bytes 983048 | tf_op jit(solution)/shard_map/ppermute | solution.py:269
  26.2 0.0 copy-start
  26.2 4.6 %all-to-all-start = ((bf16[8,16,1280]{2,1,0:T(8,128)(2,1)}), bf16[8,16,1280]{2,1,0:T(8,128)(2,1)S(1)}, u32[]{:S(2)}, u32[]{:S(2)}) async-start(bf16[8,16,1280]{2,1,0:T(8,128)(2,1)} %bitcast.1), calls=%async_computation | async-start | bytes 655360 | tf_op jit(solution)/shard_map/all_to_all | solution.py:270
  30.8 0.8 dynamic_slice.3
  31.6 0.2 copy.17
  31.9 7.2 %all-to-all-done = bf16[8,16,1280]{2,1,0:T(8,128)(2,1)S(1)} async-done(((bf16[8,16,1280]{2,1,0:T(8,128)(2,1)}), bf16[8,16,1280]{2,1,0:T(8,128)(2,1)S(1)}, u32[]{:S(2)}, u32[]{:S(2)}) %all-to-all-start) | async-done | bytes 327712 | tf_op jit(solution)/shard_map/all_to_all | solution.py:270
  39.0 29.3 %collective-permute-done = bf16[128,1280]{1,0:T(8,128)(2,1)} collective-permute-done((bf16[128,1280]{1,0:T(8,128)(2,1)S(1)}, bf16[128,1280]{1,0:T(8,128)(2,1)}, u32[]{:S(2)}, u32[]{:S(2)}) %collective-permute-start) | collective-permute-done | bytes 327712 | tf_op jit(solution)/shard_map/ppermute | solution.py:269
  68.3 4.5 %all-to-all-start.1 = ((bf16[8,16,1280]{2,1,0:T(8,128)(2,1)}), bf16[8,16,1280]{2,1,0:T(8,128)(2,1)S(1)}, u32[]{:S(2)}, u32[]{:S(2)}) async-start(bf16[8,16,1280]{2,1,0:T(8,128)(2,1)} %bitcast.3), calls=%async_computation.1 | async-start | bytes 655360 | tf_op jit(solution)/shard_map/all_to_all | solution.py:271
  72.8 0.1 fusion.1
  72.9 0.1 pad.3.clone
  73.0 0.3 maximum_maximum_fusion.router_ref
  73.2 7.8 %all-to-all-done.1 = bf16[8,16,1280]{2,1,0:T(8,128)(2,1)S(1)} async-done(((bf16[8,16,1280]{2,1,0:T(8,128)(2,1)}), bf16[8,16,1280]{2,1,0:T(8,128)(2,1)S(1)}, u32[]{:S(2)}, u32[]{:S(2)}) %all-to-all-start.1) | async-done | bytes 327712 | tf_op jit(solution)/shard_map/all_to_all | solution.py:271
  81.0 0.0 copy-done
  81.0 1.6 copy-done.1
  82.6 1.6 copy-done.2
  84.2 2.0 shard_map.87
  86.2 18.5 %all_to_all.48.mine_ref = bf16[4,40,3200]{2,1,0:T(8,128)(2,1)S(1)} all-to-all(bf16[4,40,3200]{2,1,0:T(8,128)(2,1)S(1)} %get-tuple-element.10), channel_id=1, replica_groups=mesh['dh'=2,'dl'=8,'ctx'=4,'zh'=2,'y'=4,'core'=2] {'ctx'}, dimensions={0} | all-to-all | bytes 2048000 | tf_op jit(solution)/shard_map/all_to_all | solution.py:280
  104.7 0.3 shard_map.88
  105.0 9.6 %all_to_all.49.full_ref = bf16[4,40,1152]{2,1,0:T(8,128)(2,1)S(1)} all-to-all(bf16[4,40,1152]{2,1,0:T(8,128)(2,1)S(1)} %shard_map.88), channel_id=1, replica_groups=mesh['dh'=2,'dl'=8,'ctx'=4,'zh'=2,'y'=4,'core'=2] {'ctx'}, dimensions={0} | all-to-all | bytes 737280 | tf_op jit(solution)/shard_map/all_to_all | solution.py:281
  114.6 0.8 shard_map.89
  115.4 0.9 shard_map.90
  116.3 29.8 %all-to-all-start.4 = ((f32[32,8,128]{2,1,0:T(8,128)}), f32[32,8,128]{2,1,0:T(8,128)S(1)}, u32[]{:S(2)}, u32[]{:S(2)}) async-start(f32[32,8,128]{2,1,0:T(8,128)} %shard_map.90), calls=%async_computation.4 | async-start | bytes 262144 | tf_op jit(solution)/shard_map/all_to_all | solution.py:287
  146.1 10.3 %collective-permute-start.1 = (bf16[64,1280]{1,0:T(8,128)(2,1)S(1)}, bf16[64,1280]{1,0:T(8,128)(2,1)S(1)}, u32[]{:S(2)}, u32[]{:S(2)}) collective-permute-start(bf16[64,1280]{1,0:T(8,128)(2,1)S(1)} %get-tuple-element.12.far_ref), channel_id=1, source_target_pairs={{0,520},{520,0},{8,512},{512,8},{1,521},{521,1},{9,513},{513,9},{2... | collective-permute-start | bytes 491528 | tf_op jit(solution)/shard_map/ppermute | solution.py:286
  156.4 21.8 %collective-permute-done.1.far_ref = bf16[64,1280]{1,0:T(8,128)(2,1)S(1)} collective-permute-done((bf16[64,1280]{1,0:T(8,128)(2,1)S(1)}, bf16[64,1280]{1,0:T(8,128)(2,1)S(1)}, u32[]{:S(2)}, u32[]{:S(2)}) %collective-permute-start.1) | collective-permute-done | bytes 163872 | tf_op jit(solution)/shard_map/ppermute | solution.py:286
  178.2 19.6 %all-to-all-done.4.grads_ref = f32[32,8,128]{2,1,0:T(8,128)S(1)} async-done(((f32[32,8,128]{2,1,0:T(8,128)}), f32[32,8,128]{2,1,0:T(8,128)S(1)}, u32[]{:S(2)}, u32[]{:S(2)}) %all-to-all-start.4) | async-done | bytes 131104 | tf_op jit(solution)/shard_map/all_to_all | solution.py:287
  197.8 11.5 %all_to_all.50 = bf16[8,8,3072]{2,1,0:T(8,128)(2,1)S(1)} all-to-all(bf16[8,8,3072]{2,1,0:T(8,128)(2,1)S(1)} %bitcast.15), channel_id=1, replica_groups=mesh['dh'=2,'dl'=8,'ctx'=4,'zh'=2,'y'=4,'core'=2] {'y','core'}, dimensions={0} | all-to-all | bytes 786432 | tf_op jit(solution)/shard_map/all_to_all | solution.py:288
  209.3 1.5 shard_map.92
  210.8 0.8 copy.16
  (6 shorter events, 0.1 us)
Async XLA Ops:
  1.4 0.9 copy-start.3
  2.3 0.9 copy-start.4
  5.0 63.3 %collective-permute-start = (bf16[128,1280]{1,0:T(8,128)(2,1)S(1)}, bf16[128,1280]{1,0:T(8,128)(2,1)}, u32[]{:S(2)}, u32[]{:S(2)}) collective-permute-start(bf16[128,1280]{1,0:T(8,128)(2,1)S(1)} %get-tuple-element.9), channel_id=1, source_target_pairs={{0,520},{520,0},{8,512},{512,8},{1,521},{521,1},{9,513},{513,9},{2... | collective-permute-start | bytes 983048 | tf_op jit(solution)/shard_map/ppermute | solution.py:269
  26.2 54.9 %copy-start = (bf16[1,1024,1024]{2,1,0:T(8,128)(2,1)S(1)}, bf16[1,1024,1024]{2,1,0:T(8,128)(2,1)}, u32[]{:S(2)}) copy-start(bf16[1,1024,1024]{2,1,0:T(8,128)(2,1)} %param.12) | copy-start | bytes 6291460
  26.2 12.9 %all-to-all-start = ((bf16[8,16,1280]{2,1,0:T(8,128)(2,1)}), bf16[8,16,1280]{2,1,0:T(8,128)(2,1)S(1)}, u32[]{:S(2)}, u32[]{:S(2)}) async-start(bf16[8,16,1280]{2,1,0:T(8,128)(2,1)} %bitcast.1), calls=%async_computation | async-start | bytes 655360 | tf_op jit(solution)/shard_map/all_to_all | solution.py:270
  68.3 12.7 %all-to-all-start.1 = ((bf16[8,16,1280]{2,1,0:T(8,128)(2,1)}), bf16[8,16,1280]{2,1,0:T(8,128)(2,1)S(1)}, u32[]{:S(2)}, u32[]{:S(2)}) async-start(bf16[8,16,1280]{2,1,0:T(8,128)(2,1)} %bitcast.3), calls=%async_computation.1 | async-start | bytes 655360 | tf_op jit(solution)/shard_map/all_to_all | solution.py:271
  81.0 1.6 copy-start.1
  82.6 1.6 copy-start.2
  116.3 81.5 %all-to-all-start.4 = ((f32[32,8,128]{2,1,0:T(8,128)}), f32[32,8,128]{2,1,0:T(8,128)S(1)}, u32[]{:S(2)}, u32[]{:S(2)}) async-start(f32[32,8,128]{2,1,0:T(8,128)} %shard_map.90), calls=%async_computation.4 | async-start | bytes 262144 | tf_op jit(solution)/shard_map/all_to_all | solution.py:287
  146.1 32.1 %collective-permute-start.1 = (bf16[64,1280]{1,0:T(8,128)(2,1)S(1)}, bf16[64,1280]{1,0:T(8,128)(2,1)S(1)}, u32[]{:S(2)}, u32[]{:S(2)}) collective-permute-start(bf16[64,1280]{1,0:T(8,128)(2,1)S(1)} %get-tuple-element.12.far_ref), channel_id=1, source_target_pairs={{0,520},{520,0},{8,512},{512,8},{1,521},{521,1},{9,513},{513,9},{2... | collective-permute-start | bytes 491528 | tf_op jit(solution)/shard_map/ppermute | solution.py:286

commit v3 on v2

v3 whole, which is shorter than its diff:
```python
import functools

import jax
import jax.numpy as jnp
from jax import lax
from jax.experimental import pallas as pl
from jax.experimental.pallas import tpu as pltpu
from jax.sharding import Mesh, PartitionSpec as P

BF16 = jnp.bfloat16
F32 = jnp.float32
I32 = jnp.int32
CAP = 10
N_EXP = 16
N_CTX = 4
HALF = 8
BACK = 8
MESH = (2, 8, 4, 2, 4, 2)
NAMES = ("dh", "dl", "ctx", "zh", "y", "core")
TOK = ("dh", "dl", "zh", "y", "core")
ALL_Z = ("dh", "dl", "zh")
IN_Z = ("y", "core")
PAIR = ("dh", "zh")
PAIR_PERM = ((0, 3), (3, 0), (1, 2), (2, 1))


def dot(a, b, dims=((1,), (0,))):
    return lax.dot_general(a, b, (dims, ((), ())), preferred_element_type=F32)


def iota(shape, dim):
    return lax.broadcasted_iota(I32, shape, dim)


def pick(mask):
    return mask.astype(F32).astype(BF16)


def pieces(v):
    a = v.astype(BF16)
    v = v - a.astype(F32)
    b = v.astype(BF16)
    c = (v - b.astype(F32)).astype(BF16)
    return a, b, c


def spread(lane, first, v):
    a, b, c = pieces(v)
    out = jnp.where(lane == first, a.astype(F32), 0.0)
    out = jnp.where(lane == first + 1, b.astype(F32), out)
    return jnp.where(lane == first + 2, c.astype(F32), out)


def gathered(lane, first, v):
    return jnp.sum(jnp.where((lane >= first) & (lane < first + 3), v, 0.0), axis=1, keepdims=True)


def tenth(r):
    out = jnp.zeros_like(r)
    for k in range(1, HALF):
        out = out + (r >= k * CAP).astype(I32)
    return out


def where_to(zh, route):
    count = route.shape[0]
    ids = iota((count, 128), 1)
    onehot = (route == ids).astype(F32)
    before = pick(iota((count, count), 1) < iota((count, count), 0))
    earlier = dot(before, onehot.astype(BF16))
    position = jnp.sum(earlier * onehot, axis=1, keepdims=True).astype(I32)
    far = jnp.where(route >= HALF, 1, 0)
    far = jnp.where(zh == 1, 1 - far, far)
    place = jnp.where(route >= HALF, route - HALF, route)
    return far, place, position


def packing(base, position, shape):
    slots = iota(shape, 1)
    whole = pick((slots == base + position) & (position < BACK))
    quarters = [pick((slots == base + (position - BACK) * 4 + i) & (position >= BACK)) for i in range(4)]
    return whole, quarters


def pack_kernel(zh_ref, route_ref, tok_ref, cot_ref, far_ref, near_ref):
    far, place, position = where_to(zh_ref[0], route_ref[...])
    count, width = tok_ref.shape
    quarter = width // 4
    span = width + quarter
    n = HALF * BACK
    whole, quarters = packing(far * n + place * BACK, position, (count, 2 * n))
    turn = ((0,), (0,))
    for ref, near_at, far_out, far_at in ((tok_ref, 0, far_ref, 0), (cot_ref, span, near_ref, 2 * span)):
        main = dot(whole, ref[...], turn).astype(BF16)
        extra = dot(quarters[0], ref[:, :quarter], turn)
        for i in range(1, 4):
            extra = extra + dot(quarters[i], ref[:, i * quarter : (i + 1) * quarter], turn)
        extra = extra.astype(BF16)
        near_ref[:, near_at : near_at + width], near_ref[:, near_at + width : near_at + span] = main[:n], extra[:n]
        far_out[:, far_at : far_at + width], far_out[:, far_at + width : far_at + span] = main[n:], extra[n:]


def unpacking():
    shape = (HALF * CAP, HALF * BACK)
    r, col = iota(shape, 0), iota(shape, 1)
    src = tenth(r)
    p = r - src * CAP
    whole = pick((col == src * BACK + p) & (p < BACK))
    quarters = [pick((col == src * BACK + (p - BACK) * 4 + i) & (p >= BACK)) for i in range(4)]
    return whole, quarters


def unpack(maps, main, extra):
    whole, quarters = maps
    quarter = extra.shape[1]
    return [dot(whole, main[:, i * quarter : (i + 1) * quarter]) + dot(quarters[i], extra) for i in range(4)]


def up_kernel(near_ref, far_ref, router_ref, gate_ref, up_ref, part_ref, x_ref):
    width, hid = gate_ref.shape
    quarter = width // 4
    span = width + quarter
    n = HALF * CAP
    maps = unpacking()
    for half, ref in enumerate((near_ref, far_ref)):
        for i, block in enumerate(unpack(maps, ref[:, :width], ref[:, width:span])):
            x_ref[half * n : (half + 1) * n, i * quarter : (i + 1) * quarter] = block.astype(BF16)
    x = x_ref[...]
    rows = 2 * n // N_CTX

    def put(v, at):
        for i in range(N_CTX):
            part_ref[i, :, at : at + v.shape[1]] = v[i * rows : (i + 1) * rows].astype(BF16)

    logit = jnp.sum(dot(x, router_ref[...]), axis=1, keepdims=True)
    put(spread(iota((2 * n, 128), 1), 0, logit), 2 * hid)
    put(dot(x, gate_ref[...]), 0)
    put(dot(x, up_ref[...]), hid)


def hidden_kernel(mine_ref, out_ref):
    hid = (mine_ref.shape[2] - 128) // 2

    def total(at, size):
        out = mine_ref[0, :, at : at + size].astype(F32)
        for i in range(1, N_CTX):
            out = out + mine_ref[i, :, at : at + size].astype(F32)
        return out

    gate, up = total(0, hid), total(hid, hid)
    logit = jnp.sum(total(2 * hid, 128), axis=1, keepdims=True)
    hidden = (gate / (1.0 + jnp.exp(-gate)) * up).astype(BF16)
    score = 1.0 / (1.0 + jnp.exp(-logit))
    small = spread(iota((hidden.shape[0], 128), 1), 0, score).astype(BF16)
    for i in range(N_CTX):
        out_ref[i, :, :hid] = hidden
        out_ref[i, :, hid:] = small


def down_kernel(full_ref, down_ref, near_ref, far_ref, values_ref, rows_ref):
    hid, width = down_ref.shape
    quarter = width // 4
    full = jnp.concatenate([full_ref[i].astype(F32) for i in range(N_CTX)], axis=0)
    score = gathered(iota((full.shape[0], 128), 1), 0, full[:, hid:])
    values = dot(full[:, :hid].astype(BF16), down_ref[...]).astype(BF16)
    values_ref[...] = values
    rows_ref[...] = (score * values.astype(F32)).astype(BF16)
    n = HALF * CAP
    slot, r = iota((HALF * BACK, n), 0), iota((HALF * BACK, n), 1)
    src = tenth(r)
    p = r - src * CAP
    whole = pick((slot == src * BACK + p) & (p < BACK))
    quarters = [pick((slot == src * BACK + (p - BACK) * 4 + i) & (p >= BACK)) for i in range(4)]
    for half, ref in enumerate((near_ref, far_ref)):
        mine = rows_ref[half * n : (half + 1) * n, :]
        ref[:, :width] = dot(whole, mine).astype(BF16)
        extra = dot(quarters[0], mine[:, :quarter])
        for i in range(1, 4):
            extra = extra + dot(quarters[i], mine[:, i * quarter : (i + 1) * quarter])
        ref[:, width:] = extra.astype(BF16)


def to_rows(v):
    size = v.shape[0]
    eye = pick(iota((size, size), 0) == iota((size, size), 1))
    return dot(v, eye, ((0,), (0,)))


def inner_kernel(near_ref, far_ref, values_ref, out_ref):
    rows, width = values_ref.shape
    quarter = width // 4
    span = width + quarter
    n = HALF * CAP
    maps = unpacking()
    sums = []
    for half, (ref, at) in enumerate(((near_ref, span), (far_ref, 0))):
        inner = jnp.zeros((n, 1), F32)
        for i, block in enumerate(unpack(maps, ref[:, at : at + width], ref[:, at + width : at + span])):
            value = values_ref[half * n : (half + 1) * n, i * quarter : (i + 1) * quarter].astype(F32)
            inner = inner + jnp.sum(block * value, axis=1, keepdims=True)
        sums.append(inner)
    turned = to_rows(spread(iota((rows, 128), 1), 0, jnp.concatenate(sums, axis=0)).astype(BF16))
    inner = turned[0:1] + turned[1:2] + turned[2:3]
    for i in range(N_CTX):
        out_ref[i] = jnp.broadcast_to(inner, out_ref.shape[1:])


def grad_kernel(inner_ref, full_ref, x_ref, out_ref):
    hid = full_ref.shape[2] - 128
    small = jnp.concatenate([full_ref[i, :, hid:].astype(F32) for i in range(N_CTX)], axis=0).astype(BF16)
    turned = to_rows(small)
    score = turned[0:1] + turned[1:2] + turned[2:3]
    inner = inner_ref[0]
    for i in range(1, N_CTX):
        inner = inner + inner_ref[i]
    slope = inner * (score * (1.0 - score))
    a, b, c = pieces(slope)
    line = iota(slope.shape, 0)
    slope = jnp.where(line == 0, a.astype(F32), jnp.where(line == 1, b.astype(F32), jnp.where(line == 2, c.astype(F32), 0.0)))
    grad = jnp.sum(dot(slope.astype(BF16), x_ref[...]), axis=0, keepdims=True)
    copies = out_ref.shape[0]
    for j in range(8):
        out_ref[:, j, :] = jnp.broadcast_to(grad[:, j * 128 : (j + 1) * 128], (copies, 128))


def merge_kernel(near_ref, far_ref, grads_ref, out_ref):
    span = near_ref.shape[1]
    out_ref[:, :span] = near_ref[...]
    out_ref[:, span : 2 * span] = far_ref[...]
    parts = grads_ref.shape[0] // 2
    for zh in range(2):
        total = grads_ref[zh]
        for k in range(1, parts):
            total = total + grads_ref[2 * k + zh]
        high = total.astype(BF16)
        low = (total - high.astype(F32)).astype(BF16)
        for at, v in ((2 * span + zh * 128, high), (2 * span + 256 + zh * 128, low)):
            out_ref[:, at : at + 128] = jnp.concatenate([v.astype(F32)] * HALF, axis=0).astype(BF16)


def out_kernel(zh_ref, route_ref, fin_ref, out_ref, grad_ref):
    far, place, position = where_to(zh_ref[0], route_ref[...])
    count, width = out_ref.shape
    quarter = width // 4
    span = width + quarter
    n = HALF * BACK
    slots = iota((count, n), 1)
    base = place * BACK
    for half in range(2):
        here = far == half
        of_main = pick((slots == base + position) & (position < BACK) & here)
        main = dot(of_main, fin_ref[:, half * span : half * span + width])
        extra = fin_ref[:, half * span + width : (half + 1) * span]
        for i in range(4):
            cols = slice(i * quarter, (i + 1) * quarter)
            of_extra = pick((slots == base + (position - BACK) * 4 + i) & (position >= BACK) & here)
            value = main[:, cols] + dot(of_extra, extra)
            if half:
                value = value + out_ref[:, cols].astype(F32)
            out_ref[:, cols] = value.astype(BF16)
    r = iota((n, 128), 0)
    col = iota((n, 128), 1)
    j, e = col // N_EXP, col % N_EXP
    turned = jnp.zeros((128, 128), F32)
    for zh in range(2):
        take = pick((r == (e % HALF) * BACK + j) & (e // HALF == zh))
        for part in range(2):
            at = 2 * span + part * 256 + zh * 128
            turned = turned + dot(fin_ref[:, at : at + 128], take, ((0,), (0,)))
    for k in range(8):
        grad_ref[k * 128 : (k + 1) * 128, :] = turned[:, k * N_EXP : (k + 1) * N_EXP]


def call(kernel, out, scalars=0, scratch=()):
    def run(*args):
        smem = pl.BlockSpec(memory_space=pltpu.SMEM)
        vmem = pl.BlockSpec(memory_space=pltpu.VMEM)
        specs = [smem if i < scalars else vmem for i in range(len(args))]
        return pl.pallas_call(
            kernel,
            in_specs=specs,
            out_specs=jax.tree.map(lambda _: vmem, out),
            out_shape=out,
            scratch_shapes=scratch,
            compiler_params=pltpu.CompilerParams(vmem_limit_bytes=16 * 1024 * 1024),
        )(*args)

    return run


def as_one_step(turns, body, state):
    out = lax.while_loop(lambda s: s[0] < turns, lambda s: (s[0] + 1, *body(*s[1:])), (jnp.int32(0), *state))
    return out[1:]


def shards(tokens, routes, router_weight, gate_weight, up_weight, down_weight, cotangent):
    count, width = tokens.shape
    hid = gate_weight.shape[2]
    shape = jax.ShapeDtypeStruct
    zh = lax.axis_index("zh").astype(I32)
    expert = zh * HALF + lax.axis_index("y") * 2 + lax.axis_index("core")
    zh = zh.reshape(1)
    turns = 1 + lax.axis_index("ctx").astype(I32) // N_CTX
    span = width + width // 4
    rows = N_EXP * CAP
    exchange = functools.partial(lax.all_to_all, axis_name=IN_Z, split_axis=0, concat_axis=0, tiled=True)
    over_ctx = functools.partial(lax.all_to_all, axis_name="ctx", split_axis=0, concat_axis=0, tiled=True)

    chunk = shape((HALF * BACK, span), BF16)
    x_far, near = call(pack_kernel, (chunk, shape((HALF * BACK, 3 * span), BF16)), 1)(zh, routes, tokens, cotangent)
    x_far = lax.ppermute(x_far, PAIR, PAIR_PERM)
    (near,) = as_one_step(turns, lambda v: (exchange(v),), (near,))
    cot_far = lax.ppermute(near[:, 2 * span :], PAIR, PAIR_PERM)

    router_col = lax.dynamic_slice(router_weight, (lax.axis_index("ctx") * width, expert), (width, 1))
    router_col = jnp.concatenate([*pieces(router_col), jnp.zeros((width, 125), BF16)], axis=1)
    part = shape((N_CTX, rows // N_CTX, 2 * hid + 128), BF16)
    wide = shape((rows, width), BF16)

    def to_hidden(x_far, x, full):
        x_far = exchange(x_far)
        sums, x = call(up_kernel, (part, wide))(near, x_far, router_col, gate_weight[0], up_weight[0])
        mine = over_ctx(sums)
        full = over_ctx(call(hidden_kernel, shape(full.shape, BF16))(mine))
        return x_far, x, full

    full = jnp.zeros((N_CTX, rows // N_CTX, hid + 128), BF16)
    _, x, full = as_one_step(turns, to_hidden, (x_far, jnp.zeros((rows, width), BF16), full))

    scratch = [pltpu.VMEM((rows, width), BF16)]
    near_back, far, values = call(down_kernel, (chunk, chunk, wide), scratch=scratch)(full, down_weight[0])
    far = lax.ppermute(far, PAIR, PAIR_PERM)
    inner = over_ctx(call(inner_kernel, shape((N_CTX, 8, rows), F32))(near, cot_far, values))
    grad = call(grad_kernel, shape((lax.axis_size(ALL_Z), 8, width // 8), F32))(inner, full, x)

    (grads,) = as_one_step(turns, lambda v: (lax.all_to_all(v, ALL_Z, 0, 0, tiled=True),), (grad,))
    fin = exchange(call(merge_kernel, shape((HALF * BACK, 2 * span + 512), BF16))(near_back, far, grads))
    return call(out_kernel, (shape((count, width), BF16), shape((width, N_EXP), F32)), 1)(zh, routes, fin)


def solution(mesh):
    fine = Mesh(mesh.devices.reshape(MESH), NAMES)
    ep = ("zh", "y", "core")
    return jax.shard_map(
        shards,
        mesh=fine,
        in_specs=(
            P(TOK, "ctx"),
            P(TOK, None),
            P(),
            P(ep, "ctx", None),
            P(ep, "ctx", None),
            P(ep, None, "ctx"),
            P(TOK, "ctx"),
        ),
        out_specs=(P(TOK, "ctx"), P("ctx", None)),
        check_vma=False,
    )
```

time: 212 us -> 205 us (0.967)
  the two profiles are of different devices: /device:TPU:64 before, /device:TPU:1 now
where the time goes in v3:
time: 205 us; the launch traced here: 204 us
  waiting for transfers between devices  71.2 us (35%)
  starting transfers between devices  59.2 us (29%)
  blocking collectives  49.2 us (24%)
  Pallas kernels  13.1 us (6%)
  local copies, waits for them, and re-layouts  9.67 us (5%)
    ppermute x1, waiting for transfers between devices, shards(): x_far = lax.ppermute(x_far, PAIR, PAIR_PERM)  30.7 us
    all_to_all x1, waiting for transfers between devices, shards(): lax.all_to_all(v, ALL_Z, 0, 0, tiled=True)  25.3 us
    ppermute x1, starting transfers between devices, shards(): x_far = lax.ppermute(x_far, PAIR, PAIR_PERM)  23.5 us
    all_to_all x1, blocking collectives, shards(): exchange(call(merge_kernel, shape((HALF * BACK, 2 * span + 512), BF16))(n...  17 us
    all_to_all x1, blocking collectives, to_hidden(): mine = over_ctx(sums)  14 us
    pallas_call x8, Pallas kernels, run(): pl.pallas_call(kernel, in_specs=specs, out_specs=jax.tree.map(lambda _: v...  13.1 us
    ppermute x1, starting transfers between devices, shards(): far = lax.ppermute(far, PAIR, PAIR_PERM)  12.8 us
    all_to_all x1, blocking collectives, to_hidden(): x_far = exchange(x_far)  11.5 us
  transfers between devices with their start and end apart: 6, of which 4 were waited for; matrix products, arithmetic and copies ran while one was open for 3% of the time, Pallas kernels for 4%

profile of v3, /device:TPU:1, one launch (start us, length us, event | category | flops | bytes accessed | tf_op | source)
XLA Modules:
  0.0 204.2 jit_solution(6847174482925338218)
XLA Ops:
  1.4 0.9 copy-done.1
  2.4 0.9 copy-done.2
  3.3 1.6 shard_map.86
  4.9 23.5 %collective-permute-start = (bf16[64,1280]{1,0:T(8,128)(2,1)S(1)}, bf16[64,1280]{1,0:T(8,128)(2,1)S(1)}, u32[]{:S(2)}, u32[]{:S(2)}) collective-permute-start(bf16[64,1280]{1,0:T(8,128)(2,1)S(1)} %get-tuple-element.92), channel_id=1, source_target_pairs={{0,520},{520,0},{8,512},{512,8},{1,521},{521,1},{9,513},{513,9},{2... | collective-permute-start | bytes 491528 | tf_op jit(solution)/shard_map/ppermute | solution.py:311
  28.5 15.4 %while.34 = (s32[]{:T(128)}, bf16[64,3840]{1,0:T(8,128)(2,1)}, s32[]{:T(128)}, s32[]{:T(128)}) while((s32[]{:T(128)}, bf16[64,3840]{1,0:T(8,128)(2,1)}, s32[]{:T(128)}, s32[]{:T(128)}) %tuple.49), condition=%wide.region_1.2_spmd, body=%wide.region_0.1_spmd.sunk | while | flops 2 | bytes 2457685 | solution.py:292
  28.5 5.4 %all-to-all-start = ((bf16[8,8,3840]{2,1,0:T(8,128)(2,1)}), bf16[8,8,3840]{2,1,0:T(8,128)(2,1)S(1)}, u32[]{:S(2)}, u32[]{:S(2)}) async-start(bf16[8,8,3840]{2,1,0:T(8,128)(2,1)} %bitcast.16), calls=%async_computation | async-start | bytes 983040 | tf_op jit(solution)/shard_map/while/body/all_to_all | solution.py:312
  33.9 9.1 %all-to-all-done = bf16[8,8,3840]{2,1,0:T(8,128)(2,1)S(1)} async-done(((bf16[8,8,3840]{2,1,0:T(8,128)(2,1)}), bf16[8,8,3840]{2,1,0:T(8,128)(2,1)S(1)}, u32[]{:S(2)}, u32[]{:S(2)}) %all-to-all-start) | async-done | bytes 491552 | tf_op jit(solution)/shard_map/while/body/all_to_all | solution.py:312
  43.1 0.8 copy.24
  43.9 0.9 slice.3
  44.8 2.9 %collective-permute-start.2 = (bf16[64,1280]{1,0:T(8,128)(2,1)S(1)}, bf16[64,1280]{1,0:T(8,128)(2,1)S(1)}, u32[]{:S(2)}, u32[]{:S(2)}) collective-permute-start(bf16[64,1280]{1,0:T(8,128)(2,1)S(1)} %slice.3), channel_id=1, source_target_pairs={{0,520},{520,0},{8,512},{512,8},{1,521},{521,1},{9,513},{513,9},{2... | collective-permute-start | bytes 491528 | tf_op jit(solution)/shard_map/ppermute | solution.py:313
  47.7 0.8 fusion
  48.5 0.8 dynamic_slice.12
  50.3 30.7 %collective-permute-done = bf16[64,1280]{1,0:T(8,128)(2,1)S(1)} collective-permute-done((bf16[64,1280]{1,0:T(8,128)(2,1)S(1)}, bf16[64,1280]{1,0:T(8,128)(2,1)S(1)}, u32[]{:S(2)}, u32[]{:S(2)}) %collective-permute-start) | collective-permute-done | bytes 163872 | tf_op jit(solution)/shard_map/ppermute | solution.py:311
  82.6 40.2 %while.35 = (s32[]{:T(128)}, bf16[64,1280]{1,0:T(8,128)(2,1)S(1)}, bf16[160,1024]{1,0:T(8,128)(2,1)}, bf16[4,40,1152]{2,1,0:T(8,128)(2,1)}, s32[]{:T(128)}, /*in...) while((s32[]{:T(128)}, bf16[64,1280]{1,0:T(8,128)(2,1)S(1)}, ...), condition=%wide.region_3.4_spmd, body=%wide.region_2.3_spmd.sunk | while | flops 2 | bytes 4628641 | solution.py:292
  82.6 11.5 %all_to_all.57 = bf16[8,8,1280]{2,1,0:T(8,128)(2,1)S(1)} all-to-all(bf16[8,8,1280]{2,1,0:T(8,128)(2,1)S(1)} %copy.45), channel_id=1, replica_groups=mesh['dh'=2,'dl'=8,'ctx'=4,'zh'=2,'y'=4,'core'=2] {'y','core'}, dimensions={0} | all-to-all | bytes 327680 | tf_op jit(solution)/shard_map/while/body/all_to_all | solution.py:321
  94.1 3.5 %body.2 = (bf16[4,40,2176]{2,1,0:T(8,128)(2,1)S(1)}, bf16[160,1024]{1,0:T(8,128)(2,1)}) custom-call(bf16[64,3840]{1,0:T(8,128)(2,1)} %get-tuple-element.272.near_ref, bf16[64,1280]{1,0:T(8,128)(2,1)S(1)} %bitcast.29, bf16[1024,128]{1,0:T(8,128)(2,1)S(1)} %get-tuple-element.273.router_ref, bf16[1024,1024]{1,0:T(8,128)(2,1)} %bitcast.25, ...), custom_call_target="tpu_custom_call" | custom-call | tf_op jit(solution)/shard_map/while/body/pallas_call | solution.py:279
  97.6 14.0 %all_to_all.58.mine_ref = bf16[4,40,2176]{2,1,0:T(8,128)(2,1)S(1)} all-to-all(bf16[4,40,2176]{2,1,0:T(8,128)(2,1)S(1)} %get-tuple-element.229), channel_id=1, replica_groups=mesh['dh'=2,'dl'=8,'ctx'=4,'zh'=2,'y'=4,'core'=2] {'ctx'}, dimensions={0} | all-to-all | bytes 1392640 | tf_op jit(solution)/shard_map/while/body/all_to_all | solution.py:323
  111.6 0.9 body.3
  112.5 3.5 %all-to-all-start.3 = ((bf16[4,40,1152]{2,1,0:T(8,128)(2,1)}), bf16[4,40,1152]{2,1,0:T(8,128)(2,1)S(1)}, u32[]{:S(2)}, u32[]{:S(2)}) async-start(bf16[4,40,1152]{2,1,0:T(8,128)(2,1)} %body.3), calls=%async_computation.3 | async-start | bytes 737280 | tf_op jit(solution)/shard_map/while/body/all_to_all | solution.py:324
  116.0 6.1 %all-to-all-done.3 = bf16[4,40,1152]{2,1,0:T(8,128)(2,1)S(1)} async-done(((bf16[4,40,1152]{2,1,0:T(8,128)(2,1)}), bf16[4,40,1152]{2,1,0:T(8,128)(2,1)S(1)}, u32[]{:S(2)}, u32[]{:S(2)}) %all-to-all-start.3) | async-done | bytes 368672 | tf_op jit(solution)/shard_map/while/body/all_to_all | solution.py:324
  122.8 1.8 shard_map.87
  124.6 12.8 %collective-permute-start.1 = (bf16[64,1280]{1,0:T(8,128)(2,1)S(1)}, bf16[64,1280]{1,0:T(8,128)(2,1)S(1)}, u32[]{:S(2)}, u32[]{:S(2)}) collective-permute-start(bf16[64,1280]{1,0:T(8,128)(2,1)S(1)} %get-tuple-element.97), channel_id=1, source_target_pairs={{0,520},{520,0},{8,512},{512,8},{1,521},{521,1},{9,513},{513,9},{2... | collective-permute-start | bytes 491528 | tf_op jit(solution)/shard_map/ppermute | solution.py:332
  137.5 1.7 shard_map.88
  139.2 6.7 %all_to_all.55.inner_ref = f32[4,8,160]{2,1,0:T(8,128)S(1)} all-to-all(f32[4,8,160]{2,1,0:T(8,128)S(1)} %shard_map.88), channel_id=1, replica_groups=mesh['dh'=2,'dl'=8,'ctx'=4,'zh'=2,'y'=4,'core'=2] {'ctx'}, dimensions={0} | all-to-all | bytes 40960 | tf_op jit(solution)/shard_map/all_to_all | solution.py:333
  145.9 1.0 shard_map.89
  146.9 37.0 %while.36 = (s32[]{:T(128)}, f32[32,8,128]{2,1,0:T(8,128)}, s32[]{:T(128)}, s32[]{:T(128)}) while((s32[]{:T(128)}, f32[32,8,128]{2,1,0:T(8,128)}, s32[]{:T(128)}, s32[]{:T(128)}) %tuple.55), condition=%wide.region_5.6_spmd, body=%wide.region_4.5_spmd.sunk | while | flops 2 | bytes 655445 | solution.py:292
  146.9 11.1 %all-to-all-start.4 = ((f32[32,8,128]{2,1,0:T(8,128)}), f32[32,8,128]{2,1,0:T(8,128)S(1)}, u32[]{:S(2)}, u32[]{:S(2)}) async-start(f32[32,8,128]{2,1,0:T(8,128)} %get-tuple-element.280), calls=%async_computation.4 | async-start | bytes 262144 | tf_op jit(solution)/shard_map/while/body/all_to_all | solution.py:336
  158.0 25.3 %all-to-all-done.4 = f32[32,8,128]{2,1,0:T(8,128)S(1)} async-done(((f32[32,8,128]{2,1,0:T(8,128)}), f32[32,8,128]{2,1,0:T(8,128)S(1)}, u32[]{:S(2)}, u32[]{:S(2)}) %all-to-all-start.4) | async-done | bytes 131104 | tf_op jit(solution)/shard_map/while/body/all_to_all | solution.py:336
  183.9 1.0 shard_map.90
  184.9 17.0 %all_to_all.56 = bf16[8,8,3072]{2,1,0:T(8,128)(2,1)S(1)} all-to-all(bf16[8,8,3072]{2,1,0:T(8,128)(2,1)S(1)} %bitcast.24), channel_id=1, replica_groups=mesh['dh'=2,'dl'=8,'ctx'=4,'zh'=2,'y'=4,'core'=2] {'y','core'}, dimensions={0} | all-to-all | bytes 786432 | tf_op jit(solution)/shard_map/all_to_all | solution.py:337
  201.9 1.5 shard_map.91
  203.4 0.8 copy.18
  (23 shorter events, 4.7 us)
Async XLA Ops:
  1.4 0.9 copy-start.1
  2.3 0.9 copy-start.2
  4.9 76.1 %collective-permute-start = (bf16[64,1280]{1,0:T(8,128)(2,1)S(1)}, bf16[64,1280]{1,0:T(8,128)(2,1)S(1)}, u32[]{:S(2)}, u32[]{:S(2)}) collective-permute-start(bf16[64,1280]{1,0:T(8,128)(2,1)S(1)} %get-tuple-element.92), channel_id=1, source_target_pairs={{0,520},{520,0},{8,512},{512,8},{1,521},{521,1},{9,513},{513,9},{2... | collective-permute-start | bytes 491528 | tf_op jit(solution)/shard_map/ppermute | solution.py:311
  28.5 14.6 %all-to-all-start = ((bf16[8,8,3840]{2,1,0:T(8,128)(2,1)}), bf16[8,8,3840]{2,1,0:T(8,128)(2,1)S(1)}, u32[]{:S(2)}, u32[]{:S(2)}) async-start(bf16[8,8,3840]{2,1,0:T(8,128)(2,1)} %bitcast.16), calls=%async_computation | async-start | bytes 983040 | tf_op jit(solution)/shard_map/while/body/all_to_all | solution.py:312
  44.8 92.7 %collective-permute-start.2 = (bf16[64,1280]{1,0:T(8,128)(2,1)S(1)}, bf16[64,1280]{1,0:T(8,128)(2,1)S(1)}, u32[]{:S(2)}, u32[]{:S(2)}) collective-permute-start(bf16[64,1280]{1,0:T(8,128)(2,1)S(1)} %slice.3), channel_id=1, source_target_pairs={{0,520},{520,0},{8,512},{512,8},{1,521},{521,1},{9,513},{513,9},{2... | collective-permute-start | bytes 491528 | tf_op jit(solution)/shard_map/ppermute | solution.py:313
  82.6 40.2 %copy-start = (bf16[1,1024,1024]{2,1,0:T(8,128)(2,1)S(1)}, bf16[1,1024,1024]{2,1,0:T(8,128)(2,1)}, u32[]{:S(2)}) copy-start(bf16[1,1024,1024]{2,1,0:T(8,128)(2,1)} %param.18) | copy-start | bytes 6291460
  112.5 9.5 %all-to-all-start.3 = ((bf16[4,40,1152]{2,1,0:T(8,128)(2,1)}), bf16[4,40,1152]{2,1,0:T(8,128)(2,1)S(1)}, u32[]{:S(2)}, u32[]{:S(2)}) async-start(bf16[4,40,1152]{2,1,0:T(8,128)(2,1)} %body.3), calls=%async_computation.3 | async-start | bytes 737280 | tf_op jit(solution)/shard_map/while/body/all_to_all | solution.py:324
  122.1 0.7 copy-start.3
  122.8 23.1 %copy-start.4 = (bf16[4,40,1152]{2,1,0:T(8,128)(2,1)S(1)}, bf16[4,40,1152]{2,1,0:T(8,128)(2,1)}, u32[]{:S(2)}) copy-start(bf16[4,40,1152]{2,1,0:T(8,128)(2,1)} %get-tuple-element.95.full_ref) | copy-start | bytes 1105924
  122.8 23.1 %copy-start.5 = (bf16[160,1024]{1,0:T(8,128)(2,1)S(1)}, bf16[160,1024]{1,0:T(8,128)(2,1)}, u32[]{:S(2)}) copy-start(bf16[160,1024]{1,0:T(8,128)(2,1)} %get-tuple-element.99.x_ref) | copy-start | bytes 983044
  124.6 59.3 %collective-permute-start.1 = (bf16[64,1280]{1,0:T(8,128)(2,1)S(1)}, bf16[64,1280]{1,0:T(8,128)(2,1)S(1)}, u32[]{:S(2)}, u32[]{:S(2)}) collective-permute-start(bf16[64,1280]{1,0:T(8,128)(2,1)S(1)} %get-tuple-element.97), channel_id=1, source_target_pairs={{0,520},{520,0},{8,512},{512,8},{1,521},{521,1},{9,513},{513,9},{2... | collective-permute-start | bytes 491528 | tf_op jit(solution)/shard_map/ppermute | solution.py:332
  146.9 36.4 %all-to-all-start.4 = ((f32[32,8,128]{2,1,0:T(8,128)}), f32[32,8,128]{2,1,0:T(8,128)S(1)}, u32[]{:S(2)}, u32[]{:S(2)}) async-start(f32[32,8,128]{2,1,0:T(8,128)} %get-tuple-element.280), calls=%async_computation.4 | async-start | bytes 262144 | tf_op jit(solution)/shard_map/while/body/all_to_all | solution.py:336

commit v4 on v3

--- a/solution.py
+++ b/solution.py
@@ -82,7 +82,8 @@
     return whole, quarters
 
 
-def pack_kernel(zh_ref, route_ref, tok_ref, cot_ref, far_ref, near_ref):
+def pack_kernel(zh_ref, route_ref, tok_ref, cot_ref, far_ref, near_ref, full_ref):
+    full_ref[...] = jnp.zeros(full_ref.shape, BF16)
     far, place, position = where_to(zh_ref[0], route_ref[...])
     count, width = tok_ref.shape
     quarter = width // 4
@@ -157,22 +158,42 @@
         out_ref[i, :, hid:] = small
 
 
-def down_kernel(full_ref, down_ref, near_ref, far_ref, values_ref, rows_ref):
+def to_rows(v):
+    size = v.shape[0]
+    eye = pick(iota((size, size), 0) == iota((size, size), 1))
+    return dot(v, eye, ((0,), (0,)))
+
+
+def down_kernel(full_ref, cot_near_ref, cot_far_ref, down_ref, near_ref, far_ref, inner_ref, values_ref):
     hid, width = down_ref.shape
     quarter = width // 4
+    span = width + quarter
     full = jnp.concatenate([full_ref[i].astype(F32) for i in range(N_CTX)], axis=0)
-    score = gathered(iota((full.shape[0], 128), 1), 0, full[:, hid:])
-    values = dot(full[:, :hid].astype(BF16), down_ref[...]).astype(BF16)
-    values_ref[...] = values
-    rows_ref[...] = (score * values.astype(F32)).astype(BF16)
+    rows = full.shape[0]
+    lane = iota((rows, 128), 1)
+    score = gathered(lane, 0, full[:, hid:])
+    values_ref[...] = dot(full[:, :hid].astype(BF16), down_ref[...]).astype(BF16)
     n = HALF * CAP
+    maps = unpacking()
+    sums = []
+    for half, (ref, at) in enumerate(((cot_near_ref, span), (cot_far_ref, 0))):
+        inner = jnp.zeros((n, 1), F32)
+        for i, block in enumerate(unpack(maps, ref[:, at : at + width], ref[:, at + width : at + span])):
+            value = values_ref[half * n : (half + 1) * n, i * quarter : (i + 1) * quarter].astype(F32)
+            inner = inner + jnp.sum(block * value, axis=1, keepdims=True)
+        sums.append(inner)
+    turned = to_rows(spread(lane, 0, jnp.concatenate(sums, axis=0)).astype(BF16))
+    inner = turned[0:1] + turned[1:2] + turned[2:3]
+    for i in range(N_CTX):
+        inner_ref[i] = jnp.broadcast_to(inner, inner_ref.shape[1:])
     slot, r = iota((HALF * BACK, n), 0), iota((HALF * BACK, n), 1)
     src = tenth(r)
     p = r - src * CAP
     whole = pick((slot == src * BACK + p) & (p < BACK))
     quarters = [pick((slot == src * BACK + (p - BACK) * 4 + i) & (p >= BACK)) for i in range(4)]
     for half, ref in enumerate((near_ref, far_ref)):
-        mine = rows_ref[half * n : (half + 1) * n, :]
+        part = slice(half * n, (half + 1) * n)
+        mine = (score[part] * values_ref[part, :].astype(F32)).astype(BF16)
         ref[:, :width] = dot(whole, mine).astype(BF16)
         extra = dot(quarters[0], mine[:, :quarter])
         for i in range(1, 4):
@@ -180,29 +201,8 @@
         ref[:, width:] = extra.astype(BF16)
 
 
-def to_rows(v):
-    size = v.shape[0]
-    eye = pick(iota((size, size), 0) == iota((size, size), 1))
-    return dot(v, eye, ((0,), (0,)))
-
-
-def inner_kernel(near_ref, far_ref, values_ref, out_ref):
-    rows, width = values_ref.shape
-    quarter = width // 4
-    span = width + quarter
-    n = HALF * CAP
-    maps = unpacking()
-    sums = []
-    for half, (ref, at) in enumerate(((near_ref, span), (far_ref, 0))):
-        inner = jnp.zeros((n, 1), F32)
-        for i, block in enumerate(unpack(maps, ref[:, at : at + width], ref[:, at + width : at + span])):
-            value = values_ref[half * n : (half + 1) * n, i * quarter : (i + 1) * quarter].astype(F32)
-            inner = inner + jnp.sum(block * value, axis=1, keepdims=True)
-        sums.append(inner)
-    turned = to_rows(spread(iota((rows, 128), 1), 0, jnp.concatenate(sums, axis=0)).astype(BF16))
-    inner = turned[0:1] + turned[1:2] + turned[2:3]
-    for i in range(N_CTX):
-        out_ref[i] = jnp.broadcast_to(inner, out_ref.shape[1:])
+def relay_kernel(near_ref, x_far_ref, out_ref):
+    out_ref[...] = near_ref[:, near_ref.shape[1] - out_ref.shape[1] :]
 
 
 def grad_kernel(inner_ref, full_ref, x_ref, out_ref):
@@ -219,8 +219,12 @@
     slope = jnp.where(line == 0, a.astype(F32), jnp.where(line == 1, b.astype(F32), jnp.where(line == 2, c.astype(F32), 0.0)))
     grad = jnp.sum(dot(slope.astype(BF16), x_ref[...]), axis=0, keepdims=True)
     copies = out_ref.shape[0]
+    lines = []
     for j in range(8):
-        out_ref[:, j, :] = jnp.broadcast_to(grad[:, j * 128 : (j + 1) * 128], (copies, 128))
+        lines.append(grad[:, j * 128 : (j + 1) * 128])
+    block = jnp.concatenate(lines, axis=0).astype(out_ref.dtype)
+    for k in range(copies):
+        out_ref[k] = block
 
 
 def merge_kernel(near_ref, far_ref, grads_ref, out_ref):
@@ -229,9 +233,9 @@
     out_ref[:, span : 2 * span] = far_ref[...]
     parts = grads_ref.shape[0] // 2
     for zh in range(2):
-        total = grads_ref[zh]
+        total = grads_ref[zh].astype(F32)
         for k in range(1, parts):
-            total = total + grads_ref[2 * k + zh]
+            total = total + grads_ref[2 * k + zh].astype(F32)
         high = total.astype(BF16)
         low = (total - high.astype(F32)).astype(BF16)
         for at, v in ((2 * span + zh * 128, high), (2 * span + 256 + zh * 128, low)):
@@ -258,17 +262,16 @@
             if half:
                 value = value + out_ref[:, cols].astype(F32)
             out_ref[:, cols] = value.astype(BF16)
-    r = iota((n, 128), 0)
-    col = iota((n, 128), 1)
-    j, e = col // N_EXP, col % N_EXP
-    turned = jnp.zeros((128, 128), F32)
-    for zh in range(2):
-        take = pick((r == (e % HALF) * BACK + j) & (e // HALF == zh))
-        for part in range(2):
-            at = 2 * span + part * 256 + zh * 128
-            turned = turned + dot(fin_ref[:, at : at + 128], take, ((0,), (0,)))
-    for k in range(8):
-        grad_ref[k * 128 : (k + 1) * 128, :] = turned[:, k * N_EXP : (k + 1) * N_EXP]
+    line, r = iota((N_EXP, n), 0), iota((N_EXP, n), 1)
+    place = jnp.where(line >= HALF, line - HALF, line)
+    for j in range(8):
+        total = jnp.zeros((N_EXP, 128), F32)
+        for zh in range(2):
+            take = pick((r == place * BACK + j) & ((line >= HALF) == (zh == 1)))
+            for part in range(2):
+                at = 2 * span + part * 256 + zh * 128
+                total = total + dot(take, fin_ref[:, at : at + 128])
+        grad_ref[:, j * 128 : (j + 1) * 128] = total
 
 
 def call(kernel, out, scalars=0, scratch=()):
@@ -307,35 +310,40 @@
     over_ctx = functools.partial(lax.all_to_all, axis_name="ctx", split_axis=0, concat_axis=0, tiled=True)
 
     chunk = shape((HALF * BACK, span), BF16)
-    x_far, near = call(pack_kernel, (chunk, shape((HALF * BACK, 3 * span), BF16)), 1)(zh, routes, tokens, cotangent)
+    x_far, near, full = call(
+        pack_kernel,
+        (chunk, shape((HALF * BACK, 3 * span), BF16), shape((N_CTX, rows // N_CTX, hid + 128), BF16)),
+        1,
+    )(zh, routes, tokens, cotangent)
     x_far = lax.ppermute(x_far, PAIR, PAIR_PERM)
     (near,) = as_one_step(turns, lambda v: (exchange(v),), (near,))
-    cot_far = lax.ppermute(near[:, 2 * span :], PAIR, PAIR_PERM)
+    cot_far = lax.ppermute(call(relay_kernel, chunk)(near, x_far), PAIR, PAIR_PERM)
+    x_far = exchange(x_far)
 
     router_col = lax.dynamic_slice(router_weight, (lax.axis_index("ctx") * width, expert), (width, 1))
     router_col = jnp.concatenate([*pieces(router_col), jnp.zeros((width, 125), BF16)], axis=1)
     part = shape((N_CTX, rows // N_CTX, 2 * hid + 128), BF16)
-    wide = shape((rows, width), BF16)
-
-    def to_hidden(x_far, x, full):
-        x_far = exchange(x_far)
-        sums, x = call(up_kernel, (part, wide))(near, x_far, router_col, gate_weight[0], up_weight[0])
+    sums, x = call(up_kernel, (part, shape((rows, width), BF16)))(near, x_far, router_col, gate_weight[0], up_weight[0])
+
+    def to_hidden(sums, full):
         mine = over_ctx(sums)
-        full = over_ctx(call(hidden_kernel, shape(full.shape, BF16))(mine))
-        return x_far, x, full
-
-    full = jnp.zeros((N_CTX, rows // N_CTX, hid + 128), BF16)
-    _, x, full = as_one_step(turns, to_hidden, (x_far, jnp.zeros((rows, width), BF16), full))
-
-    scratch = [pltpu.VMEM((rows, width), BF16)]
-    near_back, far, values = call(down_kernel, (chunk, chunk, wide), scratch=scratch)(full, down_weight[0])
+        return mine, over_ctx(call(hidden_kernel, shape(full.shape, BF16))(mine))
+
+    _, full = as_one_step(turns, to_hidden, (sums, full))
+
+    near_back, far, inner = call(
+        down_kernel,
+        (chunk, chunk, shape((N_CTX, 8, rows), F32)),
+        scratch=[pltpu.VMEM((rows, width), BF16)],
+    )(full, near, cot_far, down_weight[0])
     far = lax.ppermute(far, PAIR, PAIR_PERM)
-    inner = over_ctx(call(inner_kernel, shape((N_CTX, 8, rows), F32))(near, cot_far, values))
-    grad = call(grad_kernel, shape((lax.axis_size(ALL_Z), 8, width // 8), F32))(inner, full, x)
+    inner = over_ctx(inner)
+    grad = call(grad_kernel, shape((lax.axis_size(ALL_Z), 8, width // 8), BF16))(inner, full, x)
 
     (grads,) = as_one_step(turns, lambda v: (lax.all_to_all(v, ALL_Z, 0, 0, tiled=True),), (grad,))
     fin = exchange(call(merge_kernel, shape((HALF * BACK, 2 * span + 512), BF16))(near_back, far, grads))
-    return call(out_kernel, (shape((count, width), BF16), shape((width, N_EXP), F32)), 1)(zh, routes, fin)
+    block_out, grad = call(out_kernel, (shape((count, width), BF16), shape((N_EXP, width), F32)), 1)(zh, routes, fin)
+    return block_out, grad.T
 
 
 def solution(mesh):

time: 205 us -> 206 us (level)
  starting transfers between devices: 59.2 us -> 89.5 us
  waiting for transfers between devices: 71.2 us -> 53 us
  blocking collectives: 49.2 us -> 37.2 us
    ppermute x1, starting transfers between devices: 2.86 us -> 37.6 us  [shards(): lax.ppermute(call(relay_kernel, chunk)(near, x_far), PAIR, PAIR_PERM)]
    ppermute x1, waiting for transfers between devices: 30.7 us -> 10.6 us  [shards(): x_far = lax.ppermute(x_far, PAIR, PAIR_PERM)]
    all_to_all x2 -> x1, blocking collectives: 18.2 us -> 6.65 us  [shards(): inner = over_ctx(inner)]
    ppermute x1, starting transfers between devices: 12.8 us -> 1.92 us  [shards(): far = lax.ppermute(far, PAIR, PAIR_PERM)]
    all_to_all x1 -> x2, starting transfers between devices: 3.46 us -> 9.17 us  [the longest x1 5.71 us: shards(): x_far = exchange(x_far)]
    all_to_all x1 -> x2, waiting for transfers between devices: 6.06 us -> 10.4 us  [the longest x1 6.06 us: to_hidden(): return (mine, over_ctx(call(hidden_kernel, shape(full.shape, BF16))(mine)))]
    all_to_all x1, waiting for transfers between devices: 25.3 us -> 22.8 us  [shards(): lax.all_to_all(v, ALL_Z, 0, 0, tiled=True)]
    while x5 -> x7, local copies, waits for them, and re-layouts: 2.19 us -> 4.28 us
  transfers between devices with their start and end apart: 6 -> 7, of which waited for: 4 -> 5; matrix products, arithmetic and copies ran while one was open for 3% -> 3% of each run, Pallas kernels for 4% -> 2%
where the time goes in v4:
time: 206 us; the launch traced here: 205 us
  starting transfers between devices  89.5 us (43%)
  waiting for transfers between devices  53 us (26%)
  blocking collectives  37.2 us (18%)
  Pallas kernels  12.7 us (6%)
  local copies, waits for them, and re-layouts  9.69 us (5%)
    ppermute x1, starting transfers between devices, shards(): lax.ppermute(call(relay_kernel, chunk)(near, x_far), PAIR, PAIR_PERM)  37.6 us
    ppermute x1, starting transfers between devices, shards(): x_far = lax.ppermute(x_far, PAIR, PAIR_PERM)  23.5 us
    all_to_all x1, waiting for transfers between devices, shards(): lax.all_to_all(v, ALL_Z, 0, 0, tiled=True)  22.8 us
    all_to_all x1, blocking collectives, shards(): exchange(call(merge_kernel, shape((HALF * BACK, 2 * span + 512), BF16))(n...  16.5 us
    all_to_all x1, blocking collectives, to_hidden(): mine = over_ctx(sums)  14 us
    pallas_call x8, Pallas kernels, run(): pl.pallas_call(kernel, in_specs=specs, out_specs=jax.tree.map(lambda _: v...  12.7 us
    all_to_all x1, starting transfers between devices, shards(): lax.all_to_all(v, ALL_Z, 0, 0, tiled=True)  11.8 us
    ppermute x1, waiting for transfers between devices, shards(): x_far = lax.ppermute(x_far, PAIR, PAIR_PERM)  10.6 us
  transfers between devices with their start and end apart: 7, of which 5 were waited for; matrix products, arithmetic and copies ran while one was open for 3% of the time, Pallas kernels for 2%

profile of v4, /device:TPU:1, one launch (start us, length us, event | category | flops | bytes accessed | tf_op | source)
XLA Modules:
  0.0 204.8 jit_solution(15322221041717690024)
XLA Ops:
  1.4 0.9 copy-done.3
  2.4 0.9 copy-done.4
  3.3 1.7 shard_map.86
  5.0 23.5 %collective-permute-start = (bf16[64,1280]{1,0:T(8,128)(2,1)S(1)}, bf16[64,1280]{1,0:T(8,128)(2,1)}, u32[]{:S(2)}, u32[]{:S(2)}) collective-permute-start(bf16[64,1280]{1,0:T(8,128)(2,1)S(1)} %get-tuple-element.72), channel_id=1, source_target_pairs={{0,520},{520,0},{8,512},{512,8},{1,521},{521,1},{9,513},{513,9},{2... | collective-permute-start | bytes 491528 | tf_op jit(solution)/shard_map/ppermute | solution.py:318
  30.6 15.3 %while.32 = (s32[]{:T(128)}, bf16[64,3840]{1,0:T(8,128)(2,1)}, s32[]{:T(128)}, s32[]{:T(128)}) while((s32[]{:T(128)}, bf16[64,3840]{1,0:T(8,128)(2,1)}, s32[]{:T(128)}, s32[]{:T(128)}) %tuple.50), condition=%wide.region_1.2_spmd, body=%wide.region_0.1_spmd.sunk | while | flops 2 | bytes 2457685 | solution.py:295
  30.6 5.4 %all-to-all-start = ((bf16[8,8,3840]{2,1,0:T(8,128)(2,1)}), bf16[8,8,3840]{2,1,0:T(8,128)(2,1)S(1)}, u32[]{:S(2)}, u32[]{:S(2)}) async-start(bf16[8,8,3840]{2,1,0:T(8,128)(2,1)} %bitcast.13), calls=%async_computation | async-start | bytes 983040 | tf_op jit(solution)/shard_map/while/body/all_to_all | solution.py:319
  36.0 9.1 %all-to-all-done = bf16[8,8,3840]{2,1,0:T(8,128)(2,1)S(1)} async-done(((bf16[8,8,3840]{2,1,0:T(8,128)(2,1)}), bf16[8,8,3840]{2,1,0:T(8,128)(2,1)S(1)}, u32[]{:S(2)}, u32[]{:S(2)}) %all-to-all-start) | async-done | bytes 491552 | tf_op jit(solution)/shard_map/while/body/all_to_all | solution.py:319
  45.9 10.6 %collective-permute-done.x_far_ref = bf16[64,1280]{1,0:T(8,128)(2,1)} collective-permute-done((bf16[64,1280]{1,0:T(8,128)(2,1)S(1)}, bf16[64,1280]{1,0:T(8,128)(2,1)}, u32[]{:S(2)}, u32[]{:S(2)}) %collective-permute-start) | collective-permute-done | bytes 163872 | tf_op jit(solution)/shard_map/ppermute | solution.py:318
  56.5 1.1 shard_map.88
  57.6 37.6 %collective-permute-start.1 = (bf16[64,1280]{1,0:T(8,128)(2,1)S(1)}, bf16[64,1280]{1,0:T(8,128)(2,1)S(1)}, u32[]{:S(2)}, u32[]{:S(2)}) collective-permute-start(bf16[64,1280]{1,0:T(8,128)(2,1)S(1)} %shard_map.88), channel_id=1, source_target_pairs={{0,520},{520,0},{8,512},{512,8},{1,521},{521,1},{9,513},{513,9},{2... | collective-permute-start | bytes 491528 | tf_op jit(solution)/shard_map/ppermute | solution.py:320
  95.2 5.7 %all-to-all-start.4 = ((bf16[8,8,1280]{2,1,0:T(8,128)(2,1)}), bf16[8,8,1280]{2,1,0:T(8,128)(2,1)S(1)}, u32[]{:S(2)}, u32[]{:S(2)}) async-start(bf16[8,8,1280]{2,1,0:T(8,128)(2,1)} %bitcast.3), calls=%async_computation.4 | async-start | bytes 327680 | tf_op jit(solution)/shard_map/all_to_all | solution.py:321
  100.9 1.2 maximum_maximum_fusion.router_ref
  102.1 4.4 %all-to-all-done.4 = bf16[8,8,1280]{2,1,0:T(8,128)(2,1)S(1)} async-done(((bf16[8,8,1280]{2,1,0:T(8,128)(2,1)}), bf16[8,8,1280]{2,1,0:T(8,128)(2,1)S(1)}, u32[]{:S(2)}, u32[]{:S(2)}) %all-to-all-start.4) | async-done | bytes 163872 | tf_op jit(solution)/shard_map/all_to_all | solution.py:321
  106.5 1.6 copy-done.2
  108.1 3.0 %shard_map.87 = (bf16[4,40,2176]{2,1,0:T(8,128)(2,1)}, bf16[160,1024]{1,0:T(8,128)(2,1)S(1)}) custom-call(bf16[64,3840]{1,0:T(8,128)(2,1)} %get-tuple-element.71.near_ref.cot_near_ref, bf16[64,1280]{1,0:T(8,128)(2,1)S(1)} %bitcast.20, bf16[1024,128]{1,0:T(8,128)(2,1)S(1)} %maximum_maximum_fusion.router_ref, bf16[1024,1024]{1,0:T(8,128)(2,1)S(1)} %bitcast.16, ...), custom_call_target="tpu_custom_call" | custom-call | tf_op jit(solution)/shard_map/pallas_call | solution.py:282
  111.1 27.3 %while.33 = (s32[]{:T(128)}, bf16[4,40,2176]{2,1,0:T(8,128)(2,1)}, bf16[4,40,1152]{2,1,0:T(8,128)(2,1)}, s32[]{:T(128)}, s32[]{:T(128)}) while((s32[]{:T(128)}, bf16[4,40,2176]{2,1,0:T(8,128)(2,1)}, bf16[4,40,1152]{2,1,0:T(8,128)(2,1)}, s32[]{:T(128)}, s32[]{:T(128)}) %tuple.53), condition=%wide.region_3.4_spmd, body=%wide.region_2.3_spmd.sunk | while | flops 2 | bytes 8151189 | solution.py:295
  111.1 1.3 copy.39
  112.3 14.0 %all_to_all.58.mine_ref = bf16[4,40,2176]{2,1,0:T(8,128)(2,1)S(1)} all-to-all(bf16[4,40,2176]{2,1,0:T(8,128)(2,1)S(1)} %copy.39), channel_id=1, replica_groups=mesh['dh'=2,'dl'=8,'ctx'=4,'zh'=2,'y'=4,'core'=2] {'ctx'}, dimensions={0} | all-to-all | bytes 1392640 | tf_op jit(solution)/shard_map/while/body/all_to_all | solution.py:329
  126.3 0.9 copy-done.5
  127.2 0.9 body.1
  128.1 3.5 %all-to-all-start.2 = ((bf16[4,40,1152]{2,1,0:T(8,128)(2,1)}), bf16[4,40,1152]{2,1,0:T(8,128)(2,1)S(1)}, u32[]{:S(2)}, u32[]{:S(2)}) async-start(bf16[4,40,1152]{2,1,0:T(8,128)(2,1)} %body.1), calls=%async_computation.2 | async-start | bytes 737280 | tf_op jit(solution)/shard_map/while/body/all_to_all | solution.py:330
  131.5 6.1 %all-to-all-done.2 = bf16[4,40,1152]{2,1,0:T(8,128)(2,1)S(1)} async-done(((bf16[4,40,1152]{2,1,0:T(8,128)(2,1)}), bf16[4,40,1152]{2,1,0:T(8,128)(2,1)S(1)}, u32[]{:S(2)}, u32[]{:S(2)}) %all-to-all-start.2) | async-done | bytes 368672 | tf_op jit(solution)/shard_map/while/body/all_to_all | solution.py:330
  138.4 2.5 %shard_map.89 = (bf16[64,1280]{1,0:T(8,128)(2,1)S(1)}, bf16[64,1280]{1,0:T(8,128)(2,1)S(1)}, f32[4,8,160]{2,1,0:T(8,128)S(1)}) custom-call(bf16[4,40,1152]{2,1,0:T(8,128)(2,1)} %get-tuple-element.75.full_ref, bf16[64,3840]{1,0:T(8,128)(2,1)} %get-tuple-element.71.near_ref.cot_near_ref, bf16[64,1280]{1,0:T(8,128)(2,1)S(1)} %collective-permute-done.1.cot_far_ref, ...), custom_call_target="tpu_custom_call" | custom-call | tf_op jit(solution)/shard_map/pallas_call | solution.py:282
  140.9 1.9 collective-permute-start.2
  142.8 6.7 %all_to_all.56.inner_ref = f32[4,8,160]{2,1,0:T(8,128)S(1)} all-to-all(f32[4,8,160]{2,1,0:T(8,128)S(1)} %get-tuple-element.78), channel_id=1, replica_groups=mesh['dh'=2,'dl'=8,'ctx'=4,'zh'=2,'y'=4,'core'=2] {'ctx'}, dimensions={0} | all-to-all | bytes 40960 | tf_op jit(solution)/shard_map/all_to_all | solution.py:340
  149.5 1.0 shard_map.90
  150.4 35.3 %while.34 = (s32[]{:T(128)}, bf16[32,8,128]{2,1,0:T(8,128)(2,1)}, s32[]{:T(128)}, s32[]{:T(128)}) while((s32[]{:T(128)}, bf16[32,8,128]{2,1,0:T(8,128)(2,1)}, s32[]{:T(128)}, s32[]{:T(128)}) %tuple.56), condition=%wide.region_5.6_spmd, body=%wide.region_4.5_spmd.sunk | while | flops 2 | bytes 327765 | solution.py:295
  150.4 11.8 %all-to-all-start.3 = ((bf16[32,8,128]{2,1,0:T(8,128)(2,1)}), bf16[32,8,128]{2,1,0:T(8,128)(2,1)S(1)}, u32[]{:S(2)}, u32[]{:S(2)}) async-start(bf16[32,8,128]{2,1,0:T(8,128)(2,1)} %get-tuple-element.202), calls=%async_computation.3 | async-start | bytes 131072 | tf_op jit(solution)/shard_map/while/body/all_to_all | solution.py:343
  162.3 22.8 %all-to-all-done.3 = bf16[32,8,128]{2,1,0:T(8,128)(2,1)S(1)} async-done(((bf16[32,8,128]{2,1,0:T(8,128)(2,1)}), bf16[32,8,128]{2,1,0:T(8,128)(2,1)S(1)}, u32[]{:S(2)}, u32[]{:S(2)}) %all-to-all-start.3) | async-done | bytes 65568 | tf_op jit(solution)/shard_map/while/body/all_to_all | solution.py:343
  185.8 0.9 shard_map.91
  186.6 16.5 %all_to_all.57 = bf16[8,8,3072]{2,1,0:T(8,128)(2,1)S(1)} all-to-all(bf16[8,8,3072]{2,1,0:T(8,128)(2,1)S(1)} %bitcast.19), channel_id=1, replica_groups=mesh['dh'=2,'dl'=8,'ctx'=4,'zh'=2,'y'=4,'core'=2] {'y','core'}, dimensions={0} | all-to-all | bytes 786432 | tf_op jit(solution)/shard_map/all_to_all | solution.py:344
  203.2 1.6 shard_map.92
  (22 shorter events, 4.9 us)
Async XLA Ops:
  1.4 0.9 copy-start.3
  2.3 0.9 copy-start.4
  5.0 51.5 %collective-permute-start = (bf16[64,1280]{1,0:T(8,128)(2,1)S(1)}, bf16[64,1280]{1,0:T(8,128)(2,1)}, u32[]{:S(2)}, u32[]{:S(2)}) collective-permute-start(bf16[64,1280]{1,0:T(8,128)(2,1)S(1)} %get-tuple-element.72), channel_id=1, source_target_pairs={{0,520},{520,0},{8,512},{512,8},{1,521},{521,1},{9,513},{513,9},{2... | collective-permute-start | bytes 491528 | tf_op jit(solution)/shard_map/ppermute | solution.py:318
  30.6 14.6 %all-to-all-start = ((bf16[8,8,3840]{2,1,0:T(8,128)(2,1)}), bf16[8,8,3840]{2,1,0:T(8,128)(2,1)S(1)}, u32[]{:S(2)}, u32[]{:S(2)}) async-start(bf16[8,8,3840]{2,1,0:T(8,128)(2,1)} %bitcast.13), calls=%async_computation | async-start | bytes 983040 | tf_op jit(solution)/shard_map/while/body/all_to_all | solution.py:319
  45.9 60.6 %copy-start.1 = (bf16[1,1024,1024]{2,1,0:T(8,128)(2,1)S(1)}, bf16[1,1024,1024]{2,1,0:T(8,128)(2,1)}, u32[]{:S(2)}) copy-start(bf16[1,1024,1024]{2,1,0:T(8,128)(2,1)} %param.16) | copy-start | bytes 6291460
  57.6 80.7 %collective-permute-start.1 = (bf16[64,1280]{1,0:T(8,128)(2,1)S(1)}, bf16[64,1280]{1,0:T(8,128)(2,1)S(1)}, u32[]{:S(2)}, u32[]{:S(2)}) collective-permute-start(bf16[64,1280]{1,0:T(8,128)(2,1)S(1)} %shard_map.88), channel_id=1, source_target_pairs={{0,520},{520,0},{8,512},{512,8},{1,521},{521,1},{9,513},{513,9},{2... | collective-permute-start | bytes 491528 | tf_op jit(solution)/shard_map/ppermute | solution.py:320
  95.2 11.3 %all-to-all-start.4 = ((bf16[8,8,1280]{2,1,0:T(8,128)(2,1)}), bf16[8,8,1280]{2,1,0:T(8,128)(2,1)S(1)}, u32[]{:S(2)}, u32[]{:S(2)}) async-start(bf16[8,8,1280]{2,1,0:T(8,128)(2,1)} %bitcast.3), calls=%async_computation.4 | async-start | bytes 327680 | tf_op jit(solution)/shard_map/all_to_all | solution.py:321
  106.5 1.6 copy-start.2
  111.1 27.3 %copy-start = (bf16[1,1024,1024]{2,1,0:T(8,128)(2,1)S(1)}, bf16[1,1024,1024]{2,1,0:T(8,128)(2,1)}, u32[]{:S(2)}) copy-start(bf16[1,1024,1024]{2,1,0:T(8,128)(2,1)} %param.18) | copy-start | bytes 6291460
  126.3 0.9 copy-start.5
  128.1 9.5 %all-to-all-start.2 = ((bf16[4,40,1152]{2,1,0:T(8,128)(2,1)}), bf16[4,40,1152]{2,1,0:T(8,128)(2,1)S(1)}, u32[]{:S(2)}, u32[]{:S(2)}) async-start(bf16[4,40,1152]{2,1,0:T(8,128)(2,1)} %body.1), calls=%async_computation.2 | async-start | bytes 737280 | tf_op jit(solution)/shard_map/while/body/all_to_all | solution.py:330
  137.6 0.7 copy-start.6
  138.3 11.1 %copy-start.7 = (bf16[4,40,1152]{2,1,0:T(8,128)(2,1)S(1)}, bf16[4,40,1152]{2,1,0:T(8,128)(2,1)}, u32[]{:S(2)}) copy-start(bf16[4,40,1152]{2,1,0:T(8,128)(2,1)} %get-tuple-element.75.full_ref) | copy-start | bytes 1105924
  140.9 44.9 %collective-permute-start.2 = (bf16[64,1280]{1,0:T(8,128)(2,1)S(1)}, bf16[64,1280]{1,0:T(8,128)(2,1)S(1)}, u32[]{:S(2)}, u32[]{:S(2)}) collective-permute-start(bf16[64,1280]{1,0:T(8,128)(2,1)S(1)} %get-tuple-element.77), channel_id=1, source_target_pairs={{0,520},{520,0},{8,512},{512,8},{1,521},{521,1},{9,513},{513,9},{2... | collective-permute-start | bytes 491528 | tf_op jit(solution)/shard_map/ppermute | solution.py:339
  150.4 34.7 %all-to-all-start.3 = ((bf16[32,8,128]{2,1,0:T(8,128)(2,1)}), bf16[32,8,128]{2,1,0:T(8,128)(2,1)S(1)}, u32[]{:S(2)}, u32[]{:S(2)}) async-start(bf16[32,8,128]{2,1,0:T(8,128)(2,1)} %get-tuple-element.202), calls=%async_computation.3 | async-start | bytes 131072 | tf_op jit(solution)/shard_map/while/body/all_to_all | solution.py:343

commit v5 on v4

--- a/solution.py
+++ b/solution.py
@@ -82,7 +82,8 @@
     return whole, quarters
 
 
-def pack_kernel(zh_ref, route_ref, tok_ref, cot_ref, far_ref, near_ref, full_ref):
+def pack_kernel(zh_ref, route_ref, tok_ref, cot_ref, far_ref, near_ref, x_ref, full_ref):
+    x_ref[...] = jnp.zeros(x_ref.shape, BF16)
     full_ref[...] = jnp.zeros(full_ref.shape, BF16)
     far, place, position = where_to(zh_ref[0], route_ref[...])
     count, width = tok_ref.shape
@@ -117,7 +118,7 @@
     return [dot(whole, main[:, i * quarter : (i + 1) * quarter]) + dot(quarters[i], extra) for i in range(4)]
 
 
-def up_kernel(near_ref, far_ref, router_ref, gate_ref, up_ref, part_ref, x_ref):
+def up_kernel(turn_ref, near_ref, far_ref, router_ref, gate_ref, up_ref, part_ref, x_ref):
     width, hid = gate_ref.shape
     quarter = width // 4
     span = width + quarter
@@ -201,7 +202,7 @@
         ref[:, width:] = extra.astype(BF16)
 
 
-def relay_kernel(near_ref, x_far_ref, out_ref):
+def relay_kernel(near_ref, x_all_ref, out_ref):
     out_ref[...] = near_ref[:, near_ref.shape[1] - out_ref.shape[1] :]
 
 
@@ -292,7 +293,7 @@
 
 
 def as_one_step(turns, body, state):
-    out = lax.while_loop(lambda s: s[0] < turns, lambda s: (s[0] + 1, *body(*s[1:])), (jnp.int32(0), *state))
+    out = lax.while_loop(lambda s: s[0] < turns, lambda s: (s[0] + 1, *body(s[0], *s[1:])), (jnp.int32(0), *state))
     return out[1:]
 
 
@@ -310,26 +311,27 @@
     over_ctx = functools.partial(lax.all_to_all, axis_name="ctx", split_axis=0, concat_axis=0, tiled=True)
 
     chunk = shape((HALF * BACK, span), BF16)
-    x_far, near, full = call(
+    wide = shape((rows, width), BF16)
+    x_far, near, x, full = call(
         pack_kernel,
-        (chunk, shape((HALF * BACK, 3 * span), BF16), shape((N_CTX, rows // N_CTX, hid + 128), BF16)),
+        (chunk, shape((HALF * BACK, 3 * span), BF16), wide, shape((N_CTX, rows // N_CTX, hid + 128), BF16)),
         1,
     )(zh, routes, tokens, cotangent)
     x_far = lax.ppermute(x_far, PAIR, PAIR_PERM)
-    (near,) = as_one_step(turns, lambda v: (exchange(v),), (near,))
-    cot_far = lax.ppermute(call(relay_kernel, chunk)(near, x_far), PAIR, PAIR_PERM)
-    x_far = exchange(x_far)
+    (near,) = as_one_step(turns, lambda turn, v: (exchange(v),), (near,))
+    x_all = exchange(x_far)
+    cot_far = lax.ppermute(call(relay_kernel, chunk)(near, x_all), PAIR, PAIR_PERM)
 
     router_col = lax.dynamic_slice(router_weight, (lax.axis_index("ctx") * width, expert), (width, 1))
     router_col = jnp.concatenate([*pieces(router_col), jnp.zeros((width, 125), BF16)], axis=1)
     part = shape((N_CTX, rows // N_CTX, 2 * hid + 128), BF16)
-    sums, x = call(up_kernel, (part, shape((rows, width), BF16)))(near, x_far, router_col, gate_weight[0], up_weight[0])
-
-    def to_hidden(sums, full):
-        mine = over_ctx(sums)
-        return mine, over_ctx(call(hidden_kernel, shape(full.shape, BF16))(mine))
-
-    _, full = as_one_step(turns, to_hidden, (sums, full))
+
+    def to_hidden(turn, x, full):
+        weights = router_col, gate_weight[0], up_weight[0]
+        sums, x = call(up_kernel, (part, wide), 1)(turn.reshape(1), near, x_all, *weights)
+        return x, over_ctx(call(hidden_kernel, shape(full.shape, BF16))(over_ctx(sums)))
+
+    x, full = as_one_step(turns, to_hidden, (x, full))
 
     near_back, far, inner = call(
         down_kernel,
@@ -340,7 +342,7 @@
     inner = over_ctx(inner)
     grad = call(grad_kernel, shape((lax.axis_size(ALL_Z), 8, width // 8), BF16))(inner, full, x)
 
-    (grads,) = as_one_step(turns, lambda v: (lax.all_to_all(v, ALL_Z, 0, 0, tiled=True),), (grad,))
+    (grads,) = as_one_step(turns, lambda turn, v: (lax.all_to_all(v, ALL_Z, 0, 0, tiled=True),), (grad,))
     fin = exchange(call(merge_kernel, shape((HALF * BACK, 2 * span + 512), BF16))(near_back, far, grads))
     block_out, grad = call(out_kernel, (shape((count, width), BF16), shape((N_EXP, width), F32)), 1)(zh, routes, fin)
     return block_out, grad.T

time: 206 us -> 180 us (0.87)
  starting transfers between devices: 89.5 us -> 66.2 us
  local copies, waits for them, and re-layouts: 9.69 us -> 6.38 us
    ppermute x1, starting transfers between devices: 37.6 us -> 12.9 us  [shards(): lax.ppermute(call(relay_kernel, chunk)(near, x_all), PAIR, PAIR_PERM)]
    while x7 -> x4, local copies, waits for them, and re-layouts: 4.28 us -> 2.17 us
    unnamed x14 -> x11, local copies, waits for them, and re-layouts: 4.49 us -> 2.67 us
  transfers between devices with their start and end apart: 7 -> 7, of which waited for: 5 -> 5; matrix products, arithmetic and copies ran while one was open for 3% -> 2% of each run, Pallas kernels for 2% -> 3%
where the time goes in v5:
time: 180 us; the launch traced here: 179 us
  starting transfers between devices  66.2 us (37%)
  waiting for transfers between devices  53.8 us (30%)
  blocking collectives  37.1 us (21%)
  Pallas kernels  13.4 us (7%)
  local copies, waits for them, and re-layouts  6.38 us (4%)
    ppermute x1, starting transfers between devices, shards(): x_far = lax.ppermute(x_far, PAIR, PAIR_PERM)  23.5 us
    all_to_all x1, waiting for transfers between devices, shards(): lax.all_to_all(v, ALL_Z, 0, 0, tiled=True)  22.8 us
    all_to_all x1, blocking collectives, shards(): exchange(call(merge_kernel, shape((HALF * BACK, 2 * span + 512), BF16))(n...  17 us
    pallas_call x8, Pallas kernels, run(): pl.pallas_call(kernel, in_specs=specs, out_specs=jax.tree.map(lambda _: v...  13.4 us
    all_to_all x1, blocking collectives, to_hidden(): over_ctx(sums)  13.4 us
    ppermute x1, starting transfers between devices, shards(): lax.ppermute(call(relay_kernel, chunk)(near, x_all), PAIR, PAIR_PERM)  12.9 us
    all_to_all x1, starting transfers between devices, shards(): lax.all_to_all(v, ALL_Z, 0, 0, tiled=True)  12.9 us
    ppermute x1, waiting for transfers between devices, shards(): x_far = lax.ppermute(x_far, PAIR, PAIR_PERM)  12.6 us
  transfers between devices with their start and end apart: 7, of which 5 were waited for; matrix products, arithmetic and copies ran while one was open for 2% of the time, Pallas kernels for 3%

profile of v5, /device:TPU:1, one launch (start us, length us, event | category | flops | bytes accessed | tf_op | source)
XLA Modules:
  0.0 178.8 jit_solution(17131796032025545286)
XLA Ops:
  0.6 0.8 copy.16.route_ref
  1.4 0.9 copy-done.1
  2.4 0.9 copy-done.2
  3.3 1.8 %shard_map.86 = (bf16[64,1280]{1,0:T(8,128)(2,1)S(1)}, bf16[64,3840]{1,0:T(8,128)(2,1)}, bf16[160,1024]{1,0:T(8,128)(2,1)}, bf16[4,40,1152]{2,1,0:T(8,128)(2,1)}) custom-call(s32[1]{0:T(128)} %bitcast.5.zh_ref, s32[128,1]{1,0:T(8,128)S(1)} %copy.16.route_ref, bf16[128,1024]{1,0:T(8,128)(2,1)S(1)} %copy-done.1, bf16[128,1024]{1,0:T(8,128)(2,1)S(1)} %copy-done.2), custom_call_target="tpu_custom_call" | custom-call | tf_op jit(solution)/shard_map/pallas_call | solution.py:283
  5.1 23.5 %collective-permute-start = (bf16[64,1280]{1,0:T(8,128)(2,1)S(1)}, bf16[64,1280]{1,0:T(8,128)(2,1)}, u32[]{:S(2)}, u32[]{:S(2)}) collective-permute-start(bf16[64,1280]{1,0:T(8,128)(2,1)S(1)} %get-tuple-element.100), channel_id=1, source_target_pairs={{0,520},{520,0},{8,512},{512,8},{1,521},{521,1},{9,513},{513,9},{2... | collective-permute-start | bytes 491528 | tf_op jit(solution)/shard_map/ppermute | solution.py:320
  28.7 15.4 %while.32 = (s32[]{:T(128)}, bf16[64,3840]{1,0:T(8,128)(2,1)}, s32[]{:T(128)}, s32[]{:T(128)}) while((s32[]{:T(128)}, bf16[64,3840]{1,0:T(8,128)(2,1)}, s32[]{:T(128)}, s32[]{:T(128)}) %tuple.49), condition=%wide.region_1.2_spmd, body=%wide.region_0.1_spmd.sunk | while | flops 2 | bytes 2457685 | solution.py:296
  28.7 5.4 %all-to-all-start = ((bf16[8,8,3840]{2,1,0:T(8,128)(2,1)}), bf16[8,8,3840]{2,1,0:T(8,128)(2,1)S(1)}, u32[]{:S(2)}, u32[]{:S(2)}) async-start(bf16[8,8,3840]{2,1,0:T(8,128)(2,1)} %bitcast.17), calls=%async_computation | async-start | bytes 983040 | tf_op jit(solution)/shard_map/while/body/all_to_all | solution.py:321
  34.1 9.1 %all-to-all-done = bf16[8,8,3840]{2,1,0:T(8,128)(2,1)S(1)} async-done(((bf16[8,8,3840]{2,1,0:T(8,128)(2,1)}), bf16[8,8,3840]{2,1,0:T(8,128)(2,1)S(1)}, u32[]{:S(2)}, u32[]{:S(2)}) %all-to-all-start) | async-done | bytes 491552 | tf_op jit(solution)/shard_map/while/body/all_to_all | solution.py:321
  43.3 0.8 copy.22
  44.1 12.6 %collective-permute-done = bf16[64,1280]{1,0:T(8,128)(2,1)} collective-permute-done((bf16[64,1280]{1,0:T(8,128)(2,1)S(1)}, bf16[64,1280]{1,0:T(8,128)(2,1)}, u32[]{:S(2)}, u32[]{:S(2)}) %collective-permute-start) | collective-permute-done | bytes 163872 | tf_op jit(solution)/shard_map/ppermute | solution.py:320
  56.7 5.4 %all-to-all-start.4 = ((bf16[8,8,1280]{2,1,0:T(8,128)(2,1)}), bf16[8,8,1280]{2,1,0:T(8,128)(2,1)S(1)}, u32[]{:S(2)}, u32[]{:S(2)}) async-start(bf16[8,8,1280]{2,1,0:T(8,128)(2,1)} %bitcast.6), calls=%async_computation.4 | async-start | bytes 327680 | tf_op jit(solution)/shard_map/all_to_all | solution.py:322
  62.1 0.8 dynamic_slice.12
  62.9 0.8 fusion
  64.5 3.2 %all-to-all-done.4 = bf16[8,8,1280]{2,1,0:T(8,128)(2,1)S(1)} async-done(((bf16[8,8,1280]{2,1,0:T(8,128)(2,1)}), bf16[8,8,1280]{2,1,0:T(8,128)(2,1)S(1)}, u32[]{:S(2)}, u32[]{:S(2)}) %all-to-all-start.4) | async-done | bytes 163872 | tf_op jit(solution)/shard_map/all_to_all | solution.py:322
  67.7 1.0 shard_map.87
  68.7 12.9 %collective-permute-start.1 = (bf16[64,1280]{1,0:T(8,128)(2,1)S(1)}, bf16[64,1280]{1,0:T(8,128)(2,1)S(1)}, u32[]{:S(2)}, u32[]{:S(2)}) collective-permute-start(bf16[64,1280]{1,0:T(8,128)(2,1)S(1)} %shard_map.87), channel_id=1, source_target_pairs={{0,520},{520,0},{8,512},{512,8},{1,521},{521,1},{9,513},{513,9},{2... | collective-permute-start | bytes 491528 | tf_op jit(solution)/shard_map/ppermute | solution.py:323
  82.0 28.3 %while.33 = (s32[]{:T(128)}, bf16[160,1024]{1,0:T(8,128)(2,1)}, bf16[4,40,1152]{2,1,0:T(8,128)(2,1)}, s32[]{:T(128)}, bf16[1,1024,1024]{2,1,0:T(8,128)(2,1)}, /*...) while((s32[]{:T(128)}, bf16[160,1024]{1,0:T(8,128)(2,1)}, ...), condition=%wide.region_3.4_spmd, body=%wide.region_2.3_spmd.sunk | while | flops 2 | bytes 3973281 | solution.py:296
  82.0 3.6 %body.2 = (bf16[4,40,2176]{2,1,0:T(8,128)(2,1)S(1)}, bf16[160,1024]{1,0:T(8,128)(2,1)}) custom-call(s32[1]{0:T(128)} %bitcast.19.turn_ref, bf16[64,3840]{1,0:T(8,128)(2,1)} %get-tuple-element.275.near_ref, bf16[64,1280]{1,0:T(8,128)(2,1)S(1)} %get-tuple-element.276.far_ref, bf16[1024,128]{1,0:T(8,128)(2,1)S(1)} %get-tuple-element.277.router_ref, ...), custom_call_target="tpu_custom_call" | custom-call | tf_op jit(solution)/shard_map/while/body/pallas_call | solution.py:283
  85.6 13.4 %all_to_all.58.mine_ref = bf16[4,40,2176]{2,1,0:T(8,128)(2,1)S(1)} all-to-all(bf16[4,40,2176]{2,1,0:T(8,128)(2,1)S(1)} %get-tuple-element.233), channel_id=1, replica_groups=mesh['dh'=2,'dl'=8,'ctx'=4,'zh'=2,'y'=4,'core'=2] {'ctx'}, dimensions={0} | all-to-all | bytes 1392640 | tf_op jit(solution)/shard_map/while/body/all_to_all | solution.py:332
  99.0 0.9 body.3
  99.9 3.5 %all-to-all-start.2 = ((bf16[4,40,1152]{2,1,0:T(8,128)(2,1)}), bf16[4,40,1152]{2,1,0:T(8,128)(2,1)S(1)}, u32[]{:S(2)}, u32[]{:S(2)}) async-start(bf16[4,40,1152]{2,1,0:T(8,128)(2,1)} %body.3), calls=%async_computation.2 | async-start | bytes 737280 | tf_op jit(solution)/shard_map/while/body/all_to_all | solution.py:332
  103.4 6.1 %all-to-all-done.2 = bf16[4,40,1152]{2,1,0:T(8,128)(2,1)S(1)} async-done(((bf16[4,40,1152]{2,1,0:T(8,128)(2,1)}), bf16[4,40,1152]{2,1,0:T(8,128)(2,1)S(1)}, u32[]{:S(2)}, u32[]{:S(2)}) %all-to-all-start.2) | async-done | bytes 368672 | tf_op jit(solution)/shard_map/while/body/all_to_all | solution.py:332
  110.2 2.5 %shard_map.88 = (bf16[64,1280]{1,0:T(8,128)(2,1)S(1)}, bf16[64,1280]{1,0:T(8,128)(2,1)S(1)}, f32[4,8,160]{2,1,0:T(8,128)S(1)}) custom-call(bf16[4,40,1152]{2,1,0:T(8,128)(2,1)} %get-tuple-element.101.full_ref, bf16[64,3840]{1,0:T(8,128)(2,1)} %get-tuple-element.255.near_ref.cot_near_ref, bf16[64,1280]{1,0:T(8,128)(2,1)S(1)} %collective-permute-done.1.cot_far_ref, ...), custom_call_target="tpu_custom_call" | custom-call | tf_op jit(solution)/shard_map/pallas_call | solution.py:283
  112.8 2.5 %collective-permute-start.2 = (bf16[64,1280]{1,0:T(8,128)(2,1)S(1)}, bf16[64,1280]{1,0:T(8,128)(2,1)S(1)}, u32[]{:S(2)}, u32[]{:S(2)}) collective-permute-start(bf16[64,1280]{1,0:T(8,128)(2,1)S(1)} %get-tuple-element.103), channel_id=1, source_target_pairs={{0,520},{520,0},{8,512},{512,8},{1,521},{521,1},{9,513},{513,9},{2... | collective-permute-start | bytes 491528 | tf_op jit(solution)/shard_map/ppermute | solution.py:341
  115.3 6.7 %all_to_all.56.inner_ref = f32[4,8,160]{2,1,0:T(8,128)S(1)} all-to-all(f32[4,8,160]{2,1,0:T(8,128)S(1)} %get-tuple-element.104), channel_id=1, replica_groups=mesh['dh'=2,'dl'=8,'ctx'=4,'zh'=2,'y'=4,'core'=2] {'ctx'}, dimensions={0} | all-to-all | bytes 40960 | tf_op jit(solution)/shard_map/all_to_all | solution.py:342
  121.9 1.0 shard_map.89
  122.9 36.4 %while.34 = (s32[]{:T(128)}, bf16[32,8,128]{2,1,0:T(8,128)(2,1)}, s32[]{:T(128)}, s32[]{:T(128)}) while((s32[]{:T(128)}, bf16[32,8,128]{2,1,0:T(8,128)(2,1)}, s32[]{:T(128)}, s32[]{:T(128)}) %tuple.55), condition=%wide.region_5.6_spmd, body=%wide.region_4.5_spmd.sunk | while | flops 2 | bytes 327765 | solution.py:296
  122.9 12.9 %all-to-all-start.3 = ((bf16[32,8,128]{2,1,0:T(8,128)(2,1)}), bf16[32,8,128]{2,1,0:T(8,128)(2,1)S(1)}, u32[]{:S(2)}, u32[]{:S(2)}) async-start(bf16[32,8,128]{2,1,0:T(8,128)(2,1)} %get-tuple-element.284), calls=%async_computation.3 | async-start | bytes 131072 | tf_op jit(solution)/shard_map/while/body/all_to_all | solution.py:345
  135.9 22.8 %all-to-all-done.3 = bf16[32,8,128]{2,1,0:T(8,128)(2,1)S(1)} async-done(((bf16[32,8,128]{2,1,0:T(8,128)(2,1)}), bf16[32,8,128]{2,1,0:T(8,128)(2,1)S(1)}, u32[]{:S(2)}, u32[]{:S(2)}) %all-to-all-start.3) | async-done | bytes 65568 | tf_op jit(solution)/shard_map/while/body/all_to_all | solution.py:345
  159.3 0.9 shard_map.90
  160.2 17.0 %all_to_all.57 = bf16[8,8,3072]{2,1,0:T(8,128)(2,1)S(1)} all-to-all(bf16[8,8,3072]{2,1,0:T(8,128)(2,1)S(1)} %bitcast.24), channel_id=1, replica_groups=mesh['dh'=2,'dl'=8,'ctx'=4,'zh'=2,'y'=4,'core'=2] {'y','core'}, dimensions={0} | all-to-all | bytes 786432 | tf_op jit(solution)/shard_map/all_to_all | solution.py:346
  177.2 1.6 shard_map.91
  (19 shorter events, 2.4 us)
Async XLA Ops:
  1.4 0.9 copy-start.1
  2.3 0.9 copy-start.2
  5.1 51.5 %collective-permute-start = (bf16[64,1280]{1,0:T(8,128)(2,1)S(1)}, bf16[64,1280]{1,0:T(8,128)(2,1)}, u32[]{:S(2)}, u32[]{:S(2)}) collective-permute-start(bf16[64,1280]{1,0:T(8,128)(2,1)S(1)} %get-tuple-element.100), channel_id=1, source_target_pairs={{0,520},{520,0},{8,512},{512,8},{1,521},{521,1},{9,513},{513,9},{2... | collective-permute-start | bytes 491528 | tf_op jit(solution)/shard_map/ppermute | solution.py:320
  28.7 14.6 %all-to-all-start = ((bf16[8,8,3840]{2,1,0:T(8,128)(2,1)}), bf16[8,8,3840]{2,1,0:T(8,128)(2,1)S(1)}, u32[]{:S(2)}, u32[]{:S(2)}) async-start(bf16[8,8,3840]{2,1,0:T(8,128)(2,1)} %bitcast.17), calls=%async_computation | async-start | bytes 983040 | tf_op jit(solution)/shard_map/while/body/all_to_all | solution.py:321
  56.7 11.0 %all-to-all-start.4 = ((bf16[8,8,1280]{2,1,0:T(8,128)(2,1)}), bf16[8,8,1280]{2,1,0:T(8,128)(2,1)S(1)}, u32[]{:S(2)}, u32[]{:S(2)}) async-start(bf16[8,8,1280]{2,1,0:T(8,128)(2,1)} %bitcast.6), calls=%async_computation.4 | async-start | bytes 327680 | tf_op jit(solution)/shard_map/all_to_all | solution.py:322
  68.7 41.5 %collective-permute-start.1 = (bf16[64,1280]{1,0:T(8,128)(2,1)S(1)}, bf16[64,1280]{1,0:T(8,128)(2,1)S(1)}, u32[]{:S(2)}, u32[]{:S(2)}) collective-permute-start(bf16[64,1280]{1,0:T(8,128)(2,1)S(1)} %shard_map.87), channel_id=1, source_target_pairs={{0,520},{520,0},{8,512},{512,8},{1,521},{521,1},{9,513},{513,9},{2... | collective-permute-start | bytes 491528 | tf_op jit(solution)/shard_map/ppermute | solution.py:323
  81.9 28.3 %copy-start = (bf16[1,1024,1024]{2,1,0:T(8,128)(2,1)S(1)}, bf16[1,1024,1024]{2,1,0:T(8,128)(2,1)}, u32[]{:S(2)}) copy-start(bf16[1,1024,1024]{2,1,0:T(8,128)(2,1)} %param.18) | copy-start | bytes 6291460
  99.9 9.5 %all-to-all-start.2 = ((bf16[4,40,1152]{2,1,0:T(8,128)(2,1)}), bf16[4,40,1152]{2,1,0:T(8,128)(2,1)S(1)}, u32[]{:S(2)}, u32[]{:S(2)}) async-start(bf16[4,40,1152]{2,1,0:T(8,128)(2,1)} %body.3), calls=%async_computation.2 | async-start | bytes 737280 | tf_op jit(solution)/shard_map/while/body/all_to_all | solution.py:332
  109.5 0.7 copy-start.3
  110.2 11.7 %copy-start.4 = (bf16[4,40,1152]{2,1,0:T(8,128)(2,1)S(1)}, bf16[4,40,1152]{2,1,0:T(8,128)(2,1)}, u32[]{:S(2)}) copy-start(bf16[4,40,1152]{2,1,0:T(8,128)(2,1)} %get-tuple-element.101.full_ref) | copy-start | bytes 1105924
  110.2 11.7 %copy-start.5 = (bf16[160,1024]{1,0:T(8,128)(2,1)S(1)}, bf16[160,1024]{1,0:T(8,128)(2,1)}, u32[]{:S(2)}) copy-start(bf16[160,1024]{1,0:T(8,128)(2,1)} %get-tuple-element.105.x_ref) | copy-start | bytes 983044
  112.8 46.6 %collective-permute-start.2 = (bf16[64,1280]{1,0:T(8,128)(2,1)S(1)}, bf16[64,1280]{1,0:T(8,128)(2,1)S(1)}, u32[]{:S(2)}, u32[]{:S(2)}) collective-permute-start(bf16[64,1280]{1,0:T(8,128)(2,1)S(1)} %get-tuple-element.103), channel_id=1, source_target_pairs={{0,520},{520,0},{8,512},{512,8},{1,521},{521,1},{9,513},{513,9},{2... | collective-permute-start | bytes 491528 | tf_op jit(solution)/shard_map/ppermute | solution.py:341
  122.9 35.8 %all-to-all-start.3 = ((bf16[32,8,128]{2,1,0:T(8,128)(2,1)}), bf16[32,8,128]{2,1,0:T(8,128)(2,1)S(1)}, u32[]{:S(2)}, u32[]{:S(2)}) async-start(bf16[32,8,128]{2,1,0:T(8,128)(2,1)} %get-tuple-element.284), calls=%async_computation.3 | async-start | bytes 131072 | tf_op jit(solution)/shard_map/while/body/all_to_all | solution.py:345

commit v6 on v5

--- a/solution.py
+++ b/solution.py
@@ -82,8 +82,7 @@
     return whole, quarters
 
 
-def pack_kernel(zh_ref, route_ref, tok_ref, cot_ref, far_ref, near_ref, x_ref, full_ref):
-    x_ref[...] = jnp.zeros(x_ref.shape, BF16)
+def pack_kernel(zh_ref, route_ref, tok_ref, cot_ref, far_ref, near_ref, full_ref):
     full_ref[...] = jnp.zeros(full_ref.shape, BF16)
     far, place, position = where_to(zh_ref[0], route_ref[...])
     count, width = tok_ref.shape
@@ -118,7 +117,7 @@
     return [dot(whole, main[:, i * quarter : (i + 1) * quarter]) + dot(quarters[i], extra) for i in range(4)]
 
 
-def up_kernel(turn_ref, near_ref, far_ref, router_ref, gate_ref, up_ref, part_ref, x_ref):
+def up_kernel(near_ref, far_ref, router_ref, gate_ref, up_ref, part_ref, x_ref):
     width, hid = gate_ref.shape
     quarter = width // 4
     span = width + quarter
@@ -140,7 +139,7 @@
     put(dot(x, up_ref[...]), hid)
 
 
-def hidden_kernel(mine_ref, out_ref):
+def hidden_kernel(turn_ref, mine_ref, out_ref):
     hid = (mine_ref.shape[2] - 128) // 2
 
     def total(at, size):
@@ -165,28 +164,13 @@
     return dot(v, eye, ((0,), (0,)))
 
 
-def down_kernel(full_ref, cot_near_ref, cot_far_ref, down_ref, near_ref, far_ref, inner_ref, values_ref):
+def down_kernel(full_ref, down_ref, near_ref, far_ref, values_ref):
     hid, width = down_ref.shape
     quarter = width // 4
-    span = width + quarter
     full = jnp.concatenate([full_ref[i].astype(F32) for i in range(N_CTX)], axis=0)
-    rows = full.shape[0]
-    lane = iota((rows, 128), 1)
-    score = gathered(lane, 0, full[:, hid:])
+    score = gathered(iota((full.shape[0], 128), 1), 0, full[:, hid:])
     values_ref[...] = dot(full[:, :hid].astype(BF16), down_ref[...]).astype(BF16)
     n = HALF * CAP
-    maps = unpacking()
-    sums = []
-    for half, (ref, at) in enumerate(((cot_near_ref, span), (cot_far_ref, 0))):
-        inner = jnp.zeros((n, 1), F32)
-        for i, block in enumerate(unpack(maps, ref[:, at : at + width], ref[:, at + width : at + span])):
-            value = values_ref[half * n : (half + 1) * n, i * quarter : (i + 1) * quarter].astype(F32)
-            inner = inner + jnp.sum(block * value, axis=1, keepdims=True)
-        sums.append(inner)
-    turned = to_rows(spread(lane, 0, jnp.concatenate(sums, axis=0)).astype(BF16))
-    inner = turned[0:1] + turned[1:2] + turned[2:3]
-    for i in range(N_CTX):
-        inner_ref[i] = jnp.broadcast_to(inner, inner_ref.shape[1:])
     slot, r = iota((HALF * BACK, n), 0), iota((HALF * BACK, n), 1)
     src = tenth(r)
     p = r - src * CAP
@@ -202,7 +186,26 @@
         ref[:, width:] = extra.astype(BF16)
 
 
-def relay_kernel(near_ref, x_all_ref, out_ref):
+def inner_kernel(near_ref, far_ref, values_ref, inner_ref):
+    rows, width = values_ref.shape
+    quarter = width // 4
+    span = width + quarter
+    n = HALF * CAP
+    maps = unpacking()
+    sums = []
+    for half, (ref, at) in enumerate(((near_ref, span), (far_ref, 0))):
+        inner = jnp.zeros((n, 1), F32)
+        for i, block in enumerate(unpack(maps, ref[:, at : at + width], ref[:, at + width : at + span])):
+            value = values_ref[half * n : (half + 1) * n, i * quarter : (i + 1) * quarter].astype(F32)
+            inner = inner + jnp.sum(block * value, axis=1, keepdims=True)
+        sums.append(inner)
+    turned = to_rows(spread(iota((rows, 128), 1), 0, jnp.concatenate(sums, axis=0)).astype(BF16))
+    inner = turned[0:1] + turned[1:2] + turned[2:3]
+    for i in range(N_CTX):
+        inner_ref[i] = jnp.broadcast_to(inner, inner_ref.shape[1:])
+
+
+def relay_kernel(near_ref, sums_ref, out_ref):
     out_ref[...] = near_ref[:, near_ref.shape[1] - out_ref.shape[1] :]
 
 
@@ -312,34 +315,30 @@
 
     chunk = shape((HALF * BACK, span), BF16)
     wide = shape((rows, width), BF16)
-    x_far, near, x, full = call(
+    x_far, near, full = call(
         pack_kernel,
-        (chunk, shape((HALF * BACK, 3 * span), BF16), wide, shape((N_CTX, rows // N_CTX, hid + 128), BF16)),
+        (chunk, shape((HALF * BACK, 3 * span), BF16), shape((N_CTX, rows // N_CTX, hid + 128), BF16)),
         1,
     )(zh, routes, tokens, cotangent)
     x_far = lax.ppermute(x_far, PAIR, PAIR_PERM)
     (near,) = as_one_step(turns, lambda turn, v: (exchange(v),), (near,))
     x_all = exchange(x_far)
-    cot_far = lax.ppermute(call(relay_kernel, chunk)(near, x_all), PAIR, PAIR_PERM)
 
     router_col = lax.dynamic_slice(router_weight, (lax.axis_index("ctx") * width, expert), (width, 1))
     router_col = jnp.concatenate([*pieces(router_col), jnp.zeros((width, 125), BF16)], axis=1)
     part = shape((N_CTX, rows // N_CTX, 2 * hid + 128), BF16)
-
-    def to_hidden(turn, x, full):
-        weights = router_col, gate_weight[0], up_weight[0]
-        sums, x = call(up_kernel, (part, wide), 1)(turn.reshape(1), near, x_all, *weights)
-        return x, over_ctx(call(hidden_kernel, shape(full.shape, BF16))(over_ctx(sums)))
-
-    x, full = as_one_step(turns, to_hidden, (x, full))
-
-    near_back, far, inner = call(
-        down_kernel,
-        (chunk, chunk, shape((N_CTX, 8, rows), F32)),
-        scratch=[pltpu.VMEM((rows, width), BF16)],
-    )(full, near, cot_far, down_weight[0])
+    sums, x = call(up_kernel, (part, wide))(near, x_all, router_col, gate_weight[0], up_weight[0])
+    cot_far = lax.ppermute(call(relay_kernel, chunk)(near, sums), PAIR, PAIR_PERM)
+    mine = over_ctx(sums)
+
+    def to_hidden(turn, full):
+        return (over_ctx(call(hidden_kernel, shape(full.shape, BF16), 1)(turn.reshape(1), mine)),)
+
+    (full,) = as_one_step(turns, to_hidden, (full,))
+
+    near_back, far, values = call(down_kernel, (chunk, chunk, wide))(full, down_weight[0])
     far = lax.ppermute(far, PAIR, PAIR_PERM)
-    inner = over_ctx(inner)
+    inner = over_ctx(call(inner_kernel, shape((N_CTX, 8, rows), F32))(near, cot_far, values))
     grad = call(grad_kernel, shape((lax.axis_size(ALL_Z), 8, width // 8), BF16))(inner, full, x)
 
     (grads,) = as_one_step(turns, lambda turn, v: (lax.all_to_all(v, ALL_Z, 0, 0, tiled=True),), (grad,))

time: 180 us -> 197 us (1.094)
  blocking collectives: 37.1 us -> 22.2 us
  waiting for transfers between devices: 53.8 us -> 68.1 us
  starting transfers between devices: 66.2 us -> 80.2 us
    ppermute x1, waiting for transfers between devices: 0.01 us -> 15.3 us  [shards(): lax.ppermute(call(relay_kernel, chunk)(near, sums), PAIR, PAIR_PERM)]
    all_to_all x2 -> x1, blocking collectives: 20.1 us -> 8.28 us  [shards(): over_ctx(call(inner_kernel, shape((N_CTX, 8, rows), F32))(near, cot_far,...]
    ppermute x1, starting transfers between devices: 2.5 us -> 8.13 us  [shards(): far = lax.ppermute(far, PAIR, PAIR_PERM)]
    all_to_all x1 -> x2, starting transfers between devices: 3.46 us -> 8.35 us  [the longest x1 4.18 us: to_hidden(): over_ctx(call(hidden_kernel, shape(full.shape, BF16), 1)(turn.reshape(1),...]
    all_to_all x1, starting transfers between devices: 12.9 us -> 16.3 us  [shards(): lax.all_to_all(v, ALL_Z, 0, 0, tiled=True)]
    all_to_all x1, blocking collectives: 17 us -> 13.9 us  [shards(): exchange(call(merge_kernel, shape((HALF * BACK, 2 * span + 512), BF16))(n...]
    ppermute x1, waiting for transfers between devices: 12.6 us -> 10.4 us  [shards(): x_far = lax.ppermute(x_far, PAIR, PAIR_PERM)]
    unnamed x11 -> x14, local copies, waits for them, and re-layouts: 2.67 us -> 4.49 us
  transfers between devices with their start and end apart: 7 -> 8, of which waited for: 5 -> 6; matrix products, arithmetic and copies ran while one was open for 2% -> 2% of each run, Pallas kernels for 3% -> 4%
where the time goes in v6:
time: 197 us; the launch traced here: 196 us
  starting transfers between devices  80.2 us (41%)
  waiting for transfers between devices  68.1 us (35%)
  blocking collectives  22.2 us (11%)
  Pallas kernels  15.2 us (8%)
  local copies, waits for them, and re-layouts  7.58 us (4%)
  other arithmetic  2.19 us (1%)
    ppermute x1, starting transfers between devices, shards(): x_far = lax.ppermute(x_far, PAIR, PAIR_PERM)  23.5 us
    all_to_all x1, waiting for transfers between devices, shards(): lax.all_to_all(v, ALL_Z, 0, 0, tiled=True)  22.9 us
    all_to_all x1, starting transfers between devices, shards(): lax.all_to_all(v, ALL_Z, 0, 0, tiled=True)  16.3 us
    ppermute x1, waiting for transfers between devices, shards(): lax.ppermute(call(relay_kernel, chunk)(near, sums), PAIR, PAIR_PERM)  15.3 us
    pallas_call x9, Pallas kernels, run(): pl.pallas_call(kernel, in_specs=specs, out_specs=jax.tree.map(lambda _: v...  15.2 us
    all_to_all x1, blocking collectives, shards(): exchange(call(merge_kernel, shape((HALF * BACK, 2 * span + 512), BF16))(n...  13.9 us
    ppermute x1, starting transfers between devices, shards(): lax.ppermute(call(relay_kernel, chunk)(near, sums), PAIR, PAIR_PERM)  12.9 us
    ppermute x1, waiting for transfers between devices, shards(): x_far = lax.ppermute(x_far, PAIR, PAIR_PERM)  10.4 us
  transfers between devices with their start and end apart: 8, of which 6 were waited for; matrix products, arithmetic and copies ran while one was open for 2% of the time, Pallas kernels for 4%

profile of v6, /device:TPU:1, one launch (start us, length us, event | category | flops | bytes accessed | tf_op | source)
XLA Modules:
  0.0 196.2 jit_solution(910928595783655849)
XLA Ops:
  1.4 0.9 copy-done.3
  2.4 0.9 copy-done.4
  3.3 1.7 shard_map.86
  5.0 23.5 %collective-permute-start = (bf16[64,1280]{1,0:T(8,128)(2,1)S(1)}, bf16[64,1280]{1,0:T(8,128)(2,1)}, u32[]{:S(2)}, u32[]{:S(2)}) collective-permute-start(bf16[64,1280]{1,0:T(8,128)(2,1)S(1)} %get-tuple-element.73), channel_id=1, source_target_pairs={{0,520},{520,0},{8,512},{512,8},{1,521},{521,1},{9,513},{513,9},{2... | collective-permute-start | bytes 491528 | tf_op jit(solution)/shard_map/ppermute | solution.py:323
  29.7 0.9 fusion.1
  30.6 15.5 %while.30 = (s32[]{:T(128)}, bf16[64,3840]{1,0:T(8,128)(2,1)}, s32[]{:T(128)}, s32[]{:T(128)}) while((s32[]{:T(128)}, bf16[64,3840]{1,0:T(8,128)(2,1)}, s32[]{:T(128)}, s32[]{:T(128)}) %tuple.50), condition=%wide.region_1.2_spmd, body=%wide.region_0.1_spmd.sunk | while | flops 2 | bytes 2457685 | solution.py:299
  30.6 5.6 %all-to-all-start = ((bf16[8,8,3840]{2,1,0:T(8,128)(2,1)}), bf16[8,8,3840]{2,1,0:T(8,128)(2,1)S(1)}, u32[]{:S(2)}, u32[]{:S(2)}) async-start(bf16[8,8,3840]{2,1,0:T(8,128)(2,1)} %bitcast.15), calls=%async_computation | async-start | bytes 983040 | tf_op jit(solution)/shard_map/while/body/all_to_all | solution.py:324
  36.2 9.1 %all-to-all-done = bf16[8,8,3840]{2,1,0:T(8,128)(2,1)S(1)} async-done(((bf16[8,8,3840]{2,1,0:T(8,128)(2,1)}), bf16[8,8,3840]{2,1,0:T(8,128)(2,1)S(1)}, u32[]{:S(2)}, u32[]{:S(2)}) %all-to-all-start) | async-done | bytes 491552 | tf_op jit(solution)/shard_map/while/body/all_to_all | solution.py:324
  46.1 10.4 %collective-permute-done = bf16[64,1280]{1,0:T(8,128)(2,1)} collective-permute-done((bf16[64,1280]{1,0:T(8,128)(2,1)S(1)}, bf16[64,1280]{1,0:T(8,128)(2,1)}, u32[]{:S(2)}, u32[]{:S(2)}) %collective-permute-start) | collective-permute-done | bytes 163872 | tf_op jit(solution)/shard_map/ppermute | solution.py:323
  56.5 5.4 %all-to-all-start.3 = ((bf16[8,8,1280]{2,1,0:T(8,128)(2,1)}), bf16[8,8,1280]{2,1,0:T(8,128)(2,1)S(1)}, u32[]{:S(2)}, u32[]{:S(2)}) async-start(bf16[8,8,1280]{2,1,0:T(8,128)(2,1)} %bitcast.4), calls=%async_computation.3 | async-start | bytes 327680 | tf_op jit(solution)/shard_map/all_to_all | solution.py:325
  62.0 1.3 maximum_maximum_fusion.router_ref
  63.3 4.3 %all-to-all-done.3 = bf16[8,8,1280]{2,1,0:T(8,128)(2,1)S(1)} async-done(((bf16[8,8,1280]{2,1,0:T(8,128)(2,1)}), bf16[8,8,1280]{2,1,0:T(8,128)(2,1)S(1)}, u32[]{:S(2)}, u32[]{:S(2)}) %all-to-all-start.3) | async-done | bytes 163872 | tf_op jit(solution)/shard_map/all_to_all | solution.py:325
  67.6 1.6 copy-done.2
  69.1 3.1 %shard_map.87 = (bf16[4,40,2176]{2,1,0:T(8,128)(2,1)}, bf16[160,1024]{1,0:T(8,128)(2,1)S(1)}) custom-call(bf16[64,3840]{1,0:T(8,128)(2,1)} %get-tuple-element.72.near_ref, bf16[64,1280]{1,0:T(8,128)(2,1)S(1)} %bitcast.23, bf16[1024,128]{1,0:T(8,128)(2,1)S(1)} %maximum_maximum_fusion.router_ref, bf16[1024,1024]{1,0:T(8,128)(2,1)S(1)} %bitcast.19, ...), custom_call_target="tpu_custom_call" | custom-call | tf_op jit(solution)/shard_map/pallas_call | solution.py:286
  72.2 4.2 %all-to-all-start.4 = ((bf16[4,40,2176]{2,1,0:T(8,128)(2,1)}), bf16[4,40,2176]{2,1,0:T(8,128)(2,1)}, u32[]{:S(2)}, u32[]{:S(2)}) async-start(bf16[4,40,2176]{2,1,0:T(8,128)(2,1)} %get-tuple-element.74.sums_ref), calls=%async_computation.4 | async-start | bytes 1392640 | tf_op jit(solution)/shard_map/all_to_all | solution.py:332
  76.4 1.4 shard_map.89
  77.8 12.9 %collective-permute-start.2 = (bf16[64,1280]{1,0:T(8,128)(2,1)S(1)}, bf16[64,1280]{1,0:T(8,128)(2,1)S(1)}, u32[]{:S(2)}, u32[]{:S(2)}) collective-permute-start(bf16[64,1280]{1,0:T(8,128)(2,1)S(1)} %shard_map.89), channel_id=1, source_target_pairs={{0,520},{520,0},{8,512},{512,8},{1,521},{521,1},{9,513},{513,9},{2... | collective-permute-start | bytes 491528 | tf_op jit(solution)/shard_map/ppermute | solution.py:331
  90.8 13.1 %while.31 = (s32[]{:T(128)}, bf16[4,40,1152]{2,1,0:T(8,128)(2,1)}, s32[]{:T(128)}, bf16[4,40,2176]{2,1,0:T(8,128)(2,1)}, s32[]{:T(128)}) while((s32[]{:T(128)}, bf16[4,40,1152]{2,1,0:T(8,128)(2,1)}, s32[]{:T(128)}, bf16[4,40,2176]{2,1,0:T(8,128)(2,1)}, s32[]{:T(128)}) %tuple.53), condition=%wide.region_3.4_spmd, body=%wide.region_2.3_spmd.sunk | while | flops 2 | bytes 2580601 | solution.py:299
  90.8 2.0 %body.1 = bf16[4,40,1152]{2,1,0:T(8,128)(2,1)} custom-call(s32[1]{0:T(128)} %bitcast.17.turn_ref, bf16[4,40,2176]{2,1,0:T(8,128)(2,1)} %get-tuple-element.195.mine_ref), custom_call_target="tpu_custom_call" | custom-call | tf_op jit(solution)/shard_map/while/body/pallas_call | solution.py:286
  92.8 4.2 %all-to-all-start.1 = ((bf16[4,40,1152]{2,1,0:T(8,128)(2,1)}), bf16[4,40,1152]{2,1,0:T(8,128)(2,1)S(1)}, u32[]{:S(2)}, u32[]{:S(2)}) async-start(bf16[4,40,1152]{2,1,0:T(8,128)(2,1)} %body.1), calls=%async_computation.1 | async-start | bytes 737280 | tf_op jit(solution)/shard_map/while/body/all_to_all | solution.py:335
  97.0 6.1 %all-to-all-done.1 = bf16[4,40,1152]{2,1,0:T(8,128)(2,1)S(1)} async-done(((bf16[4,40,1152]{2,1,0:T(8,128)(2,1)}), bf16[4,40,1152]{2,1,0:T(8,128)(2,1)S(1)}, u32[]{:S(2)}, u32[]{:S(2)}) %all-to-all-start.1) | async-done | bytes 368672 | tf_op jit(solution)/shard_map/while/body/all_to_all | solution.py:335
  103.8 1.8 shard_map.88
  105.7 8.1 %collective-permute-start.1 = (bf16[64,1280]{1,0:T(8,128)(2,1)S(1)}, bf16[64,1280]{1,0:T(8,128)(2,1)S(1)}, u32[]{:S(2)}, u32[]{:S(2)}) collective-permute-start(bf16[64,1280]{1,0:T(8,128)(2,1)S(1)} %get-tuple-element.77), channel_id=1, source_target_pairs={{0,520},{520,0},{8,512},{512,8},{1,521},{521,1},{9,513},{513,9},{2... | collective-permute-start | bytes 491528 | tf_op jit(solution)/shard_map/ppermute | solution.py:340
  113.8 15.3 %collective-permute-done.2.far_ref = bf16[64,1280]{1,0:T(8,128)(2,1)S(1)} collective-permute-done((bf16[64,1280]{1,0:T(8,128)(2,1)S(1)}, bf16[64,1280]{1,0:T(8,128)(2,1)S(1)}, u32[]{:S(2)}, u32[]{:S(2)}) %collective-permute-start.2) | collective-permute-done | bytes 163872 | tf_op jit(solution)/shard_map/ppermute | solution.py:331
  129.1 1.7 shard_map.90
  130.8 8.3 %all_to_all.55.inner_ref = f32[4,8,160]{2,1,0:T(8,128)S(1)} all-to-all(f32[4,8,160]{2,1,0:T(8,128)S(1)} %shard_map.90), channel_id=1, replica_groups=mesh['dh'=2,'dl'=8,'ctx'=4,'zh'=2,'y'=4,'core'=2] {'ctx'}, dimensions={0} | all-to-all | bytes 40960 | tf_op jit(solution)/shard_map/all_to_all | solution.py:341
  139.1 1.0 shard_map.91
  140.1 39.8 %while.32 = (s32[]{:T(128)}, bf16[32,8,128]{2,1,0:T(8,128)(2,1)}, s32[]{:T(128)}, s32[]{:T(128)}) while((s32[]{:T(128)}, bf16[32,8,128]{2,1,0:T(8,128)(2,1)}, s32[]{:T(128)}, s32[]{:T(128)}) %tuple.56), condition=%wide.region_5.6_spmd, body=%wide.region_4.5_spmd.sunk | while | flops 2 | bytes 327765 | solution.py:299
  140.1 16.3 %all-to-all-start.2 = ((bf16[32,8,128]{2,1,0:T(8,128)(2,1)}), bf16[32,8,128]{2,1,0:T(8,128)(2,1)S(1)}, u32[]{:S(2)}, u32[]{:S(2)}) async-start(bf16[32,8,128]{2,1,0:T(8,128)(2,1)} %get-tuple-element.202), calls=%async_computation.2 | async-start | bytes 131072 | tf_op jit(solution)/shard_map/while/body/all_to_all | solution.py:344
  156.4 22.9 %all-to-all-done.2 = bf16[32,8,128]{2,1,0:T(8,128)(2,1)S(1)} async-done(((bf16[32,8,128]{2,1,0:T(8,128)(2,1)}), bf16[32,8,128]{2,1,0:T(8,128)(2,1)S(1)}, u32[]{:S(2)}, u32[]{:S(2)}) %all-to-all-start.2) | async-done | bytes 65568 | tf_op jit(solution)/shard_map/while/body/all_to_all | solution.py:344
  180.8 13.9 %all_to_all.56 = bf16[8,8,3072]{2,1,0:T(8,128)(2,1)S(1)} all-to-all(bf16[8,8,3072]{2,1,0:T(8,128)(2,1)S(1)} %bitcast.22), channel_id=1, replica_groups=mesh['dh'=2,'dl'=8,'ctx'=4,'zh'=2,'y'=4,'core'=2] {'y','core'}, dimensions={0} | all-to-all | bytes 786432 | tf_op jit(solution)/shard_map/all_to_all | solution.py:345
  194.7 1.6 shard_map.93
  (21 shorter events, 5.0 us)
Async XLA Ops:
  1.4 0.9 copy-start.3
  2.3 0.9 copy-start.4
  5.0 51.6 %collective-permute-start = (bf16[64,1280]{1,0:T(8,128)(2,1)S(1)}, bf16[64,1280]{1,0:T(8,128)(2,1)}, u32[]{:S(2)}, u32[]{:S(2)}) collective-permute-start(bf16[64,1280]{1,0:T(8,128)(2,1)S(1)} %get-tuple-element.73), channel_id=1, source_target_pairs={{0,520},{520,0},{8,512},{512,8},{1,521},{521,1},{9,513},{513,9},{2... | collective-permute-start | bytes 491528 | tf_op jit(solution)/shard_map/ppermute | solution.py:323
  30.6 36.9 %copy-start.1 = (bf16[1,1024,1024]{2,1,0:T(8,128)(2,1)S(1)}, bf16[1,1024,1024]{2,1,0:T(8,128)(2,1)}, u32[]{:S(2)}) copy-start(bf16[1,1024,1024]{2,1,0:T(8,128)(2,1)} %param.16) | copy-start | bytes 6291460
  30.6 14.7 %all-to-all-start = ((bf16[8,8,3840]{2,1,0:T(8,128)(2,1)}), bf16[8,8,3840]{2,1,0:T(8,128)(2,1)S(1)}, u32[]{:S(2)}, u32[]{:S(2)}) async-start(bf16[8,8,3840]{2,1,0:T(8,128)(2,1)} %bitcast.15), calls=%async_computation | async-start | bytes 983040 | tf_op jit(solution)/shard_map/while/body/all_to_all | solution.py:324
  56.5 11.0 %all-to-all-start.3 = ((bf16[8,8,1280]{2,1,0:T(8,128)(2,1)}), bf16[8,8,1280]{2,1,0:T(8,128)(2,1)S(1)}, u32[]{:S(2)}, u32[]{:S(2)}) async-start(bf16[8,8,1280]{2,1,0:T(8,128)(2,1)} %bitcast.4), calls=%async_computation.3 | async-start | bytes 327680 | tf_op jit(solution)/shard_map/all_to_all | solution.py:325
  67.6 1.6 copy-start.2
  72.2 18.5 %all-to-all-start.4 = ((bf16[4,40,2176]{2,1,0:T(8,128)(2,1)}), bf16[4,40,2176]{2,1,0:T(8,128)(2,1)}, u32[]{:S(2)}, u32[]{:S(2)}) async-start(bf16[4,40,2176]{2,1,0:T(8,128)(2,1)} %get-tuple-element.74.sums_ref), calls=%async_computation.4 | async-start | bytes 1392640 | tf_op jit(solution)/shard_map/all_to_all | solution.py:332
  76.4 27.4 %copy-start = (bf16[1,1024,1024]{2,1,0:T(8,128)(2,1)S(1)}, bf16[1,1024,1024]{2,1,0:T(8,128)(2,1)}, u32[]{:S(2)}) copy-start(bf16[1,1024,1024]{2,1,0:T(8,128)(2,1)} %param.18) | copy-start | bytes 6291460
  77.8 51.3 %collective-permute-start.2 = (bf16[64,1280]{1,0:T(8,128)(2,1)S(1)}, bf16[64,1280]{1,0:T(8,128)(2,1)S(1)}, u32[]{:S(2)}, u32[]{:S(2)}) collective-permute-start(bf16[64,1280]{1,0:T(8,128)(2,1)S(1)} %shard_map.89), channel_id=1, source_target_pairs={{0,520},{520,0},{8,512},{512,8},{1,521},{521,1},{9,513},{513,9},{2... | collective-permute-start | bytes 491528 | tf_op jit(solution)/shard_map/ppermute | solution.py:331
  92.8 10.3 %all-to-all-start.1 = ((bf16[4,40,1152]{2,1,0:T(8,128)(2,1)}), bf16[4,40,1152]{2,1,0:T(8,128)(2,1)S(1)}, u32[]{:S(2)}, u32[]{:S(2)}) async-start(bf16[4,40,1152]{2,1,0:T(8,128)(2,1)} %body.1), calls=%async_computation.1 | async-start | bytes 737280 | tf_op jit(solution)/shard_map/while/body/all_to_all | solution.py:335
  103.1 0.7 copy-start.5
  103.8 35.3 %copy-start.6 = (bf16[4,40,1152]{2,1,0:T(8,128)(2,1)S(1)}, bf16[4,40,1152]{2,1,0:T(8,128)(2,1)}, u32[]{:S(2)}) copy-start(bf16[4,40,1152]{2,1,0:T(8,128)(2,1)} %get-tuple-element.75.full_ref) | copy-start | bytes 1105924
  105.7 74.2 %collective-permute-start.1 = (bf16[64,1280]{1,0:T(8,128)(2,1)S(1)}, bf16[64,1280]{1,0:T(8,128)(2,1)S(1)}, u32[]{:S(2)}, u32[]{:S(2)}) collective-permute-start(bf16[64,1280]{1,0:T(8,128)(2,1)S(1)} %get-tuple-element.77), channel_id=1, source_target_pairs={{0,520},{520,0},{8,512},{512,8},{1,521},{521,1},{9,513},{513,9},{2... | collective-permute-start | bytes 491528 | tf_op jit(solution)/shard_map/ppermute | solution.py:340
  140.1 39.1 %all-to-all-start.2 = ((bf16[32,8,128]{2,1,0:T(8,128)(2,1)}), bf16[32,8,128]{2,1,0:T(8,128)(2,1)S(1)}, u32[]{:S(2)}, u32[]{:S(2)}) async-start(bf16[32,8,128]{2,1,0:T(8,128)(2,1)} %get-tuple-element.202), calls=%async_computation.2 | async-start | bytes 131072 | tf_op jit(solution)/shard_map/while/body/all_to_all | solution.py:344

commit v7 on v5

--- a/solution.py
+++ b/solution.py
@@ -62,8 +62,10 @@
     return out
 
 
-def where_to(zh, route):
-    count = route.shape[0]
+def where_to(zh, routes):
+    count = routes.shape[1]
+    own = iota((count, count), 0) == iota((count, count), 1)
+    route = jnp.sum(jnp.where(own, routes, 0).astype(F32), axis=1, keepdims=True).astype(I32)
     ids = iota((count, 128), 1)
     onehot = (route == ids).astype(F32)
     before = pick(iota((count, count), 1) < iota((count, count), 0))
@@ -82,10 +84,10 @@
     return whole, quarters
 
 
-def pack_kernel(zh_ref, route_ref, tok_ref, cot_ref, far_ref, near_ref, x_ref, full_ref):
+def pack_kernel(zh_ref, routes_ref, tok_ref, cot_ref, far_ref, near_ref, x_ref, full_ref):
     x_ref[...] = jnp.zeros(x_ref.shape, BF16)
     full_ref[...] = jnp.zeros(full_ref.shape, BF16)
-    far, place, position = where_to(zh_ref[0], route_ref[...])
+    far, place, position = where_to(zh_ref[0], routes_ref[...])
     count, width = tok_ref.shape
     quarter = width // 4
     span = width + quarter
@@ -118,7 +120,10 @@
     return [dot(whole, main[:, i * quarter : (i + 1) * quarter]) + dot(quarters[i], extra) for i in range(4)]
 
 
-def up_kernel(turn_ref, near_ref, far_ref, router_ref, gate_ref, up_ref, part_ref, x_ref):
+def up_kernel(turn_ref, near_ref, far_ref, router_ref, gate_in, up_in, part_ref, x_ref, gate_ref, up_ref, sems):
+    moves = [pltpu.make_async_copy(gate_in.at[0], gate_ref, sems.at[0]), pltpu.make_async_copy(up_in.at[0], up_ref, sems.at[1])]
+    for move in moves:
+        move.start()
     width, hid = gate_ref.shape
     quarter = width // 4
     span = width + quarter
@@ -136,7 +141,9 @@
 
     logit = jnp.sum(dot(x, router_ref[...]), axis=1, keepdims=True)
     put(spread(iota((2 * n, 128), 1), 0, logit), 2 * hid)
+    moves[0].wait()
     put(dot(x, gate_ref[...]), 0)
+    moves[1].wait()
     put(dot(x, up_ref[...]), hid)
 
 
@@ -202,8 +209,12 @@
         ref[:, width:] = extra.astype(BF16)
 
 
-def relay_kernel(near_ref, x_all_ref, out_ref):
+def slice_kernel(near_ref, out_ref):
     out_ref[...] = near_ref[:, near_ref.shape[1] - out_ref.shape[1] :]
+
+
+def gate_kernel(v_ref, other_ref, out_ref):
+    pass
 
 
 def grad_kernel(inner_ref, full_ref, x_ref, out_ref):
@@ -243,8 +254,8 @@
             out_ref[:, at : at + 128] = jnp.concatenate([v.astype(F32)] * HALF, axis=0).astype(BF16)
 
 
-def out_kernel(zh_ref, route_ref, fin_ref, out_ref, grad_ref):
-    far, place, position = where_to(zh_ref[0], route_ref[...])
+def out_kernel(zh_ref, routes_ref, fin_ref, out_ref, grad_ref):
+    far, place, position = where_to(zh_ref[0], routes_ref[...])
     count, width = out_ref.shape
     quarter = width // 4
     span = width + quarter
@@ -275,17 +286,19 @@
         grad_ref[:, j * 128 : (j + 1) * 128] = total
 
 
-def call(kernel, out, scalars=0, scratch=()):
+def call(kernel, out, scalars=0, scratch=(), far_in=(), aliases={}):
     def run(*args):
         smem = pl.BlockSpec(memory_space=pltpu.SMEM)
         vmem = pl.BlockSpec(memory_space=pltpu.VMEM)
-        specs = [smem if i < scalars else vmem for i in range(len(args))]
+        anywhere = pl.BlockSpec(memory_space=pl.ANY)
+        specs = [smem if i < scalars else anywhere if i in far_in else vmem for i in range(len(args))]
         return pl.pallas_call(
             kernel,
             in_specs=specs,
             out_specs=jax.tree.map(lambda _: vmem, out),
             out_shape=out,
             scratch_shapes=scratch,
+            input_output_aliases=aliases,
             compiler_params=pltpu.CompilerParams(vmem_limit_bytes=16 * 1024 * 1024),
         )(*args)
 
@@ -299,6 +312,7 @@
 
 def shards(tokens, routes, router_weight, gate_weight, up_weight, down_weight, cotangent):
     count, width = tokens.shape
+    routes = routes.reshape(1, count)
     hid = gate_weight.shape[2]
     shape = jax.ShapeDtypeStruct
     zh = lax.axis_index("zh").astype(I32)
@@ -320,15 +334,18 @@
     x_far = lax.ppermute(x_far, PAIR, PAIR_PERM)
     (near,) = as_one_step(turns, lambda turn, v: (exchange(v),), (near,))
     x_all = exchange(x_far)
-    cot_far = lax.ppermute(call(relay_kernel, chunk)(near, x_all), PAIR, PAIR_PERM)
+    cot_far = call(gate_kernel, chunk, aliases={0: 0})(call(slice_kernel, chunk)(near), x_all)
+    cot_far = lax.ppermute(cot_far, PAIR, PAIR_PERM)
 
     router_col = lax.dynamic_slice(router_weight, (lax.axis_index("ctx") * width, expert), (width, 1))
     router_col = jnp.concatenate([*pieces(router_col), jnp.zeros((width, 125), BF16)], axis=1)
     part = shape((N_CTX, rows // N_CTX, 2 * hid + 128), BF16)
 
+    loads = [pltpu.VMEM((width, hid), BF16), pltpu.VMEM((width, hid), BF16), pltpu.SemaphoreType.DMA((2,))]
+
     def to_hidden(turn, x, full):
-        weights = router_col, gate_weight[0], up_weight[0]
-        sums, x = call(up_kernel, (part, wide), 1)(turn.reshape(1), near, x_all, *weights)
+        weights = router_col, gate_weight, up_weight
+        sums, x = call(up_kernel, (part, wide), 1, loads, (4, 5))(turn.reshape(1), near, x_all, *weights)
         return x, over_ctx(call(hidden_kernel, shape(full.shape, BF16))(over_ctx(sums)))
 
     x, full = as_one_step(turns, to_hidden, (x, full))

time: 180 us -> 179 us (level)
    pallas_call x8 -> x9, Pallas kernels: 13.4 us -> 14 us  [run(): pl.pallas_call(kernel, in_specs=specs, out_specs=jax.tree.map(lambda _: v...]
  transfers between devices with their start and end apart: 7 -> 7, of which waited for: 5 -> 5; matrix products, arithmetic and copies ran while one was open for 2% -> 2% of each run, Pallas kernels for 3% -> 4%
where the time goes in v7:
time: 179 us; the launch traced here: 178 us
  starting transfers between devices  66.2 us (37%)
  waiting for transfers between devices  52.8 us (29%)
  blocking collectives  37.1 us (21%)
  Pallas kernels  14 us (8%)
  local copies, waits for them, and re-layouts  6.29 us (4%)
    ppermute x1, starting transfers between devices, shards(): x_far = lax.ppermute(x_far, PAIR, PAIR_PERM)  23.5 us
    all_to_all x1, waiting for transfers between devices, shards(): lax.all_to_all(v, ALL_Z, 0, 0, tiled=True)  22.8 us
    all_to_all x1, blocking collectives, shards(): exchange(call(merge_kernel, shape((HALF * BACK, 2 * span + 512), BF16))(n...  17 us
    pallas_call x9, Pallas kernels, run(): pl.pallas_call(kernel, in_specs=specs, out_specs=jax.tree.map(lambda _: v...  14 us
    all_to_all x1, blocking collectives, to_hidden(): over_ctx(sums)  13.4 us
    ppermute x1, starting transfers between devices, shards(): cot_far = lax.ppermute(cot_far, PAIR, PAIR_PERM)  12.9 us
    all_to_all x1, starting transfers between devices, shards(): lax.all_to_all(v, ALL_Z, 0, 0, tiled=True)  12.9 us
    ppermute x1, waiting for transfers between devices, shards(): x_far = lax.ppermute(x_far, PAIR, PAIR_PERM)  12.6 us
  transfers between devices with their start and end apart: 7, of which 5 were waited for; matrix products, arithmetic and copies ran while one was open for 2% of the time, Pallas kernels for 4%

profile of v7, /device:TPU:1, one launch (start us, length us, event | category | flops | bytes accessed | tf_op | source)
XLA Modules:
  0.0 178.2 jit_solution(6312363296623383597)
XLA Ops:
  0.6 0.9 copy-done.1
  1.6 0.9 copy-done.2
  3.2 1.7 shard_map.86
  4.9 23.5 %collective-permute-start = (bf16[64,1280]{1,0:T(8,128)(2,1)S(1)}, bf16[64,1280]{1,0:T(8,128)(2,1)}, u32[]{:S(2)}, u32[]{:S(2)}) collective-permute-start(bf16[64,1280]{1,0:T(8,128)(2,1)S(1)} %get-tuple-element.100), channel_id=1, source_target_pairs={{0,520},{520,0},{8,512},{512,8},{1,521},{521,1},{9,513},{513,9},{2... | collective-permute-start | bytes 491528 | tf_op jit(solution)/shard_map/ppermute | solution.py:334
  28.5 15.4 %while.32 = (s32[]{:T(128)}, bf16[64,3840]{1,0:T(8,128)(2,1)}, s32[]{:T(128)}, s32[]{:T(128)}) while((s32[]{:T(128)}, bf16[64,3840]{1,0:T(8,128)(2,1)}, s32[]{:T(128)}, s32[]{:T(128)}) %tuple.49), condition=%wide.region_1.2_spmd, body=%wide.region_0.1_spmd.sunk | while | flops 2 | bytes 2457685 | solution.py:309
  28.5 5.4 %all-to-all-start = ((bf16[8,8,3840]{2,1,0:T(8,128)(2,1)}), bf16[8,8,3840]{2,1,0:T(8,128)(2,1)S(1)}, u32[]{:S(2)}, u32[]{:S(2)}) async-start(bf16[8,8,3840]{2,1,0:T(8,128)(2,1)} %bitcast.14), calls=%async_computation | async-start | bytes 983040 | tf_op jit(solution)/shard_map/while/body/all_to_all | solution.py:335
  33.9 9.1 %all-to-all-done = bf16[8,8,3840]{2,1,0:T(8,128)(2,1)S(1)} async-done(((bf16[8,8,3840]{2,1,0:T(8,128)(2,1)}), bf16[8,8,3840]{2,1,0:T(8,128)(2,1)S(1)}, u32[]{:S(2)}, u32[]{:S(2)}) %all-to-all-start) | async-done | bytes 491552 | tf_op jit(solution)/shard_map/while/body/all_to_all | solution.py:335
  43.1 0.8 copy.19
  43.9 12.6 %collective-permute-done = bf16[64,1280]{1,0:T(8,128)(2,1)} collective-permute-done((bf16[64,1280]{1,0:T(8,128)(2,1)S(1)}, bf16[64,1280]{1,0:T(8,128)(2,1)}, u32[]{:S(2)}, u32[]{:S(2)}) %collective-permute-start) | collective-permute-done | bytes 163872 | tf_op jit(solution)/shard_map/ppermute | solution.py:334
  56.5 5.4 %all-to-all-start.4 = ((bf16[8,8,1280]{2,1,0:T(8,128)(2,1)}), bf16[8,8,1280]{2,1,0:T(8,128)(2,1)S(1)}, u32[]{:S(2)}, u32[]{:S(2)}) async-start(bf16[8,8,1280]{2,1,0:T(8,128)(2,1)} %bitcast.5), calls=%async_computation.4 | async-start | bytes 327680 | tf_op jit(solution)/shard_map/all_to_all | solution.py:336
  61.9 0.8 dynamic_slice.12
  62.7 0.8 fusion
  64.2 1.0 shard_map.87.v_ref
  65.3 2.1 %all-to-all-done.4 = bf16[8,8,1280]{2,1,0:T(8,128)(2,1)S(1)} async-done(((bf16[8,8,1280]{2,1,0:T(8,128)(2,1)}), bf16[8,8,1280]{2,1,0:T(8,128)(2,1)S(1)}, u32[]{:S(2)}, u32[]{:S(2)}) %all-to-all-start.4) | async-done | bytes 163872 | tf_op jit(solution)/shard_map/all_to_all | solution.py:336
  67.5 12.9 %collective-permute-start.1 = (bf16[64,1280]{1,0:T(8,128)(2,1)S(1)}, bf16[64,1280]{1,0:T(8,128)(2,1)S(1)}, u32[]{:S(2)}, u32[]{:S(2)}) collective-permute-start(bf16[64,1280]{1,0:T(8,128)(2,1)S(1)} %shard_map.88), channel_id=1, source_target_pairs={{0,520},{520,0},{8,512},{512,8},{1,521},{521,1},{9,513},{513,9},{2... | collective-permute-start | bytes 491528 | tf_op jit(solution)/shard_map/ppermute | solution.py:338
  80.7 29.0 %while.33 = (s32[]{:T(128)}, bf16[160,1024]{1,0:T(8,128)(2,1)}, bf16[4,40,1152]{2,1,0:T(8,128)(2,1)}, s32[]{:T(128)}, bf16[64,3840]{1,0:T(8,128)(2,1)}, /*index=...) while((s32[]{:T(128)}, bf16[160,1024]{1,0:T(8,128)(2,1)}, ...), condition=%wide.region_3.4_spmd, body=%wide.region_2.3_spmd.sunk | while | flops 2 | bytes 3973281 | solution.py:309
  80.7 4.4 %body.2 = (bf16[4,40,2176]{2,1,0:T(8,128)(2,1)S(1)}, bf16[160,1024]{1,0:T(8,128)(2,1)}) custom-call(s32[1]{0:T(128)} %bitcast.16.turn_ref, bf16[64,3840]{1,0:T(8,128)(2,1)} %get-tuple-element.273.near_ref, bf16[64,1280]{1,0:T(8,128)(2,1)S(1)} %get-tuple-element.274.far_ref, bf16[1024,128]{1,0:T(8,128)(2,1)S(1)} %get-tuple-element.275.router_ref, ...), custom_call_target="tpu_custom_call" | custom-call | tf_op jit(solution)/shard_map/while/body/pallas_call | solution.py:295
  85.1 13.4 %all_to_all.58.mine_ref = bf16[4,40,2176]{2,1,0:T(8,128)(2,1)S(1)} all-to-all(bf16[4,40,2176]{2,1,0:T(8,128)(2,1)S(1)} %get-tuple-element.233), channel_id=1, replica_groups=mesh['dh'=2,'dl'=8,'ctx'=4,'zh'=2,'y'=4,'core'=2] {'ctx'}, dimensions={0} | all-to-all | bytes 1392640 | tf_op jit(solution)/shard_map/while/body/all_to_all | solution.py:349
  98.5 0.9 body.3
  99.4 3.5 %all-to-all-start.2 = ((bf16[4,40,1152]{2,1,0:T(8,128)(2,1)}), bf16[4,40,1152]{2,1,0:T(8,128)(2,1)S(1)}, u32[]{:S(2)}, u32[]{:S(2)}) async-start(bf16[4,40,1152]{2,1,0:T(8,128)(2,1)} %body.3), calls=%async_computation.2 | async-start | bytes 737280 | tf_op jit(solution)/shard_map/while/body/all_to_all | solution.py:349
  102.9 6.1 %all-to-all-done.2 = bf16[4,40,1152]{2,1,0:T(8,128)(2,1)S(1)} async-done(((bf16[4,40,1152]{2,1,0:T(8,128)(2,1)}), bf16[4,40,1152]{2,1,0:T(8,128)(2,1)S(1)}, u32[]{:S(2)}, u32[]{:S(2)}) %all-to-all-start.2) | async-done | bytes 368672 | tf_op jit(solution)/shard_map/while/body/all_to_all | solution.py:349
  108.9 0.8 copy-done.5
  109.7 2.5 %shard_map.89 = (bf16[64,1280]{1,0:T(8,128)(2,1)S(1)}, bf16[64,1280]{1,0:T(8,128)(2,1)S(1)}, f32[4,8,160]{2,1,0:T(8,128)S(1)}) custom-call(bf16[4,40,1152]{2,1,0:T(8,128)(2,1)} %get-tuple-element.101.full_ref, bf16[64,3840]{1,0:T(8,128)(2,1)} %get-tuple-element.253.near_ref.cot_near_ref, bf16[64,1280]{1,0:T(8,128)(2,1)S(1)} %collective-permute-done.1.cot_far_ref, ...), custom_call_target="tpu_custom_call" | custom-call | tf_op jit(solution)/shard_map/pallas_call | solution.py:295
  112.3 2.5 %collective-permute-start.2 = (bf16[64,1280]{1,0:T(8,128)(2,1)S(1)}, bf16[64,1280]{1,0:T(8,128)(2,1)S(1)}, u32[]{:S(2)}, u32[]{:S(2)}) collective-permute-start(bf16[64,1280]{1,0:T(8,128)(2,1)S(1)} %get-tuple-element.103), channel_id=1, source_target_pairs={{0,520},{520,0},{8,512},{512,8},{1,521},{521,1},{9,513},{513,9},{2... | collective-permute-start | bytes 491528 | tf_op jit(solution)/shard_map/ppermute | solution.py:358
  114.8 6.7 %all_to_all.56.inner_ref = f32[4,8,160]{2,1,0:T(8,128)S(1)} all-to-all(f32[4,8,160]{2,1,0:T(8,128)S(1)} %get-tuple-element.104), channel_id=1, replica_groups=mesh['dh'=2,'dl'=8,'ctx'=4,'zh'=2,'y'=4,'core'=2] {'ctx'}, dimensions={0} | all-to-all | bytes 40960 | tf_op jit(solution)/shard_map/all_to_all | solution.py:359
  121.4 1.0 shard_map.90
  122.4 36.4 %while.34 = (s32[]{:T(128)}, bf16[32,8,128]{2,1,0:T(8,128)(2,1)}, s32[]{:T(128)}, s32[]{:T(128)}) while((s32[]{:T(128)}, bf16[32,8,128]{2,1,0:T(8,128)(2,1)}, s32[]{:T(128)}, s32[]{:T(128)}) %tuple.55), condition=%wide.region_5.6_spmd, body=%wide.region_4.5_spmd.sunk | while | flops 2 | bytes 327765 | solution.py:309
  122.4 12.9 %all-to-all-start.3 = ((bf16[32,8,128]{2,1,0:T(8,128)(2,1)}), bf16[32,8,128]{2,1,0:T(8,128)(2,1)S(1)}, u32[]{:S(2)}, u32[]{:S(2)}) async-start(bf16[32,8,128]{2,1,0:T(8,128)(2,1)} %get-tuple-element.284), calls=%async_computation.3 | async-start | bytes 131072 | tf_op jit(solution)/shard_map/while/body/all_to_all | solution.py:362
  135.3 22.8 %all-to-all-done.3 = bf16[32,8,128]{2,1,0:T(8,128)(2,1)S(1)} async-done(((bf16[32,8,128]{2,1,0:T(8,128)(2,1)}), bf16[32,8,128]{2,1,0:T(8,128)(2,1)S(1)}, u32[]{:S(2)}, u32[]{:S(2)}) %all-to-all-start.3) | async-done | bytes 65568 | tf_op jit(solution)/shard_map/while/body/all_to_all | solution.py:362
  158.8 0.9 shard_map.91
  159.7 17.0 %all_to_all.57 = bf16[8,8,3072]{2,1,0:T(8,128)(2,1)S(1)} all-to-all(bf16[8,8,3072]{2,1,0:T(8,128)(2,1)S(1)} %bitcast.19), channel_id=1, replica_groups=mesh['dh'=2,'dl'=8,'ctx'=4,'zh'=2,'y'=4,'core'=2] {'y','core'}, dimensions={0} | all-to-all | bytes 786432 | tf_op jit(solution)/shard_map/all_to_all | solution.py:363
  176.7 1.5 shard_map.92
  (23 shorter events, 2.3 us)
Async XLA Ops:
  0.6 1.0 copy-start.1
  1.6 0.9 copy-start.2
  2.5 0.7 copy-start.3
  4.9 51.5 %collective-permute-start = (bf16[64,1280]{1,0:T(8,128)(2,1)S(1)}, bf16[64,1280]{1,0:T(8,128)(2,1)}, u32[]{:S(2)}, u32[]{:S(2)}) collective-permute-start(bf16[64,1280]{1,0:T(8,128)(2,1)S(1)} %get-tuple-element.100), channel_id=1, source_target_pairs={{0,520},{520,0},{8,512},{512,8},{1,521},{521,1},{9,513},{513,9},{2... | collective-permute-start | bytes 491528 | tf_op jit(solution)/shard_map/ppermute | solution.py:334
  28.5 14.6 %all-to-all-start = ((bf16[8,8,3840]{2,1,0:T(8,128)(2,1)}), bf16[8,8,3840]{2,1,0:T(8,128)(2,1)S(1)}, u32[]{:S(2)}, u32[]{:S(2)}) async-start(bf16[8,8,3840]{2,1,0:T(8,128)(2,1)} %bitcast.14), calls=%async_computation | async-start | bytes 983040 | tf_op jit(solution)/shard_map/while/body/all_to_all | solution.py:335
  56.5 11.0 %all-to-all-start.4 = ((bf16[8,8,1280]{2,1,0:T(8,128)(2,1)}), bf16[8,8,1280]{2,1,0:T(8,128)(2,1)S(1)}, u32[]{:S(2)}, u32[]{:S(2)}) async-start(bf16[8,8,1280]{2,1,0:T(8,128)(2,1)} %bitcast.5), calls=%async_computation.4 | async-start | bytes 327680 | tf_op jit(solution)/shard_map/all_to_all | solution.py:336
  67.5 42.2 %collective-permute-start.1 = (bf16[64,1280]{1,0:T(8,128)(2,1)S(1)}, bf16[64,1280]{1,0:T(8,128)(2,1)S(1)}, u32[]{:S(2)}, u32[]{:S(2)}) collective-permute-start(bf16[64,1280]{1,0:T(8,128)(2,1)S(1)} %shard_map.88), channel_id=1, source_target_pairs={{0,520},{520,0},{8,512},{512,8},{1,521},{521,1},{9,513},{513,9},{2... | collective-permute-start | bytes 491528 | tf_op jit(solution)/shard_map/ppermute | solution.py:338
  80.7 29.0 %copy-start = (bf16[1,1024,1024]{2,1,0:T(8,128)(2,1)S(1)}, bf16[1,1024,1024]{2,1,0:T(8,128)(2,1)}, u32[]{:S(2)}) copy-start(bf16[1,1024,1024]{2,1,0:T(8,128)(2,1)} %param.18) | copy-start | bytes 6291460
  99.4 9.5 %all-to-all-start.2 = ((bf16[4,40,1152]{2,1,0:T(8,128)(2,1)}), bf16[4,40,1152]{2,1,0:T(8,128)(2,1)S(1)}, u32[]{:S(2)}, u32[]{:S(2)}) async-start(bf16[4,40,1152]{2,1,0:T(8,128)(2,1)} %body.3), calls=%async_computation.2 | async-start | bytes 737280 | tf_op jit(solution)/shard_map/while/body/all_to_all | solution.py:349
  108.9 0.8 copy-start.5
  109.7 11.7 %copy-start.6 = (bf16[4,40,1152]{2,1,0:T(8,128)(2,1)S(1)}, bf16[4,40,1152]{2,1,0:T(8,128)(2,1)}, u32[]{:S(2)}) copy-start(bf16[4,40,1152]{2,1,0:T(8,128)(2,1)} %get-tuple-element.101.full_ref) | copy-start | bytes 1105924
  109.7 11.7 %copy-start.7 = (bf16[160,1024]{1,0:T(8,128)(2,1)S(1)}, bf16[160,1024]{1,0:T(8,128)(2,1)}, u32[]{:S(2)}) copy-start(bf16[160,1024]{1,0:T(8,128)(2,1)} %get-tuple-element.105.x_ref) | copy-start | bytes 983044
  112.3 64.5 %copy-start.4 = (s32[128,1]{0,1:T(1,128)S(1)}, s32[128,1]{0,1:T(1,128)}, u32[]{:S(2)}) copy-start(s32[128,1]{0,1:T(1,128)} %param.14) | copy-start | bytes 1540
  112.3 46.5 %collective-permute-start.2 = (bf16[64,1280]{1,0:T(8,128)(2,1)S(1)}, bf16[64,1280]{1,0:T(8,128)(2,1)S(1)}, u32[]{:S(2)}, u32[]{:S(2)}) collective-permute-start(bf16[64,1280]{1,0:T(8,128)(2,1)S(1)} %get-tuple-element.103), channel_id=1, source_target_pairs={{0,520},{520,0},{8,512},{512,8},{1,521},{521,1},{9,513},{513,9},{2... | collective-permute-start | bytes 491528 | tf_op jit(solution)/shard_map/ppermute | solution.py:358
  122.4 35.8 %all-to-all-start.3 = ((bf16[32,8,128]{2,1,0:T(8,128)(2,1)}), bf16[32,8,128]{2,1,0:T(8,128)(2,1)S(1)}, u32[]{:S(2)}, u32[]{:S(2)}) async-start(bf16[32,8,128]{2,1,0:T(8,128)(2,1)} %get-tuple-element.284), calls=%async_computation.3 | async-start | bytes 131072 | tf_op jit(solution)/shard_map/while/body/all_to_all | solution.py:362

commit v8 on v5

v8 whole, which is shorter than its diff:
```python
import functools

import jax
import jax.numpy as jnp
from jax import lax
from jax.experimental import pallas as pl
from jax.experimental.pallas import tpu as pltpu
from jax.sharding import Mesh, PartitionSpec as P

BF16 = jnp.bfloat16
F32 = jnp.float32
I32 = jnp.int32
CAP = 10
N_EXP = 16
N_CTX = 4
BLOCK = 24
HALF = 8
BACK = 8
MESH = (2, 8, 4, 2, 4, 2)
NAMES = ("dh", "dl", "ctx", "zh", "y", "core")
TOK = ("dh", "dl", "zh", "y", "core")
ALL_Z = ("dh", "dl", "zh")
IN_Z = ("y", "core")
PAIR = ("dh", "zh")
PAIR_PERM = ((0, 3), (3, 0), (1, 2), (2, 1))


def dot(a, b, dims=((1,), (0,))):
    return lax.dot_general(a, b, (dims, ((), ())), preferred_element_type=F32)


def iota(shape, dim):
    return lax.broadcasted_iota(I32, shape, dim)


def pick(mask):
    return mask.astype(F32).astype(BF16)


def pieces(v):
    a = v.astype(BF16)
    v = v - a.astype(F32)
    b = v.astype(BF16)
    c = (v - b.astype(F32)).astype(BF16)
    return a, b, c


def spread(lane, first, v):
    a, b, c = pieces(v)
    out = jnp.where(lane == first, a.astype(F32), 0.0)
    out = jnp.where(lane == first + 1, b.astype(F32), out)
    return jnp.where(lane == first + 2, c.astype(F32), out)


def gathered(lane, first, v):
    return jnp.sum(jnp.where((lane >= first) & (lane < first + 3), v, 0.0), axis=1, keepdims=True)


def places(q):
    block = jnp.zeros_like(q)
    for k in range(1, N_CTX):
        block = block + (q >= k * BLOCK).astype(I32)
    k = q - block * BLOCK
    second = (k >= CAP).astype(I32)
    return block * 2 + second, k - second * CAP, k < 2 * CAP


def where_to(zh, routes):
    count = routes.shape[1]
    own = iota((count, count), 0) == iota((count, count), 1)
    route = jnp.sum(jnp.where(own, routes, 0).astype(F32), axis=1, keepdims=True).astype(I32)
    ids = iota((count, 128), 1)
    onehot = (route == ids).astype(F32)
    before = pick(iota((count, count), 1) < iota((count, count), 0))
    earlier = dot(before, onehot.astype(BF16))
    position = jnp.sum(earlier * onehot, axis=1, keepdims=True).astype(I32)
    far = jnp.where(route >= HALF, 1, 0)
    far = jnp.where(zh == 1, 1 - far, far)
    place = jnp.where(route >= HALF, route - HALF, route)
    return far, place, position


def packing(base, position, shape):
    slots = iota(shape, 1)
    whole = pick((slots == base + position) & (position < BACK))
    quarters = [pick((slots == base + (position - BACK) * 4 + i) & (position >= BACK)) for i in range(4)]
    return whole, quarters


def pack_kernel(zh_ref, routes_ref, tok_ref, cot_ref, far_ref, near_ref, x_ref, mine_ref, full_ref):
    for ref in (x_ref, mine_ref, full_ref):
        ref[...] = jnp.zeros(ref.shape, BF16)
    far, place, position = where_to(zh_ref[0], routes_ref[...])
    count, width = tok_ref.shape
    quarter = width // 4
    span = width + quarter
    n = HALF * BACK
    whole, quarters = packing(far * n + place * BACK, position, (count, 2 * n))
    turn = ((0,), (0,))
    for ref, near_at, far_out, far_at in ((tok_ref, 0, far_ref, 0), (cot_ref, span, near_ref, 2 * span)):
        main = dot(whole, ref[...], turn).astype(BF16)
        extra = dot(quarters[0], ref[:, :quarter], turn)
        for i in range(1, 4):
            extra = extra + dot(quarters[i], ref[:, i * quarter : (i + 1) * quarter], turn)
        extra = extra.astype(BF16)
        near_ref[:, near_at : near_at + width], near_ref[:, near_at + width : near_at + span] = main[:n], extra[:n]
        far_out[:, far_at : far_at + width], far_out[:, far_at + width : far_at + span] = main[n:], extra[n:]


def chunk_maps(q, slot):
    src, p, real = places(q)
    whole = pick((slot == src * BACK + p) & (p < BACK) & real)
    quarters = [pick((slot == src * BACK + (p - BACK) * 4 + i) & (p >= BACK) & real) for i in range(4)]
    return whole, quarters


def unpacking():
    shape = (N_CTX * BLOCK, HALF * BACK)
    return chunk_maps(iota(shape, 0), iota(shape, 1))


def unpack(maps, main, extra):
    whole, quarters = maps
    quarter = extra.shape[1]
    return [dot(whole, main[:, i * quarter : (i + 1) * quarter]) + dot(quarters[i], extra) for i in range(4)]


def up_kernel(turn_ref, rows_ref, router_ref, gate_ref, up_ref, part_ref, x_ref):
    width, hid = gate_ref.shape
    quarter = width // 4
    for i, block in enumerate(unpack(unpacking(), rows_ref[:, :width], rows_ref[:, width : width + quarter])):
        x_ref[:, i * quarter : (i + 1) * quarter] = block.astype(BF16)
    x = x_ref[...]

    def put(v, at):
        for i in range(N_CTX):
            part_ref[i, :, at : at + v.shape[1]] = v[i * BLOCK : (i + 1) * BLOCK].astype(BF16)

    logit = jnp.sum(dot(x, router_ref[...]), axis=1, keepdims=True)
    put(spread(iota((N_CTX * BLOCK, 128), 1), 0, logit), 2 * hid)
    put(dot(x, gate_ref[...]), 0)
    put(dot(x, up_ref[...]), hid)


def hidden_kernel(near_ref, far_ref, out_ref):
    hid = (near_ref.shape[2] - 128) // 2
    halves = []
    for ref in (near_ref, far_ref):

        def total(at, size):
            out = ref[0, :, at : at + size].astype(F32)
            for i in range(1, N_CTX):
                out = out + ref[i, :, at : at + size].astype(F32)
            return out

        gate, up = total(0, hid), total(hid, hid)
        logit = jnp.sum(total(2 * hid, 128), axis=1, keepdims=True)
        score = 1.0 / (1.0 + jnp.exp(-logit))
        halves.append((gate / (1.0 + jnp.exp(-gate)) * up, spread(iota((BLOCK, 128), 1), 0, score)))
    hidden, small = (jnp.concatenate(v, axis=0).astype(BF16) for v in zip(*halves))
    for i in range(N_CTX):
        out_ref[i, :, :hid] = hidden
        out_ref[i, :, hid:] = small


def half_of(v, half):
    at = [(2 * i + half) * BLOCK for i in range(N_CTX)]
    return jnp.concatenate([v[k : k + BLOCK] for k in at], axis=0)


def to_rows(v):
    size = v.shape[0]
    eye = pick(iota((size, size), 0) == iota((size, size), 1))
    return dot(v, eye, ((0,), (0,)))


def down_kernel(full_ref, cot_near_ref, cot_far_ref, down_ref, near_ref, far_ref, inner_ref):
    hid, width = down_ref.shape
    quarter = width // 4
    span = width + quarter
    full = jnp.concatenate([full_ref[i].astype(F32) for i in range(N_CTX)], axis=0)
    score = gathered(iota((full.shape[0], 128), 1), 0, full[:, hid:])
    values = dot(full[:, :hid].astype(BF16), down_ref[...]).astype(BF16).astype(F32)
    n = N_CTX * BLOCK
    back, maps = chunk_maps(iota((HALF * BACK, n), 1), iota((HALF * BACK, n), 0)), unpacking()
    lane = iota((n, 128), 1)
    halves = ((cot_near_ref, span, near_ref), (cot_far_ref, 0, far_ref))
    for half, (cot_ref, at, ref) in enumerate(halves):
        mine = half_of(values, half)
        inner = jnp.zeros((n, 1), F32)
        for i, block in enumerate(unpack(maps, cot_ref[:, at : at + width], cot_ref[:, at + width : at + span])):
            inner = inner + jnp.sum(block * mine[:, i * quarter : (i + 1) * quarter], axis=1, keepdims=True)
        turned = to_rows(spread(lane, 0, inner).astype(BF16))
        inner = turned[0:1] + turned[1:2] + turned[2:3]
        for i in range(N_CTX):
            inner_ref[i, 8 * half : 8 * half + 8, :] = jnp.broadcast_to(inner, (8, n))
        mine = (half_of(score, half) * mine).astype(BF16)
        ref[:, :width] = dot(back[0], mine).astype(BF16)
        extra = dot(back[1][0], mine[:, :quarter])
        for i in range(1, 4):
            extra = extra + dot(back[1][i], mine[:, i * quarter : (i + 1) * quarter])
        ref[:, width:] = extra.astype(BF16)


def relay_kernel(near_ref, x_all_ref, out_ref):
    out_ref[...] = near_ref[:, near_ref.shape[1] - out_ref.shape[1] :]


def grad_kernel(inner_ref, full_ref, near_ref, far_ref, out_ref):
    hid = full_ref.shape[2] - 128
    small = jnp.concatenate([full_ref[i, :, hid:].astype(F32) for i in range(N_CTX)], axis=0)
    grad = jnp.zeros((1, near_ref.shape[1]), F32)
    for half, x_ref in enumerate((near_ref, far_ref)):
        turned = to_rows(half_of(small, half).astype(BF16))
        score = turned[0:1] + turned[1:2] + turned[2:3]
        inner = inner_ref[0, 8 * half : 8 * half + 8, :]
        for i in range(1, N_CTX):
            inner = inner + inner_ref[i, 8 * half : 8 * half + 8, :]
        slope = inner * (score * (1.0 - score))
        a, b, c = (v.astype(F32) for v in pieces(slope))
        line = iota(slope.shape, 0)
        slope = jnp.where(line == 0, a, jnp.where(line == 1, b, jnp.where(line == 2, c, 0.0)))
        grad = grad + jnp.sum(dot(slope.astype(BF16), x_ref[...]), axis=0, keepdims=True)
    copies = out_ref.shape[0]
    lines = []
    for j in range(8):
        lines.append(grad[:, j * 128 : (j + 1) * 128])
    block = jnp.concatenate(lines, axis=0).astype(out_ref.dtype)
    for k in range(copies):
        out_ref[k] = block


def merge_kernel(near_ref, far_ref, grads_ref, out_ref):
    span = near_ref.shape[1]
    out_ref[:, :span] = near_ref[...]
    out_ref[:, span : 2 * span] = far_ref[...]
    parts = grads_ref.shape[0] // 2
    for zh in range(2):
        total = grads_ref[zh].astype(F32)
        for k in range(1, parts):
            total = total + grads_ref[2 * k + zh].astype(F32)
        high = total.astype(BF16)
        low = (total - high.astype(F32)).astype(BF16)
        for at, v in ((2 * span + zh * 128, high), (2 * span + 256 + zh * 128, low)):
            out_ref[:, at : at + 128] = jnp.concatenate([v.astype(F32)] * HALF, axis=0).astype(BF16)


def out_kernel(zh_ref, routes_ref, fin_ref, out_ref, grad_ref):
    far, place, position = where_to(zh_ref[0], routes_ref[...])
    count, width = out_ref.shape
    quarter = width // 4
    span = width + quarter
    n = HALF * BACK
    slots = iota((count, n), 1)
    base = place * BACK
    for half in range(2):
        here = far == half
        of_main = pick((slots == base + position) & (position < BACK) & here)
        main = dot(of_main, fin_ref[:, half * span : half * span + width])
        extra = fin_ref[:, half * span + width : (half + 1) * span]
        for i in range(4):
            cols = slice(i * quarter, (i + 1) * quarter)
            of_extra = pick((slots == base + (position - BACK) * 4 + i) & (position >= BACK) & here)
            value = main[:, cols] + dot(of_extra, extra)
            if half:
                value = value + out_ref[:, cols].astype(F32)
            out_ref[:, cols] = value.astype(BF16)
    line, r = iota((N_EXP, n), 0), iota((N_EXP, n), 1)
    place = jnp.where(line >= HALF, line - HALF, line)
    for j in range(8):
        total = jnp.zeros((N_EXP, 128), F32)
        for zh in range(2):
            take = pick((r == place * BACK + j) & ((line >= HALF) == (zh == 1)))
            for part in range(2):
                at = 2 * span + part * 256 + zh * 128
                total = total + dot(take, fin_ref[:, at : at + 128])
        grad_ref[:, j * 128 : (j + 1) * 128] = total


def call(kernel, out, scalars=0, scratch=()):
    def run(*args):
        smem = pl.BlockSpec(memory_space=pltpu.SMEM)
        vmem = pl.BlockSpec(memory_space=pltpu.VMEM)
        specs = [smem if i < scalars else vmem for i in range(len(args))]
        return pl.pallas_call(
            kernel,
            in_specs=specs,
            out_specs=jax.tree.map(lambda _: vmem, out),
            out_shape=out,
            scratch_shapes=scratch,
            compiler_params=pltpu.CompilerParams(vmem_limit_bytes=16 * 1024 * 1024),
        )(*args)

    return run


def as_one_step(turns, body, state):
    out = lax.while_loop(lambda s: s[0] < turns, lambda s: (s[0] + 1, *body(s[0], *s[1:])), (jnp.int32(0), *state))
    return out[1:]


def shards(tokens, routes, router_weight, gate_weight, up_weight, down_weight, cotangent):
    count, width = tokens.shape
    routes = routes.reshape(1, count)
    hid = gate_weight.shape[2]
    shape = jax.ShapeDtypeStruct
    zh = lax.axis_index("zh").astype(I32)
    expert = zh * HALF + lax.axis_index("y") * 2 + lax.axis_index("core")
    zh = zh.reshape(1)
    turns = 1 + lax.axis_index("ctx").astype(I32) // N_CTX
    span = width + width // 4
    exchange = functools.partial(lax.all_to_all, axis_name=IN_Z, split_axis=0, concat_axis=0, tiled=True)
    over_ctx = functools.partial(lax.all_to_all, axis_name="ctx", split_axis=0, concat_axis=0, tiled=True)

    chunk = shape((HALF * BACK, span), BF16)
    wide = shape((N_CTX * BLOCK, width), BF16)
    part = shape((N_CTX, BLOCK, 2 * hid + 128), BF16)
    whole = shape((N_CTX, 2 * BLOCK, hid + 128), BF16)
    x_far, near, x, mine, full = call(
        pack_kernel,
        (chunk, shape((HALF * BACK, 3 * span), BF16), wide, part, whole),
        1,
    )(zh, routes, tokens, cotangent)
    router_col = lax.dynamic_slice(router_weight, (lax.axis_index("ctx") * width, expert), (width, 1))
    router_col = jnp.concatenate([*pieces(router_col), jnp.zeros((width, 125), BF16)], axis=1)
    weights = router_col, gate_weight[0], up_weight[0]
    x_far = lax.ppermute(x_far, PAIR, PAIR_PERM)

    def near_half(turn, near, x, mine):
        near = exchange(near)
        sums, x = call(up_kernel, (part, wide), 1)(turn.reshape(1), near, *weights)
        return near, x, over_ctx(sums)

    near, x_near, mine_near = as_one_step(turns, near_half, (near, x, mine))
    x_all = exchange(x_far)
    cot_far = lax.ppermute(call(relay_kernel, chunk)(near, x_all), PAIR, PAIR_PERM)

    def to_hidden(turn, x, full):
        sums, x = call(up_kernel, (part, wide), 1)(turn.reshape(1), x_all, *weights)
        return x, over_ctx(call(hidden_kernel, whole)(mine_near, over_ctx(sums)))

    x_far, full = as_one_step(turns, to_hidden, (x, full))

    near_back, far, inner = call(
        down_kernel,
        (chunk, chunk, shape((N_CTX, 16, N_CTX * BLOCK), F32)),
    )(full, near, cot_far, down_weight[0])
    far = lax.ppermute(far, PAIR, PAIR_PERM)
    inner = over_ctx(inner)
    grad = call(grad_kernel, shape((lax.axis_size(ALL_Z), 8, width // 8), BF16))(inner, full, x_near, x_far)

    (grads,) = as_one_step(turns, lambda turn, v: (lax.all_to_all(v, ALL_Z, 0, 0, tiled=True),), (grad,))
    fin = exchange(call(merge_kernel, shape((HALF * BACK, 2 * span + 512), BF16))(near_back, far, grads))
    block_out, grad = call(out_kernel, (shape((count, width), BF16), shape((N_EXP, width), F32)), 1)(zh, routes, fin)
    return block_out, grad.T


def solution(mesh):
    fine = Mesh(mesh.devices.reshape(MESH), NAMES)
    ep = ("zh", "y", "core")
    return jax.shard_map(
        shards,
        mesh=fine,
        in_specs=(
            P(TOK, "ctx"),
            P(TOK, None),
            P(),
            P(ep, "ctx", None),
            P(ep, "ctx", None),
            P(ep, None, "ctx"),
            P(TOK, "ctx"),
        ),
        out_specs=(P(TOK, "ctx"), P("ctx", None)),
        check_vma=False,
    )
```

time: 180 us -> 186 us (1.033)
  waiting for transfers between devices: 53.8 us -> 44.5 us
  blocking collectives: 37.1 us -> 42.9 us
  starting transfers between devices: 66.2 us -> 70.8 us
  Pallas kernels: 13.4 us -> 17 us
    ppermute x1, waiting for transfers between devices: 12.6 us -> 0.01 us  [shards(): x_far = lax.ppermute(x_far, PAIR, PAIR_PERM)]
    ppermute x1, starting transfers between devices: 2.5 us -> 10.9 us  [shards(): far = lax.ppermute(far, PAIR, PAIR_PERM)]
    all_to_all x1 -> x2, blocking collectives: 13.4 us -> 21.6 us  [the longest x1 11.2 us: shards(): x_all = exchange(x_far)]
    ppermute x1, starting transfers between devices: 12.9 us -> 7.62 us  [shards(): lax.ppermute(call(relay_kernel, chunk)(near, x_all), PAIR, PAIR_PERM)]
    pallas_call x8 -> x9, Pallas kernels: 13.4 us -> 17 us  [run(): pl.pallas_call(kernel, in_specs=specs, out_specs=jax.tree.map(lambda _: v...]
    all_to_all x3, waiting for transfers between devices: 18.4 us -> 21.7 us  [the longest x1 9.13 us: near_half(): near = exchange(near)]
    all_to_all x1, starting transfers between devices: 12.9 us -> 15.9 us  [shards(): lax.all_to_all(v, ALL_Z, 0, 0, tiled=True)]
    all_to_all x1, blocking collectives: 17 us -> 14.3 us  [shards(): exchange(call(merge_kernel, shape((HALF * BACK, 2 * span + 512), BF16))(n...]
  transfers between devices with their start and end apart: 7 -> 7, of which waited for: 5 -> 4; matrix products, arithmetic and copies ran while one was open for 2% -> 3% of each run, Pallas kernels for 3% -> 5%
where the time goes in v8:
time: 186 us; the launch traced here: 185 us
  starting transfers between devices  70.8 us (38%)
  waiting for transfers between devices  44.5 us (24%)
  blocking collectives  42.9 us (23%)
  Pallas kernels  17 us (9%)
  local copies, waits for them, and re-layouts  7.78 us (4%)
    ppermute x1, starting transfers between devices, shards(): x_far = lax.ppermute(x_far, PAIR, PAIR_PERM)  23.5 us
    all_to_all x1, waiting for transfers between devices, shards(): lax.all_to_all(v, ALL_Z, 0, 0, tiled=True)  22.8 us
    pallas_call x9, Pallas kernels, run(): pl.pallas_call(kernel, in_specs=specs, out_specs=jax.tree.map(lambda _: v...  17 us
    all_to_all x1, starting transfers between devices, shards(): lax.all_to_all(v, ALL_Z, 0, 0, tiled=True)  15.9 us
    all_to_all x1, blocking collectives, shards(): exchange(call(merge_kernel, shape((HALF * BACK, 2 * span + 512), BF16))(n...  14.3 us
    all_to_all x1, blocking collectives, shards(): x_all = exchange(x_far)  11.2 us
    ppermute x1, starting transfers between devices, shards(): far = lax.ppermute(far, PAIR, PAIR_PERM)  10.9 us
    all_to_all x1, blocking collectives, to_hidden(): return (x, over_ctx(call(hidden_kernel, whole)(mine_near, over_ctx(sums))))  10.4 us
  transfers between devices with their start and end apart: 7, of which 4 were waited for; matrix products, arithmetic and copies ran while one was open for 3% of the time, Pallas kernels for 5%

profile of v8, /device:TPU:1, one launch (start us, length us, event | category | flops | bytes accessed | tf_op | source)
XLA Modules:
  0.0 185.0 jit_solution(12265989403648700748)
XLA Ops:
  0.6 0.9 copy-done.1
  1.6 0.9 copy-done.2
  3.2 1.8 shard_map.86
  5.0 23.5 %collective-permute-start = (bf16[64,1280]{1,0:T(8,128)(2,1)S(1)}, bf16[64,1280]{1,0:T(8,128)(2,1)}, u32[]{:S(2)}, u32[]{:S(2)}) collective-permute-start(bf16[64,1280]{1,0:T(8,128)(2,1)S(1)} %get-tuple-element.126), channel_id=1, source_target_pairs={{0,520},{520,0},{8,512},{512,8},{1,521},{521,1},{9,513},{513,9},{2... | collective-permute-start | bytes 491528 | tf_op jit(solution)/shard_map/ppermute | solution.py:327
  28.5 0.8 fusion
  29.4 0.8 dynamic_slice.12
  31.9 29.7 %while.36 = (s32[]{:T(128)}, bf16[64,3840]{1,0:T(8,128)(2,1)}, bf16[96,1024]{1,0:T(8,128)(2,1)}, bf16[4,24,2176]{2,1,0:T(8,128)(2,1)}, s32[]{:T(128)}, /*index=5...) while((s32[]{:T(128)}, bf16[64,3840]{1,0:T(8,128)(2,1)}, ...), condition=%wide.region_1.2_spmd, body=%wide.region_0.1_spmd.sunk | while | flops 2 | bytes 5382329 | solution.py:298
  32.0 5.4 %all-to-all-start = ((bf16[8,8,3840]{2,1,0:T(8,128)(2,1)}), bf16[8,8,3840]{2,1,0:T(8,128)(2,1)S(1)}, u32[]{:S(2)}, u32[]{:S(2)}) async-start(bf16[8,8,3840]{2,1,0:T(8,128)(2,1)} %bitcast.18), calls=%async_computation | async-start | bytes 983040 | tf_op jit(solution)/shard_map/while/body/all_to_all | solution.py:330
  37.4 9.1 %all-to-all-done = bf16[8,8,3840]{2,1,0:T(8,128)(2,1)S(1)} async-done(((bf16[8,8,3840]{2,1,0:T(8,128)(2,1)}), bf16[8,8,3840]{2,1,0:T(8,128)(2,1)S(1)}, u32[]{:S(2)}, u32[]{:S(2)}) %all-to-all-start) | async-done | bytes 491552 | tf_op jit(solution)/shard_map/while/body/all_to_all | solution.py:330
  46.5 3.4 %body.3 = (bf16[4,24,2176]{2,1,0:T(8,128)(2,1)}, bf16[96,1024]{1,0:T(8,128)(2,1)}) custom-call(s32[1]{0:T(128)} %bitcast.20.turn_ref, bf16[64,3840]{1,0:T(8,128)(2,1)S(1)} %bitcast.22, bf16[1024,128]{1,0:T(8,128)(2,1)S(1)} %get-tuple-element.331.router_ref, bf16[1024,1024]{1,0:T(8,128)(2,1)S(1)} %get-tuple-element.332.gate_ref, ...), custom_call_target="tpu_custom_call" | custom-call | tf_op jit(solution)/shard_map/while/body/pallas_call | solution.py:285
  49.9 4.0 %all-to-all-start.1 = ((bf16[4,24,2176]{2,1,0:T(8,128)(2,1)}), bf16[4,24,2176]{2,1,0:T(8,128)(2,1)S(1)}, u32[]{:S(2)}, u32[]{:S(2)}) async-start(bf16[4,24,2176]{2,1,0:T(8,128)(2,1)} %get-tuple-element.295), calls=%async_computation.1 | async-start | bytes 835584 | tf_op jit(solution)/shard_map/while/body/all_to_all | solution.py:332
  53.9 0.8 copy.22
  54.7 6.1 %all-to-all-done.1 = bf16[4,24,2176]{2,1,0:T(8,128)(2,1)S(1)} async-done(((bf16[4,24,2176]{2,1,0:T(8,128)(2,1)}), bf16[4,24,2176]{2,1,0:T(8,128)(2,1)S(1)}, u32[]{:S(2)}, u32[]{:S(2)}) %all-to-all-start.1) | async-done | bytes 417824 | tf_op jit(solution)/shard_map/while/body/all_to_all | solution.py:332
  61.6 11.2 %all_to_all.61 = bf16[8,8,1280]{2,1,0:T(8,128)(2,1)S(1)} all-to-all(bf16[8,8,1280]{2,1,0:T(8,128)(2,1)} %bitcast.6), channel_id=1, replica_groups=mesh['dh'=2,'dl'=8,'ctx'=4,'zh'=2,'y'=4,'core'=2] {'y','core'}, dimensions={0} | all-to-all | bytes 327680 | tf_op jit(solution)/shard_map/all_to_all | solution.py:335
  72.8 1.0 shard_map.87
  73.9 7.6 %collective-permute-start.1 = (bf16[64,1280]{1,0:T(8,128)(2,1)S(1)}, bf16[64,1280]{1,0:T(8,128)(2,1)S(1)}, u32[]{:S(2)}, u32[]{:S(2)}) collective-permute-start(bf16[64,1280]{1,0:T(8,128)(2,1)S(1)} %shard_map.87), channel_id=1, source_target_pairs={{0,520},{520,0},{8,512},{512,8},{1,521},{521,1},{9,513},{513,9},{2... | collective-permute-start | bytes 491528 | tf_op jit(solution)/shard_map/ppermute | solution.py:336
  81.5 25.5 %while.37 = (s32[]{:T(128)}, bf16[96,1024]{1,0:T(8,128)(2,1)}, bf16[4,48,1152]{2,1,0:T(8,128)(2,1)}, s32[]{:T(128)}, bf16[64,1280]{1,0:T(8,128)(2,1)S(1)}, /*ind...) while((s32[]{:T(128)}, bf16[96,1024]{1,0:T(8,128)(2,1)}, ...), condition=%wide.region_3.4_spmd, body=%wide.region_2.3_spmd.sunk | while | flops 2 | bytes 5603517 | solution.py:298
  81.6 3.4 %body.4 = (bf16[4,24,2176]{2,1,0:T(8,128)(2,1)S(1)}, bf16[96,1024]{1,0:T(8,128)(2,1)}) custom-call(s32[1]{0:T(128)} %bitcast.21.turn_ref, bf16[64,1280]{1,0:T(8,128)(2,1)S(1)} %get-tuple-element.359.rows_ref, bf16[1024,128]{1,0:T(8,128)(2,1)S(1)} %get-tuple-element.360.router_ref, bf16[1024,1024]{1,0:T(8,128)(2,1)} %get-tuple-element.361.gate_ref, ...), custom_call_target="tpu_custom_call" | custom-call | tf_op jit(solution)/shard_map/while/body/pallas_call | solution.py:285
  85.0 10.4 %all_to_all.64.far_ref = bf16[4,24,2176]{2,1,0:T(8,128)(2,1)S(1)} all-to-all(bf16[4,24,2176]{2,1,0:T(8,128)(2,1)S(1)} %get-tuple-element.304), channel_id=1, replica_groups=mesh['dh'=2,'dl'=8,'ctx'=4,'zh'=2,'y'=4,'core'=2] {'ctx'}, dimensions={0} | all-to-all | bytes 835584 | tf_op jit(solution)/shard_map/while/body/all_to_all | solution.py:340
  95.4 1.0 body.5
  96.4 3.5 %all-to-all-start.3 = ((bf16[4,48,1152]{2,1,0:T(8,128)(2,1)}), bf16[4,48,1152]{2,1,0:T(8,128)(2,1)S(1)}, u32[]{:S(2)}, u32[]{:S(2)}) async-start(bf16[4,48,1152]{2,1,0:T(8,128)(2,1)} %body.5), calls=%async_computation.3 | async-start | bytes 884736 | tf_op jit(solution)/shard_map/while/body/all_to_all | solution.py:340
  99.8 6.5 %all-to-all-done.3 = bf16[4,48,1152]{2,1,0:T(8,128)(2,1)S(1)} async-done(((bf16[4,48,1152]{2,1,0:T(8,128)(2,1)}), bf16[4,48,1152]{2,1,0:T(8,128)(2,1)S(1)}, u32[]{:S(2)}, u32[]{:S(2)}) %all-to-all-start.3) | async-done | bytes 442400 | tf_op jit(solution)/shard_map/while/body/all_to_all | solution.py:340
  107.1 2.8 %shard_map.88 = (bf16[64,1280]{1,0:T(8,128)(2,1)S(1)}, bf16[64,1280]{1,0:T(8,128)(2,1)S(1)}, f32[4,16,96]{2,1,0:T(8,128)S(1)}) custom-call(bf16[4,48,1152]{2,1,0:T(8,128)(2,1)} %get-tuple-element.130.full_ref, bf16[64,3840]{1,0:T(8,128)(2,1)} %get-tuple-element.131.near_ref.cot_near_ref, bf16[64,1280]{1,0:T(8,128)(2,1)S(1)} %collective-permute-done.1.cot_far_ref, ...), custom_call_target="tpu_custom_call" | custom-call | tf_op jit(solution)/shard_map/pallas_call | solution.py:285
  109.9 10.9 %collective-permute-start.2 = (bf16[64,1280]{1,0:T(8,128)(2,1)S(1)}, bf16[64,1280]{1,0:T(8,128)(2,1)S(1)}, u32[]{:S(2)}, u32[]{:S(2)}) collective-permute-start(bf16[64,1280]{1,0:T(8,128)(2,1)S(1)} %get-tuple-element.133), channel_id=1, source_target_pairs={{0,520},{520,0},{8,512},{512,8},{1,521},{521,1},{9,513},{513,9},{2... | collective-permute-start | bytes 491528 | tf_op jit(solution)/shard_map/ppermute | solution.py:348
  120.8 7.0 %all_to_all.62.inner_ref = f32[4,16,96]{2,1,0:T(8,128)S(1)} all-to-all(f32[4,16,96]{2,1,0:T(8,128)S(1)} %get-tuple-element.134), channel_id=1, replica_groups=mesh['dh'=2,'dl'=8,'ctx'=4,'zh'=2,'y'=4,'core'=2] {'ctx'}, dimensions={0} | all-to-all | bytes 49152 | tf_op jit(solution)/shard_map/all_to_all | solution.py:349
  127.8 1.1 shard_map.89
  129.0 39.4 %while.38 = (s32[]{:T(128)}, bf16[32,8,128]{2,1,0:T(8,128)(2,1)}, s32[]{:T(128)}, s32[]{:T(128)}) while((s32[]{:T(128)}, bf16[32,8,128]{2,1,0:T(8,128)(2,1)}, s32[]{:T(128)}, s32[]{:T(128)}) %tuple.55), condition=%wide.region_5.6_spmd, body=%wide.region_4.5_spmd.sunk | while | flops 2 | bytes 327765 | solution.py:298
  129.0 15.9 %all-to-all-start.4 = ((bf16[32,8,128]{2,1,0:T(8,128)(2,1)}), bf16[32,8,128]{2,1,0:T(8,128)(2,1)S(1)}, u32[]{:S(2)}, u32[]{:S(2)}) async-start(bf16[32,8,128]{2,1,0:T(8,128)(2,1)} %get-tuple-element.370), calls=%async_computation.4 | async-start | bytes 131072 | tf_op jit(solution)/shard_map/while/body/all_to_all | solution.py:352
  144.9 22.8 %all-to-all-done.4 = bf16[32,8,128]{2,1,0:T(8,128)(2,1)S(1)} async-done(((bf16[32,8,128]{2,1,0:T(8,128)(2,1)}), bf16[32,8,128]{2,1,0:T(8,128)(2,1)S(1)}, u32[]{:S(2)}, u32[]{:S(2)}) %all-to-all-start.4) | async-done | bytes 65568 | tf_op jit(solution)/shard_map/while/body/all_to_all | solution.py:352
  168.3 0.9 shard_map.90
  169.2 14.3 %all_to_all.63 = bf16[8,8,3072]{2,1,0:T(8,128)(2,1)S(1)} all-to-all(bf16[8,8,3072]{2,1,0:T(8,128)(2,1)S(1)} %bitcast.26), channel_id=1, replica_groups=mesh['dh'=2,'dl'=8,'ctx'=4,'zh'=2,'y'=4,'core'=2] {'y','core'}, dimensions={0} | all-to-all | bytes 786432 | tf_op jit(solution)/shard_map/all_to_all | solution.py:353
  183.5 1.5 shard_map.91
  (35 shorter events, 4.5 us)
Async XLA Ops:
  0.6 1.0 copy-start.1
  1.6 0.9 copy-start.2
  2.5 0.7 copy-start.3
  3.2 28.7 %copy-start.5 = (bf16[1,1024,1024]{2,1,0:T(8,128)(2,1)S(1)}, bf16[1,1024,1024]{2,1,0:T(8,128)(2,1)}, u32[]{:S(2)}) copy-start(bf16[1,1024,1024]{2,1,0:T(8,128)(2,1)} %param.16) | copy-start | bytes 6291460
  5.0 26.9 %copy-start.10 = (bf16[96,1024]{1,0:T(8,128)(2,1)}, bf16[96,1024]{1,0:T(8,128)(2,1)S(1)}, u32[]{:S(2)}) copy-start(bf16[96,1024]{1,0:T(8,128)(2,1)S(1)} %get-tuple-element.336) | copy-start | bytes 589828
  5.0 56.6 %collective-permute-start = (bf16[64,1280]{1,0:T(8,128)(2,1)S(1)}, bf16[64,1280]{1,0:T(8,128)(2,1)}, u32[]{:S(2)}, u32[]{:S(2)}) collective-permute-start(bf16[64,1280]{1,0:T(8,128)(2,1)S(1)} %get-tuple-element.126), channel_id=1, source_target_pairs={{0,520},{520,0},{8,512},{512,8},{1,521},{521,1},{9,513},{513,9},{2... | collective-permute-start | bytes 491528 | tf_op jit(solution)/shard_map/ppermute | solution.py:327
  32.0 14.6 %all-to-all-start = ((bf16[8,8,3840]{2,1,0:T(8,128)(2,1)}), bf16[8,8,3840]{2,1,0:T(8,128)(2,1)S(1)}, u32[]{:S(2)}, u32[]{:S(2)}) async-start(bf16[8,8,3840]{2,1,0:T(8,128)(2,1)} %bitcast.18), calls=%async_computation | async-start | bytes 983040 | tf_op jit(solution)/shard_map/while/body/all_to_all | solution.py:330
  49.9 10.9 %all-to-all-start.1 = ((bf16[4,24,2176]{2,1,0:T(8,128)(2,1)}), bf16[4,24,2176]{2,1,0:T(8,128)(2,1)S(1)}, u32[]{:S(2)}, u32[]{:S(2)}) async-start(bf16[4,24,2176]{2,1,0:T(8,128)(2,1)} %get-tuple-element.295), calls=%async_computation.1 | async-start | bytes 835584 | tf_op jit(solution)/shard_map/while/body/all_to_all | solution.py:332
  60.8 0.8 copy-start.6
  73.9 33.2 %collective-permute-start.1 = (bf16[64,1280]{1,0:T(8,128)(2,1)S(1)}, bf16[64,1280]{1,0:T(8,128)(2,1)S(1)}, u32[]{:S(2)}, u32[]{:S(2)}) collective-permute-start(bf16[64,1280]{1,0:T(8,128)(2,1)S(1)} %shard_map.87), channel_id=1, source_target_pairs={{0,520},{520,0},{8,512},{512,8},{1,521},{521,1},{9,513},{513,9},{2... | collective-permute-start | bytes 491528 | tf_op jit(solution)/shard_map/ppermute | solution.py:336
  81.5 25.5 %copy-start = (bf16[1,1024,1024]{2,1,0:T(8,128)(2,1)S(1)}, bf16[1,1024,1024]{2,1,0:T(8,128)(2,1)}, u32[]{:S(2)}) copy-start(bf16[1,1024,1024]{2,1,0:T(8,128)(2,1)} %param.18) | copy-start | bytes 6291460
  81.6 13.8 %copy-start.7 = (bf16[4,24,2176]{2,1,0:T(8,128)(2,1)S(1)}, bf16[4,24,2176]{2,1,0:T(8,128)(2,1)}, u32[]{:S(2)}) copy-start(bf16[4,24,2176]{2,1,0:T(8,128)(2,1)} %get-tuple-element.363.near_ref) | copy-start | bytes 1253380 | tf_op jit(solution)/shard_map/while
  96.4 9.9 %all-to-all-start.3 = ((bf16[4,48,1152]{2,1,0:T(8,128)(2,1)}), bf16[4,48,1152]{2,1,0:T(8,128)(2,1)S(1)}, u32[]{:S(2)}, u32[]{:S(2)}) async-start(bf16[4,48,1152]{2,1,0:T(8,128)(2,1)} %body.5), calls=%async_computation.3 | async-start | bytes 884736 | tf_op jit(solution)/shard_map/while/body/all_to_all | solution.py:340
  106.3 0.8 copy-start.8
  107.1 20.8 %copy-start.9 = (bf16[4,48,1152]{2,1,0:T(8,128)(2,1)S(1)}, bf16[4,48,1152]{2,1,0:T(8,128)(2,1)}, u32[]{:S(2)}) copy-start(bf16[4,48,1152]{2,1,0:T(8,128)(2,1)} %get-tuple-element.130.full_ref) | copy-start | bytes 1327108
  107.1 20.8 %copy-start.11 = (bf16[96,1024]{1,0:T(8,128)(2,1)S(1)}, bf16[96,1024]{1,0:T(8,128)(2,1)}, u32[]{:S(2)}) copy-start(bf16[96,1024]{1,0:T(8,128)(2,1)} %get-tuple-element.136.far_ref) | copy-start | bytes 589828
  107.1 20.8 %copy-start.12 = (bf16[96,1024]{1,0:T(8,128)(2,1)S(1)}, bf16[96,1024]{1,0:T(8,128)(2,1)}, u32[]{:S(2)}) copy-start(bf16[96,1024]{1,0:T(8,128)(2,1)} %get-tuple-element.135.near_ref) | copy-start | bytes 589828
  109.9 73.6 %copy-start.4 = (s32[128,1]{0,1:T(1,128)S(1)}, s32[128,1]{0,1:T(1,128)}, u32[]{:S(2)}) copy-start(s32[128,1]{0,1:T(1,128)} %param.14) | copy-start | bytes 1540
  109.9 58.4 %collective-permute-start.2 = (bf16[64,1280]{1,0:T(8,128)(2,1)S(1)}, bf16[64,1280]{1,0:T(8,128)(2,1)S(1)}, u32[]{:S(2)}, u32[]{:S(2)}) collective-permute-start(bf16[64,1280]{1,0:T(8,128)(2,1)S(1)} %get-tuple-element.133), channel_id=1, source_target_pairs={{0,520},{520,0},{8,512},{512,8},{1,521},{521,1},{9,513},{513,9},{2... | collective-permute-start | bytes 491528 | tf_op jit(solution)/shard_map/ppermute | solution.py:348
  129.0 38.7 %all-to-all-start.4 = ((bf16[32,8,128]{2,1,0:T(8,128)(2,1)}), bf16[32,8,128]{2,1,0:T(8,128)(2,1)S(1)}, u32[]{:S(2)}, u32[]{:S(2)}) async-start(bf16[32,8,128]{2,1,0:T(8,128)(2,1)} %get-tuple-element.370), calls=%async_computation.4 | async-start | bytes 131072 | tf_op jit(solution)/shard_map/while/body/all_to_all | solution.py:352

commit v9 on v7

--- a/solution.py
+++ b/solution.py
@@ -120,10 +120,7 @@
     return [dot(whole, main[:, i * quarter : (i + 1) * quarter]) + dot(quarters[i], extra) for i in range(4)]
 
 
-def up_kernel(turn_ref, near_ref, far_ref, router_ref, gate_in, up_in, part_ref, x_ref, gate_ref, up_ref, sems):
-    moves = [pltpu.make_async_copy(gate_in.at[0], gate_ref, sems.at[0]), pltpu.make_async_copy(up_in.at[0], up_ref, sems.at[1])]
-    for move in moves:
-        move.start()
+def up_kernel(turn_ref, near_ref, far_ref, router_ref, gate_ref, up_ref, part_ref, x_ref):
     width, hid = gate_ref.shape
     quarter = width // 4
     span = width + quarter
@@ -141,9 +138,7 @@
 
     logit = jnp.sum(dot(x, router_ref[...]), axis=1, keepdims=True)
     put(spread(iota((2 * n, 128), 1), 0, logit), 2 * hid)
-    moves[0].wait()
     put(dot(x, gate_ref[...]), 0)
-    moves[1].wait()
     put(dot(x, up_ref[...]), hid)
 
 
@@ -286,12 +281,11 @@
         grad_ref[:, j * 128 : (j + 1) * 128] = total
 
 
-def call(kernel, out, scalars=0, scratch=(), far_in=(), aliases={}):
+def call(kernel, out, scalars=0, scratch=(), aliases={}):
     def run(*args):
         smem = pl.BlockSpec(memory_space=pltpu.SMEM)
         vmem = pl.BlockSpec(memory_space=pltpu.VMEM)
-        anywhere = pl.BlockSpec(memory_space=pl.ANY)
-        specs = [smem if i < scalars else anywhere if i in far_in else vmem for i in range(len(args))]
+        specs = [smem if i < scalars else vmem for i in range(len(args))]
         return pl.pallas_call(
             kernel,
             in_specs=specs,
@@ -341,11 +335,9 @@
     router_col = jnp.concatenate([*pieces(router_col), jnp.zeros((width, 125), BF16)], axis=1)
     part = shape((N_CTX, rows // N_CTX, 2 * hid + 128), BF16)
 
-    loads = [pltpu.VMEM((width, hid), BF16), pltpu.VMEM((width, hid), BF16), pltpu.SemaphoreType.DMA((2,))]
-
     def to_hidden(turn, x, full):
-        weights = router_col, gate_weight, up_weight
-        sums, x = call(up_kernel, (part, wide), 1, loads, (4, 5))(turn.reshape(1), near, x_all, *weights)
+        weights = router_col, gate_weight[0], up_weight[0]
+        sums, x = call(up_kernel, (part, wide), 1)(turn.reshape(1), near, x_all, *weights)
         return x, over_ctx(call(hidden_kernel, shape(full.shape, BF16))(over_ctx(sums)))
 
     x, full = as_one_step(turns, to_hidden, (x, full))

time: 179 us -> 178 us (level)
  no operation moved by 1% of the time
where the time goes in v9:
time: 178 us
  starting transfers between devices  66.2 us (37%)
  waiting for transfers between devices  52.8 us (30%)
  blocking collectives  37.1 us (21%)
  Pallas kernels  13.3 us (7%)
  local copies, waits for them, and re-layouts  6.29 us (4%)
    ppermute x1, starting transfers between devices, shards(): x_far = lax.ppermute(x_far, PAIR, PAIR_PERM)  23.5 us
    all_to_all x1, waiting for transfers between devices, shards(): lax.all_to_all(v, ALL_Z, 0, 0, tiled=True)  22.8 us
    all_to_all x1, blocking collectives, shards(): exchange(call(merge_kernel, shape((HALF * BACK, 2 * span + 512), BF16))(n...  17 us
    all_to_all x1, blocking collectives, to_hidden(): over_ctx(sums)  13.4 us
    pallas_call x9, Pallas kernels, run(): pl.pallas_call(kernel, in_specs=specs, out_specs=jax.tree.map(lambda _: v...  13.3 us
    ppermute x1, starting transfers between devices, shards(): cot_far = lax.ppermute(cot_far, PAIR, PAIR_PERM)  12.9 us
    all_to_all x1, starting transfers between devices, shards(): lax.all_to_all(v, ALL_Z, 0, 0, tiled=True)  12.9 us
    ppermute x1, waiting for transfers between devices, shards(): x_far = lax.ppermute(x_far, PAIR, PAIR_PERM)  12.6 us
  transfers between devices with their start and end apart: 7, of which 5 were waited for; matrix products, arithmetic and copies ran while one was open for 2% of the time, Pallas kernels for 4%

profile of v9, /device:TPU:1, one launch (start us, length us, event | category | flops | bytes accessed | tf_op | source)
XLA Modules:
  0.0 177.5 jit_solution(15257770867689051212)
XLA Ops:
  0.6 0.9 copy-done.1
  1.6 0.9 copy-done.2
  3.2 1.7 shard_map.86
  4.9 23.5 %collective-permute-start = (bf16[64,1280]{1,0:T(8,128)(2,1)S(1)}, bf16[64,1280]{1,0:T(8,128)(2,1)}, u32[]{:S(2)}, u32[]{:S(2)}) collective-permute-start(bf16[64,1280]{1,0:T(8,128)(2,1)S(1)} %get-tuple-element.100), channel_id=1, source_target_pairs={{0,520},{520,0},{8,512},{512,8},{1,521},{521,1},{9,513},{513,9},{2... | collective-permute-start | bytes 491528 | tf_op jit(solution)/shard_map/ppermute | solution.py:328
  28.5 15.4 %while.32 = (s32[]{:T(128)}, bf16[64,3840]{1,0:T(8,128)(2,1)}, s32[]{:T(128)}, s32[]{:T(128)}) while((s32[]{:T(128)}, bf16[64,3840]{1,0:T(8,128)(2,1)}, s32[]{:T(128)}, s32[]{:T(128)}) %tuple.49), condition=%wide.region_1.2_spmd, body=%wide.region_0.1_spmd.sunk | while | flops 2 | bytes 2457685 | solution.py:303
  28.5 5.4 %all-to-all-start = ((bf16[8,8,3840]{2,1,0:T(8,128)(2,1)}), bf16[8,8,3840]{2,1,0:T(8,128)(2,1)S(1)}, u32[]{:S(2)}, u32[]{:S(2)}) async-start(bf16[8,8,3840]{2,1,0:T(8,128)(2,1)} %bitcast.18), calls=%async_computation | async-start | bytes 983040 | tf_op jit(solution)/shard_map/while/body/all_to_all | solution.py:329
  33.9 9.1 %all-to-all-done = bf16[8,8,3840]{2,1,0:T(8,128)(2,1)S(1)} async-done(((bf16[8,8,3840]{2,1,0:T(8,128)(2,1)}), bf16[8,8,3840]{2,1,0:T(8,128)(2,1)S(1)}, u32[]{:S(2)}, u32[]{:S(2)}) %all-to-all-start) | async-done | bytes 491552 | tf_op jit(solution)/shard_map/while/body/all_to_all | solution.py:329
  43.1 0.8 copy.19
  43.9 12.6 %collective-permute-done = bf16[64,1280]{1,0:T(8,128)(2,1)} collective-permute-done((bf16[64,1280]{1,0:T(8,128)(2,1)S(1)}, bf16[64,1280]{1,0:T(8,128)(2,1)}, u32[]{:S(2)}, u32[]{:S(2)}) %collective-permute-start) | collective-permute-done | bytes 163872 | tf_op jit(solution)/shard_map/ppermute | solution.py:328
  56.5 5.4 %all-to-all-start.4 = ((bf16[8,8,1280]{2,1,0:T(8,128)(2,1)}), bf16[8,8,1280]{2,1,0:T(8,128)(2,1)S(1)}, u32[]{:S(2)}, u32[]{:S(2)}) async-start(bf16[8,8,1280]{2,1,0:T(8,128)(2,1)} %bitcast.7), calls=%async_computation.4 | async-start | bytes 327680 | tf_op jit(solution)/shard_map/all_to_all | solution.py:330
  61.9 0.8 dynamic_slice.12
  62.7 0.8 fusion
  64.2 1.0 shard_map.87.v_ref
  65.3 2.1 %all-to-all-done.4 = bf16[8,8,1280]{2,1,0:T(8,128)(2,1)S(1)} async-done(((bf16[8,8,1280]{2,1,0:T(8,128)(2,1)}), bf16[8,8,1280]{2,1,0:T(8,128)(2,1)S(1)}, u32[]{:S(2)}, u32[]{:S(2)}) %all-to-all-start.4) | async-done | bytes 163872 | tf_op jit(solution)/shard_map/all_to_all | solution.py:330
  67.5 12.9 %collective-permute-start.1 = (bf16[64,1280]{1,0:T(8,128)(2,1)S(1)}, bf16[64,1280]{1,0:T(8,128)(2,1)S(1)}, u32[]{:S(2)}, u32[]{:S(2)}) collective-permute-start(bf16[64,1280]{1,0:T(8,128)(2,1)S(1)} %shard_map.88), channel_id=1, source_target_pairs={{0,520},{520,0},{8,512},{512,8},{1,521},{521,1},{9,513},{513,9},{2... | collective-permute-start | bytes 491528 | tf_op jit(solution)/shard_map/ppermute | solution.py:332
  80.7 28.3 %while.33 = (s32[]{:T(128)}, bf16[160,1024]{1,0:T(8,128)(2,1)}, bf16[4,40,1152]{2,1,0:T(8,128)(2,1)}, s32[]{:T(128)}, bf16[1,1024,1024]{2,1,0:T(8,128)(2,1)}, /*...) while((s32[]{:T(128)}, bf16[160,1024]{1,0:T(8,128)(2,1)}, ...), condition=%wide.region_3.4_spmd, body=%wide.region_2.3_spmd.sunk | while | flops 2 | bytes 3973281 | solution.py:303
  80.7 3.7 %body.2 = (bf16[4,40,2176]{2,1,0:T(8,128)(2,1)S(1)}, bf16[160,1024]{1,0:T(8,128)(2,1)}) custom-call(s32[1]{0:T(128)} %bitcast.20.turn_ref, bf16[64,3840]{1,0:T(8,128)(2,1)} %get-tuple-element.275.near_ref, bf16[64,1280]{1,0:T(8,128)(2,1)S(1)} %get-tuple-element.276.far_ref, bf16[1024,128]{1,0:T(8,128)(2,1)S(1)} %get-tuple-element.277.router_ref, ...), custom_call_target="tpu_custom_call" | custom-call | tf_op jit(solution)/shard_map/while/body/pallas_call | solution.py:289
  84.4 13.4 %all_to_all.58.mine_ref = bf16[4,40,2176]{2,1,0:T(8,128)(2,1)S(1)} all-to-all(bf16[4,40,2176]{2,1,0:T(8,128)(2,1)S(1)} %get-tuple-element.233), channel_id=1, replica_groups=mesh['dh'=2,'dl'=8,'ctx'=4,'zh'=2,'y'=4,'core'=2] {'ctx'}, dimensions={0} | all-to-all | bytes 1392640 | tf_op jit(solution)/shard_map/while/body/all_to_all | solution.py:341
  97.8 0.9 body.3
  98.7 3.5 %all-to-all-start.2 = ((bf16[4,40,1152]{2,1,0:T(8,128)(2,1)}), bf16[4,40,1152]{2,1,0:T(8,128)(2,1)S(1)}, u32[]{:S(2)}, u32[]{:S(2)}) async-start(bf16[4,40,1152]{2,1,0:T(8,128)(2,1)} %body.3), calls=%async_computation.2 | async-start | bytes 737280 | tf_op jit(solution)/shard_map/while/body/all_to_all | solution.py:341
  102.2 6.1 %all-to-all-done.2 = bf16[4,40,1152]{2,1,0:T(8,128)(2,1)S(1)} async-done(((bf16[4,40,1152]{2,1,0:T(8,128)(2,1)}), bf16[4,40,1152]{2,1,0:T(8,128)(2,1)S(1)}, u32[]{:S(2)}, u32[]{:S(2)}) %all-to-all-start.2) | async-done | bytes 368672 | tf_op jit(solution)/shard_map/while/body/all_to_all | solution.py:341
  108.2 0.8 copy-done.5
  109.0 2.5 %shard_map.89 = (bf16[64,1280]{1,0:T(8,128)(2,1)S(1)}, bf16[64,1280]{1,0:T(8,128)(2,1)S(1)}, f32[4,8,160]{2,1,0:T(8,128)S(1)}) custom-call(bf16[4,40,1152]{2,1,0:T(8,128)(2,1)} %get-tuple-element.101.full_ref, bf16[64,3840]{1,0:T(8,128)(2,1)} %get-tuple-element.255.near_ref.cot_near_ref, bf16[64,1280]{1,0:T(8,128)(2,1)S(1)} %collective-permute-done.1.cot_far_ref, ...), custom_call_target="tpu_custom_call" | custom-call | tf_op jit(solution)/shard_map/pallas_call | solution.py:289
  111.6 2.5 %collective-permute-start.2 = (bf16[64,1280]{1,0:T(8,128)(2,1)S(1)}, bf16[64,1280]{1,0:T(8,128)(2,1)S(1)}, u32[]{:S(2)}, u32[]{:S(2)}) collective-permute-start(bf16[64,1280]{1,0:T(8,128)(2,1)S(1)} %get-tuple-element.103), channel_id=1, source_target_pairs={{0,520},{520,0},{8,512},{512,8},{1,521},{521,1},{9,513},{513,9},{2... | collective-permute-start | bytes 491528 | tf_op jit(solution)/shard_map/ppermute | solution.py:350
  114.1 6.7 %all_to_all.56.inner_ref = f32[4,8,160]{2,1,0:T(8,128)S(1)} all-to-all(f32[4,8,160]{2,1,0:T(8,128)S(1)} %get-tuple-element.104), channel_id=1, replica_groups=mesh['dh'=2,'dl'=8,'ctx'=4,'zh'=2,'y'=4,'core'=2] {'ctx'}, dimensions={0} | all-to-all | bytes 40960 | tf_op jit(solution)/shard_map/all_to_all | solution.py:351
  120.7 1.0 shard_map.90
  121.7 36.4 %while.34 = (s32[]{:T(128)}, bf16[32,8,128]{2,1,0:T(8,128)(2,1)}, s32[]{:T(128)}, s32[]{:T(128)}) while((s32[]{:T(128)}, bf16[32,8,128]{2,1,0:T(8,128)(2,1)}, s32[]{:T(128)}, s32[]{:T(128)}) %tuple.55), condition=%wide.region_5.6_spmd, body=%wide.region_4.5_spmd.sunk | while | flops 2 | bytes 327765 | solution.py:303
  121.7 12.9 %all-to-all-start.3 = ((bf16[32,8,128]{2,1,0:T(8,128)(2,1)}), bf16[32,8,128]{2,1,0:T(8,128)(2,1)S(1)}, u32[]{:S(2)}, u32[]{:S(2)}) async-start(bf16[32,8,128]{2,1,0:T(8,128)(2,1)} %get-tuple-element.284), calls=%async_computation.3 | async-start | bytes 131072 | tf_op jit(solution)/shard_map/while/body/all_to_all | solution.py:354
  134.6 22.8 %all-to-all-done.3 = bf16[32,8,128]{2,1,0:T(8,128)(2,1)S(1)} async-done(((bf16[32,8,128]{2,1,0:T(8,128)(2,1)}), bf16[32,8,128]{2,1,0:T(8,128)(2,1)S(1)}, u32[]{:S(2)}, u32[]{:S(2)}) %all-to-all-start.3) | async-done | bytes 65568 | tf_op jit(solution)/shard_map/while/body/all_to_all | solution.py:354
  158.1 0.9 shard_map.91
  159.0 17.0 %all_to_all.57 = bf16[8,8,3072]{2,1,0:T(8,128)(2,1)S(1)} all-to-all(bf16[8,8,3072]{2,1,0:T(8,128)(2,1)S(1)} %bitcast.25), channel_id=1, replica_groups=mesh['dh'=2,'dl'=8,'ctx'=4,'zh'=2,'y'=4,'core'=2] {'y','core'}, dimensions={0} | all-to-all | bytes 786432 | tf_op jit(solution)/shard_map/all_to_all | solution.py:355
  176.0 1.5 shard_map.92
  (23 shorter events, 2.3 us)
Async XLA Ops:
  0.6 1.0 copy-start.1
  1.6 0.9 copy-start.2
  2.5 0.7 copy-start.3
  4.9 51.5 %collective-permute-start = (bf16[64,1280]{1,0:T(8,128)(2,1)S(1)}, bf16[64,1280]{1,0:T(8,128)(2,1)}, u32[]{:S(2)}, u32[]{:S(2)}) collective-permute-start(bf16[64,1280]{1,0:T(8,128)(2,1)S(1)} %get-tuple-element.100), channel_id=1, source_target_pairs={{0,520},{520,0},{8,512},{512,8},{1,521},{521,1},{9,513},{513,9},{2... | collective-permute-start | bytes 491528 | tf_op jit(solution)/shard_map/ppermute | solution.py:328
  28.5 14.6 %all-to-all-start = ((bf16[8,8,3840]{2,1,0:T(8,128)(2,1)}), bf16[8,8,3840]{2,1,0:T(8,128)(2,1)S(1)}, u32[]{:S(2)}, u32[]{:S(2)}) async-start(bf16[8,8,3840]{2,1,0:T(8,128)(2,1)} %bitcast.18), calls=%async_computation | async-start | bytes 983040 | tf_op jit(solution)/shard_map/while/body/all_to_all | solution.py:329
  56.5 11.0 %all-to-all-start.4 = ((bf16[8,8,1280]{2,1,0:T(8,128)(2,1)}), bf16[8,8,1280]{2,1,0:T(8,128)(2,1)S(1)}, u32[]{:S(2)}, u32[]{:S(2)}) async-start(bf16[8,8,1280]{2,1,0:T(8,128)(2,1)} %bitcast.7), calls=%async_computation.4 | async-start | bytes 327680 | tf_op jit(solution)/shard_map/all_to_all | solution.py:330
  67.5 41.5 %collective-permute-start.1 = (bf16[64,1280]{1,0:T(8,128)(2,1)S(1)}, bf16[64,1280]{1,0:T(8,128)(2,1)S(1)}, u32[]{:S(2)}, u32[]{:S(2)}) collective-permute-start(bf16[64,1280]{1,0:T(8,128)(2,1)S(1)} %shard_map.88), channel_id=1, source_target_pairs={{0,520},{520,0},{8,512},{512,8},{1,521},{521,1},{9,513},{513,9},{2... | collective-permute-start | bytes 491528 | tf_op jit(solution)/shard_map/ppermute | solution.py:332
  80.7 28.3 %copy-start = (bf16[1,1024,1024]{2,1,0:T(8,128)(2,1)S(1)}, bf16[1,1024,1024]{2,1,0:T(8,128)(2,1)}, u32[]{:S(2)}) copy-start(bf16[1,1024,1024]{2,1,0:T(8,128)(2,1)} %param.18) | copy-start | bytes 6291460
  98.7 9.5 %all-to-all-start.2 = ((bf16[4,40,1152]{2,1,0:T(8,128)(2,1)}), bf16[4,40,1152]{2,1,0:T(8,128)(2,1)S(1)}, u32[]{:S(2)}, u32[]{:S(2)}) async-start(bf16[4,40,1152]{2,1,0:T(8,128)(2,1)} %body.3), calls=%async_computation.2 | async-start | bytes 737280 | tf_op jit(solution)/shard_map/while/body/all_to_all | solution.py:341
  108.2 0.8 copy-start.5
  109.0 11.7 %copy-start.6 = (bf16[4,40,1152]{2,1,0:T(8,128)(2,1)S(1)}, bf16[4,40,1152]{2,1,0:T(8,128)(2,1)}, u32[]{:S(2)}) copy-start(bf16[4,40,1152]{2,1,0:T(8,128)(2,1)} %get-tuple-element.101.full_ref) | copy-start | bytes 1105924
  109.0 11.7 %copy-start.7 = (bf16[160,1024]{1,0:T(8,128)(2,1)S(1)}, bf16[160,1024]{1,0:T(8,128)(2,1)}, u32[]{:S(2)}) copy-start(bf16[160,1024]{1,0:T(8,128)(2,1)} %get-tuple-element.105.x_ref) | copy-start | bytes 983044
  111.5 64.4 %copy-start.4 = (s32[128,1]{0,1:T(1,128)S(1)}, s32[128,1]{0,1:T(1,128)}, u32[]{:S(2)}) copy-start(s32[128,1]{0,1:T(1,128)} %param.14) | copy-start | bytes 1540
  111.6 46.5 %collective-permute-start.2 = (bf16[64,1280]{1,0:T(8,128)(2,1)S(1)}, bf16[64,1280]{1,0:T(8,128)(2,1)S(1)}, u32[]{:S(2)}, u32[]{:S(2)}) collective-permute-start(bf16[64,1280]{1,0:T(8,128)(2,1)S(1)} %get-tuple-element.103), channel_id=1, source_target_pairs={{0,520},{520,0},{8,512},{512,8},{1,521},{521,1},{9,513},{513,9},{2... | collective-permute-start | bytes 491528 | tf_op jit(solution)/shard_map/ppermute | solution.py:350
  121.7 35.7 %all-to-all-start.3 = ((bf16[32,8,128]{2,1,0:T(8,128)(2,1)}), bf16[32,8,128]{2,1,0:T(8,128)(2,1)S(1)}, u32[]{:S(2)}, u32[]{:S(2)}) async-start(bf16[32,8,128]{2,1,0:T(8,128)(2,1)} %get-tuple-element.284), calls=%async_computation.3 | async-start | bytes 131072 | tf_op jit(solution)/shard_map/while/body/all_to_all | solution.py:354

commit v10 on v9

--- a/solution.py
+++ b/solution.py
@@ -209,7 +209,7 @@
 
 
 def gate_kernel(v_ref, other_ref, out_ref):
-    pass
+    out_ref[...] = v_ref[...]
 
 
 def grad_kernel(inner_ref, full_ref, x_ref, out_ref):
@@ -281,7 +281,7 @@
         grad_ref[:, j * 128 : (j + 1) * 128] = total
 
 
-def call(kernel, out, scalars=0, scratch=(), aliases={}):
+def call(kernel, out, scalars=0, scratch=()):
     def run(*args):
         smem = pl.BlockSpec(memory_space=pltpu.SMEM)
         vmem = pl.BlockSpec(memory_space=pltpu.VMEM)
@@ -292,7 +292,6 @@
             out_specs=jax.tree.map(lambda _: vmem, out),
             out_shape=out,
             scratch_shapes=scratch,
-            input_output_aliases=aliases,
             compiler_params=pltpu.CompilerParams(vmem_limit_bytes=16 * 1024 * 1024),
         )(*args)
 
@@ -328,7 +327,7 @@
     x_far = lax.ppermute(x_far, PAIR, PAIR_PERM)
     (near,) = as_one_step(turns, lambda turn, v: (exchange(v),), (near,))
     x_all = exchange(x_far)
-    cot_far = call(gate_kernel, chunk, aliases={0: 0})(call(slice_kernel, chunk)(near), x_all)
+    cot_far = call(gate_kernel, chunk)(call(slice_kernel, chunk)(near), x_all)
     cot_far = lax.ppermute(cot_far, PAIR, PAIR_PERM)
 
     router_col = lax.dynamic_slice(router_weight, (lax.axis_index("ctx") * width, expert), (width, 1))

time: 178 us -> 178 us (level)
  no operation moved by 1% of the time
where the time goes in v10:
time: 178 us
  starting transfers between devices  66.2 us (37%)
  waiting for transfers between devices  52.8 us (30%)
  blocking collectives  37.1 us (21%)
  Pallas kernels  13.3 us (7%)
  local copies, waits for them, and re-layouts  6.29 us (4%)
    ppermute x1, starting transfers between devices, shards(): x_far = lax.ppermute(x_far, PAIR, PAIR_PERM)  23.5 us
    all_to_all x1, waiting for transfers between devices, shards(): lax.all_to_all(v, ALL_Z, 0, 0, tiled=True)  22.8 us
    all_to_all x1, blocking collectives, shards(): exchange(call(merge_kernel, shape((HALF * BACK, 2 * span + 512), BF16))(n...  17 us
    all_to_all x1, blocking collectives, to_hidden(): over_ctx(sums)  13.4 us
    pallas_call x9, Pallas kernels, run(): pl.pallas_call(kernel, in_specs=specs, out_specs=jax.tree.map(lambda _: v...  13.3 us
    ppermute x1, starting transfers between devices, shards(): cot_far = lax.ppermute(cot_far, PAIR, PAIR_PERM)  12.9 us
    all_to_all x1, starting transfers between devices, shards(): lax.all_to_all(v, ALL_Z, 0, 0, tiled=True)  12.9 us
    ppermute x1, waiting for transfers between devices, shards(): x_far = lax.ppermute(x_far, PAIR, PAIR_PERM)  12.6 us
  transfers between devices with their start and end apart: 7, of which 5 were waited for; matrix products, arithmetic and copies ran while one was open for 2% of the time, Pallas kernels for 4%

profile of v10, /device:TPU:1, one launch (start us, length us, event | category | flops | bytes accessed | tf_op | source)
XLA Modules:
  0.0 177.5 jit_solution(8014335244767898207)
XLA Ops:
  0.6 0.9 copy-done.1
  1.6 0.9 copy-done.2
  3.2 1.7 shard_map.86
  4.9 23.5 %collective-permute-start = (bf16[64,1280]{1,0:T(8,128)(2,1)S(1)}, bf16[64,1280]{1,0:T(8,128)(2,1)}, u32[]{:S(2)}, u32[]{:S(2)}) collective-permute-start(bf16[64,1280]{1,0:T(8,128)(2,1)S(1)} %get-tuple-element.100), channel_id=1, source_target_pairs={{0,520},{520,0},{8,512},{512,8},{1,521},{521,1},{9,513},{513,9},{2... | collective-permute-start | bytes 491528 | tf_op jit(solution)/shard_map/ppermute | solution.py:327
  28.5 15.4 %while.32 = (s32[]{:T(128)}, bf16[64,3840]{1,0:T(8,128)(2,1)}, s32[]{:T(128)}, s32[]{:T(128)}) while((s32[]{:T(128)}, bf16[64,3840]{1,0:T(8,128)(2,1)}, s32[]{:T(128)}, s32[]{:T(128)}) %tuple.49), condition=%wide.region_1.2_spmd, body=%wide.region_0.1_spmd.sunk | while | flops 2 | bytes 2457685 | solution.py:302
  28.5 5.4 %all-to-all-start = ((bf16[8,8,3840]{2,1,0:T(8,128)(2,1)}), bf16[8,8,3840]{2,1,0:T(8,128)(2,1)S(1)}, u32[]{:S(2)}, u32[]{:S(2)}) async-start(bf16[8,8,3840]{2,1,0:T(8,128)(2,1)} %bitcast.18), calls=%async_computation | async-start | bytes 983040 | tf_op jit(solution)/shard_map/while/body/all_to_all | solution.py:328
  33.9 9.1 %all-to-all-done = bf16[8,8,3840]{2,1,0:T(8,128)(2,1)S(1)} async-done(((bf16[8,8,3840]{2,1,0:T(8,128)(2,1)}), bf16[8,8,3840]{2,1,0:T(8,128)(2,1)S(1)}, u32[]{:S(2)}, u32[]{:S(2)}) %all-to-all-start) | async-done | bytes 491552 | tf_op jit(solution)/shard_map/while/body/all_to_all | solution.py:328
  43.1 0.8 copy.18
  43.9 12.6 %collective-permute-done = bf16[64,1280]{1,0:T(8,128)(2,1)} collective-permute-done((bf16[64,1280]{1,0:T(8,128)(2,1)S(1)}, bf16[64,1280]{1,0:T(8,128)(2,1)}, u32[]{:S(2)}, u32[]{:S(2)}) %collective-permute-start) | collective-permute-done | bytes 163872 | tf_op jit(solution)/shard_map/ppermute | solution.py:327
  56.5 5.4 %all-to-all-start.4 = ((bf16[8,8,1280]{2,1,0:T(8,128)(2,1)}), bf16[8,8,1280]{2,1,0:T(8,128)(2,1)S(1)}, u32[]{:S(2)}, u32[]{:S(2)}) async-start(bf16[8,8,1280]{2,1,0:T(8,128)(2,1)} %bitcast.7), calls=%async_computation.4 | async-start | bytes 327680 | tf_op jit(solution)/shard_map/all_to_all | solution.py:329
  61.9 0.8 dynamic_slice.12
  62.7 0.8 fusion
  64.2 1.0 shard_map.87.v_ref
  65.3 2.1 %all-to-all-done.4 = bf16[8,8,1280]{2,1,0:T(8,128)(2,1)S(1)} async-done(((bf16[8,8,1280]{2,1,0:T(8,128)(2,1)}), bf16[8,8,1280]{2,1,0:T(8,128)(2,1)S(1)}, u32[]{:S(2)}, u32[]{:S(2)}) %all-to-all-start.4) | async-done | bytes 163872 | tf_op jit(solution)/shard_map/all_to_all | solution.py:329
  67.5 12.9 %collective-permute-start.1 = (bf16[64,1280]{1,0:T(8,128)(2,1)S(1)}, bf16[64,1280]{1,0:T(8,128)(2,1)S(1)}, u32[]{:S(2)}, u32[]{:S(2)}) collective-permute-start(bf16[64,1280]{1,0:T(8,128)(2,1)S(1)} %shard_map.88), channel_id=1, source_target_pairs={{0,520},{520,0},{8,512},{512,8},{1,521},{521,1},{9,513},{513,9},{2... | collective-permute-start | bytes 491528 | tf_op jit(solution)/shard_map/ppermute | solution.py:331
  80.7 28.3 %while.33 = (s32[]{:T(128)}, bf16[160,1024]{1,0:T(8,128)(2,1)}, bf16[4,40,1152]{2,1,0:T(8,128)(2,1)}, s32[]{:T(128)}, bf16[1,1024,1024]{2,1,0:T(8,128)(2,1)}, /*...) while((s32[]{:T(128)}, bf16[160,1024]{1,0:T(8,128)(2,1)}, ...), condition=%wide.region_3.4_spmd, body=%wide.region_2.3_spmd.sunk | while | flops 2 | bytes 3973281 | solution.py:302
  80.7 3.7 %body.2 = (bf16[4,40,2176]{2,1,0:T(8,128)(2,1)S(1)}, bf16[160,1024]{1,0:T(8,128)(2,1)}) custom-call(s32[1]{0:T(128)} %bitcast.20.turn_ref, bf16[64,3840]{1,0:T(8,128)(2,1)} %get-tuple-element.275.near_ref, bf16[64,1280]{1,0:T(8,128)(2,1)S(1)} %get-tuple-element.276.far_ref, bf16[1024,128]{1,0:T(8,128)(2,1)S(1)} %get-tuple-element.277.router_ref, ...), custom_call_target="tpu_custom_call" | custom-call | tf_op jit(solution)/shard_map/while/body/pallas_call | solution.py:289
  84.4 13.4 %all_to_all.58.mine_ref = bf16[4,40,2176]{2,1,0:T(8,128)(2,1)S(1)} all-to-all(bf16[4,40,2176]{2,1,0:T(8,128)(2,1)S(1)} %get-tuple-element.233), channel_id=1, replica_groups=mesh['dh'=2,'dl'=8,'ctx'=4,'zh'=2,'y'=4,'core'=2] {'ctx'}, dimensions={0} | all-to-all | bytes 1392640 | tf_op jit(solution)/shard_map/while/body/all_to_all | solution.py:340
  97.8 0.9 body.3
  98.7 3.5 %all-to-all-start.2 = ((bf16[4,40,1152]{2,1,0:T(8,128)(2,1)}), bf16[4,40,1152]{2,1,0:T(8,128)(2,1)S(1)}, u32[]{:S(2)}, u32[]{:S(2)}) async-start(bf16[4,40,1152]{2,1,0:T(8,128)(2,1)} %body.3), calls=%async_computation.2 | async-start | bytes 737280 | tf_op jit(solution)/shard_map/while/body/all_to_all | solution.py:340
  102.2 6.1 %all-to-all-done.2 = bf16[4,40,1152]{2,1,0:T(8,128)(2,1)S(1)} async-done(((bf16[4,40,1152]{2,1,0:T(8,128)(2,1)}), bf16[4,40,1152]{2,1,0:T(8,128)(2,1)S(1)}, u32[]{:S(2)}, u32[]{:S(2)}) %all-to-all-start.2) | async-done | bytes 368672 | tf_op jit(solution)/shard_map/while/body/all_to_all | solution.py:340
  108.2 0.8 copy-done.5
  109.0 2.5 %shard_map.89 = (bf16[64,1280]{1,0:T(8,128)(2,1)S(1)}, bf16[64,1280]{1,0:T(8,128)(2,1)S(1)}, f32[4,8,160]{2,1,0:T(8,128)S(1)}) custom-call(bf16[4,40,1152]{2,1,0:T(8,128)(2,1)} %get-tuple-element.101.full_ref, bf16[64,3840]{1,0:T(8,128)(2,1)} %get-tuple-element.255.near_ref.cot_near_ref, bf16[64,1280]{1,0:T(8,128)(2,1)S(1)} %collective-permute-done.1.cot_far_ref, ...), custom_call_target="tpu_custom_call" | custom-call | tf_op jit(solution)/shard_map/pallas_call | solution.py:289
  111.6 2.5 %collective-permute-start.2 = (bf16[64,1280]{1,0:T(8,128)(2,1)S(1)}, bf16[64,1280]{1,0:T(8,128)(2,1)S(1)}, u32[]{:S(2)}, u32[]{:S(2)}) collective-permute-start(bf16[64,1280]{1,0:T(8,128)(2,1)S(1)} %get-tuple-element.103), channel_id=1, source_target_pairs={{0,520},{520,0},{8,512},{512,8},{1,521},{521,1},{9,513},{513,9},{2... | collective-permute-start | bytes 491528 | tf_op jit(solution)/shard_map/ppermute | solution.py:349
  114.1 6.7 %all_to_all.56.inner_ref = f32[4,8,160]{2,1,0:T(8,128)S(1)} all-to-all(f32[4,8,160]{2,1,0:T(8,128)S(1)} %get-tuple-element.104), channel_id=1, replica_groups=mesh['dh'=2,'dl'=8,'ctx'=4,'zh'=2,'y'=4,'core'=2] {'ctx'}, dimensions={0} | all-to-all | bytes 40960 | tf_op jit(solution)/shard_map/all_to_all | solution.py:350
  120.7 1.0 shard_map.90
  121.7 36.4 %while.34 = (s32[]{:T(128)}, bf16[32,8,128]{2,1,0:T(8,128)(2,1)}, s32[]{:T(128)}, s32[]{:T(128)}) while((s32[]{:T(128)}, bf16[32,8,128]{2,1,0:T(8,128)(2,1)}, s32[]{:T(128)}, s32[]{:T(128)}) %tuple.55), condition=%wide.region_5.6_spmd, body=%wide.region_4.5_spmd.sunk | while | flops 2 | bytes 327765 | solution.py:302
  121.7 12.9 %all-to-all-start.3 = ((bf16[32,8,128]{2,1,0:T(8,128)(2,1)}), bf16[32,8,128]{2,1,0:T(8,128)(2,1)S(1)}, u32[]{:S(2)}, u32[]{:S(2)}) async-start(bf16[32,8,128]{2,1,0:T(8,128)(2,1)} %get-tuple-element.284), calls=%async_computation.3 | async-start | bytes 131072 | tf_op jit(solution)/shard_map/while/body/all_to_all | solution.py:353
  134.6 22.8 %all-to-all-done.3 = bf16[32,8,128]{2,1,0:T(8,128)(2,1)S(1)} async-done(((bf16[32,8,128]{2,1,0:T(8,128)(2,1)}), bf16[32,8,128]{2,1,0:T(8,128)(2,1)S(1)}, u32[]{:S(2)}, u32[]{:S(2)}) %all-to-all-start.3) | async-done | bytes 65568 | tf_op jit(solution)/shard_map/while/body/all_to_all | solution.py:353
  158.1 0.9 shard_map.91
  159.0 17.0 %all_to_all.57 = bf16[8,8,3072]{2,1,0:T(8,128)(2,1)S(1)} all-to-all(bf16[8,8,3072]{2,1,0:T(8,128)(2,1)S(1)} %bitcast.25), channel_id=1, replica_groups=mesh['dh'=2,'dl'=8,'ctx'=4,'zh'=2,'y'=4,'core'=2] {'y','core'}, dimensions={0} | all-to-all | bytes 786432 | tf_op jit(solution)/shard_map/all_to_all | solution.py:354
  176.0 1.5 shard_map.92
  (23 shorter events, 2.3 us)
Async XLA Ops:
  0.6 1.0 copy-start.1
  1.6 0.9 copy-start.2
  2.5 0.7 copy-start.3
  4.9 51.5 %collective-permute-start = (bf16[64,1280]{1,0:T(8,128)(2,1)S(1)}, bf16[64,1280]{1,0:T(8,128)(2,1)}, u32[]{:S(2)}, u32[]{:S(2)}) collective-permute-start(bf16[64,1280]{1,0:T(8,128)(2,1)S(1)} %get-tuple-element.100), channel_id=1, source_target_pairs={{0,520},{520,0},{8,512},{512,8},{1,521},{521,1},{9,513},{513,9},{2... | collective-permute-start | bytes 491528 | tf_op jit(solution)/shard_map/ppermute | solution.py:327
  28.5 14.6 %all-to-all-start = ((bf16[8,8,3840]{2,1,0:T(8,128)(2,1)}), bf16[8,8,3840]{2,1,0:T(8,128)(2,1)S(1)}, u32[]{:S(2)}, u32[]{:S(2)}) async-start(bf16[8,8,3840]{2,1,0:T(8,128)(2,1)} %bitcast.18), calls=%async_computation | async-start | bytes 983040 | tf_op jit(solution)/shard_map/while/body/all_to_all | solution.py:328
  56.5 11.0 %all-to-all-start.4 = ((bf16[8,8,1280]{2,1,0:T(8,128)(2,1)}), bf16[8,8,1280]{2,1,0:T(8,128)(2,1)S(1)}, u32[]{:S(2)}, u32[]{:S(2)}) async-start(bf16[8,8,1280]{2,1,0:T(8,128)(2,1)} %bitcast.7), calls=%async_computation.4 | async-start | bytes 327680 | tf_op jit(solution)/shard_map/all_to_all | solution.py:329
  67.5 41.5 %collective-permute-start.1 = (bf16[64,1280]{1,0:T(8,128)(2,1)S(1)}, bf16[64,1280]{1,0:T(8,128)(2,1)S(1)}, u32[]{:S(2)}, u32[]{:S(2)}) collective-permute-start(bf16[64,1280]{1,0:T(8,128)(2,1)S(1)} %shard_map.88), channel_id=1, source_target_pairs={{0,520},{520,0},{8,512},{512,8},{1,521},{521,1},{9,513},{513,9},{2... | collective-permute-start | bytes 491528 | tf_op jit(solution)/shard_map/ppermute | solution.py:331
  80.7 28.3 %copy-start = (bf16[1,1024,1024]{2,1,0:T(8,128)(2,1)S(1)}, bf16[1,1024,1024]{2,1,0:T(8,128)(2,1)}, u32[]{:S(2)}) copy-start(bf16[1,1024,1024]{2,1,0:T(8,128)(2,1)} %param.18) | copy-start | bytes 6291460
  98.7 9.5 %all-to-all-start.2 = ((bf16[4,40,1152]{2,1,0:T(8,128)(2,1)}), bf16[4,40,1152]{2,1,0:T(8,128)(2,1)S(1)}, u32[]{:S(2)}, u32[]{:S(2)}) async-start(bf16[4,40,1152]{2,1,0:T(8,128)(2,1)} %body.3), calls=%async_computation.2 | async-start | bytes 737280 | tf_op jit(solution)/shard_map/while/body/all_to_all | solution.py:340
  108.2 0.8 copy-start.5
  109.0 11.7 %copy-start.6 = (bf16[4,40,1152]{2,1,0:T(8,128)(2,1)S(1)}, bf16[4,40,1152]{2,1,0:T(8,128)(2,1)}, u32[]{:S(2)}) copy-start(bf16[4,40,1152]{2,1,0:T(8,128)(2,1)} %get-tuple-element.101.full_ref) | copy-start | bytes 1105924
  109.0 11.7 %copy-start.7 = (bf16[160,1024]{1,0:T(8,128)(2,1)S(1)}, bf16[160,1024]{1,0:T(8,128)(2,1)}, u32[]{:S(2)}) copy-start(bf16[160,1024]{1,0:T(8,128)(2,1)} %get-tuple-element.105.x_ref) | copy-start | bytes 983044
  111.6 64.5 %copy-start.4 = (s32[128,1]{0,1:T(1,128)S(1)}, s32[128,1]{0,1:T(1,128)}, u32[]{:S(2)}) copy-start(s32[128,1]{0,1:T(1,128)} %param.14) | copy-start | bytes 1540
  111.6 46.5 %collective-permute-start.2 = (bf16[64,1280]{1,0:T(8,128)(2,1)S(1)}, bf16[64,1280]{1,0:T(8,128)(2,1)S(1)}, u32[]{:S(2)}, u32[]{:S(2)}) collective-permute-start(bf16[64,1280]{1,0:T(8,128)(2,1)S(1)} %get-tuple-element.103), channel_id=1, source_target_pairs={{0,520},{520,0},{8,512},{512,8},{1,521},{521,1},{9,513},{513,9},{2... | collective-permute-start | bytes 491528 | tf_op jit(solution)/shard_map/ppermute | solution.py:349
  121.7 35.8 %all-to-all-start.3 = ((bf16[32,8,128]{2,1,0:T(8,128)(2,1)}), bf16[32,8,128]{2,1,0:T(8,128)(2,1)S(1)}, u32[]{:S(2)}, u32[]{:S(2)}) async-start(bf16[32,8,128]{2,1,0:T(8,128)(2,1)} %get-tuple-element.284), calls=%async_computation.3 | async-start | bytes 131072 | tf_op jit(solution)/shard_map/while/body/all_to_all | solution.py:353

commit v11 on v10

--- a/solution.py
+++ b/solution.py
@@ -243,10 +243,8 @@
         total = grads_ref[zh].astype(F32)
         for k in range(1, parts):
             total = total + grads_ref[2 * k + zh].astype(F32)
-        high = total.astype(BF16)
-        low = (total - high.astype(F32)).astype(BF16)
-        for at, v in ((2 * span + zh * 128, high), (2 * span + 256 + zh * 128, low)):
-            out_ref[:, at : at + 128] = jnp.concatenate([v.astype(F32)] * HALF, axis=0).astype(BF16)
+        at = 2 * span + zh * 128
+        out_ref[:, at : at + 128] = jnp.concatenate([total] * HALF, axis=0).astype(BF16)
 
 
 def out_kernel(zh_ref, routes_ref, fin_ref, out_ref, grad_ref):
@@ -275,9 +273,8 @@
         total = jnp.zeros((N_EXP, 128), F32)
         for zh in range(2):
             take = pick((r == place * BACK + j) & ((line >= HALF) == (zh == 1)))
-            for part in range(2):
-                at = 2 * span + part * 256 + zh * 128
-                total = total + dot(take, fin_ref[:, at : at + 128])
+            at = 2 * span + zh * 128
+            total = total + dot(take, fin_ref[:, at : at + 128])
         grad_ref[:, j * 128 : (j + 1) * 128] = total
 
 
@@ -351,7 +348,7 @@
     grad = call(grad_kernel, shape((lax.axis_size(ALL_Z), 8, width // 8), BF16))(inner, full, x)
 
     (grads,) = as_one_step(turns, lambda turn, v: (lax.all_to_all(v, ALL_Z, 0, 0, tiled=True),), (grad,))
-    fin = exchange(call(merge_kernel, shape((HALF * BACK, 2 * span + 512), BF16))(near_back, far, grads))
+    fin = exchange(call(merge_kernel, shape((HALF * BACK, 2 * span + 256), BF16))(near_back, far, grads))
     block_out, grad = call(out_kernel, (shape((count, width), BF16), shape((N_EXP, width), F32)), 1)(zh, routes, fin)
     return block_out, grad.T
 

time: 178 us -> 178 us (level)
  no operation moved by 1% of the time
where the time goes in v11:
time: 178 us; the launch traced here: 177 us
  starting transfers between devices  66.2 us (37%)
  waiting for transfers between devices  52.8 us (30%)
  blocking collectives  36.7 us (21%)
  Pallas kernels  13.2 us (7%)
  local copies, waits for them, and re-layouts  6.29 us (4%)
    ppermute x1, starting transfers between devices, shards(): x_far = lax.ppermute(x_far, PAIR, PAIR_PERM)  23.5 us
    all_to_all x1, waiting for transfers between devices, shards(): lax.all_to_all(v, ALL_Z, 0, 0, tiled=True)  22.8 us
    all_to_all x1, blocking collectives, shards(): exchange(call(merge_kernel, shape((HALF * BACK, 2 * span + 256), BF16))(n...  16.7 us
    all_to_all x1, blocking collectives, to_hidden(): over_ctx(sums)  13.4 us
    pallas_call x9, Pallas kernels, run(): pl.pallas_call(kernel, in_specs=specs, out_specs=jax.tree.map(lambda _: v...  13.2 us
    ppermute x1, starting transfers between devices, shards(): cot_far = lax.ppermute(cot_far, PAIR, PAIR_PERM)  12.9 us
    all_to_all x1, starting transfers between devices, shards(): lax.all_to_all(v, ALL_Z, 0, 0, tiled=True)  12.9 us
    ppermute x1, waiting for transfers between devices, shards(): x_far = lax.ppermute(x_far, PAIR, PAIR_PERM)  12.6 us
  transfers between devices with their start and end apart: 7, of which 5 were waited for; matrix products, arithmetic and copies ran while one was open for 2% of the time, Pallas kernels for 4%

profile of v11, /device:TPU:1, one launch (start us, length us, event | category | flops | bytes accessed | tf_op | source)
XLA Modules:
  0.0 177.2 jit_solution(12751853965160882629)
XLA Ops:
  0.6 0.9 copy-done.1
  1.6 0.9 copy-done.2
  3.2 1.7 shard_map.86
  4.9 23.5 %collective-permute-start = (bf16[64,1280]{1,0:T(8,128)(2,1)S(1)}, bf16[64,1280]{1,0:T(8,128)(2,1)}, u32[]{:S(2)}, u32[]{:S(2)}) collective-permute-start(bf16[64,1280]{1,0:T(8,128)(2,1)S(1)} %get-tuple-element.100), channel_id=1, source_target_pairs={{0,520},{520,0},{8,512},{512,8},{1,521},{521,1},{9,513},{513,9},{2... | collective-permute-start | bytes 491528 | tf_op jit(solution)/shard_map/ppermute | solution.py:324
  28.5 15.4 %while.32 = (s32[]{:T(128)}, bf16[64,3840]{1,0:T(8,128)(2,1)}, s32[]{:T(128)}, s32[]{:T(128)}) while((s32[]{:T(128)}, bf16[64,3840]{1,0:T(8,128)(2,1)}, s32[]{:T(128)}, s32[]{:T(128)}) %tuple.49), condition=%wide.region_1.2_spmd, body=%wide.region_0.1_spmd.sunk | while | flops 2 | bytes 2457685 | solution.py:299
  28.5 5.4 %all-to-all-start = ((bf16[8,8,3840]{2,1,0:T(8,128)(2,1)}), bf16[8,8,3840]{2,1,0:T(8,128)(2,1)S(1)}, u32[]{:S(2)}, u32[]{:S(2)}) async-start(bf16[8,8,3840]{2,1,0:T(8,128)(2,1)} %bitcast.18), calls=%async_computation | async-start | bytes 983040 | tf_op jit(solution)/shard_map/while/body/all_to_all | solution.py:325
  33.9 9.1 %all-to-all-done = bf16[8,8,3840]{2,1,0:T(8,128)(2,1)S(1)} async-done(((bf16[8,8,3840]{2,1,0:T(8,128)(2,1)}), bf16[8,8,3840]{2,1,0:T(8,128)(2,1)S(1)}, u32[]{:S(2)}, u32[]{:S(2)}) %all-to-all-start) | async-done | bytes 491552 | tf_op jit(solution)/shard_map/while/body/all_to_all | solution.py:325
  43.1 0.8 copy.18
  43.9 12.6 %collective-permute-done = bf16[64,1280]{1,0:T(8,128)(2,1)} collective-permute-done((bf16[64,1280]{1,0:T(8,128)(2,1)S(1)}, bf16[64,1280]{1,0:T(8,128)(2,1)}, u32[]{:S(2)}, u32[]{:S(2)}) %collective-permute-start) | collective-permute-done | bytes 163872 | tf_op jit(solution)/shard_map/ppermute | solution.py:324
  56.5 5.4 %all-to-all-start.4 = ((bf16[8,8,1280]{2,1,0:T(8,128)(2,1)}), bf16[8,8,1280]{2,1,0:T(8,128)(2,1)S(1)}, u32[]{:S(2)}, u32[]{:S(2)}) async-start(bf16[8,8,1280]{2,1,0:T(8,128)(2,1)} %bitcast.7), calls=%async_computation.4 | async-start | bytes 327680 | tf_op jit(solution)/shard_map/all_to_all | solution.py:326
  61.9 0.8 dynamic_slice.12
  62.7 0.8 fusion
  64.2 1.0 shard_map.87.v_ref
  65.3 2.1 %all-to-all-done.4 = bf16[8,8,1280]{2,1,0:T(8,128)(2,1)S(1)} async-done(((bf16[8,8,1280]{2,1,0:T(8,128)(2,1)}), bf16[8,8,1280]{2,1,0:T(8,128)(2,1)S(1)}, u32[]{:S(2)}, u32[]{:S(2)}) %all-to-all-start.4) | async-done | bytes 163872 | tf_op jit(solution)/shard_map/all_to_all | solution.py:326
  67.5 12.9 %collective-permute-start.1 = (bf16[64,1280]{1,0:T(8,128)(2,1)S(1)}, bf16[64,1280]{1,0:T(8,128)(2,1)S(1)}, u32[]{:S(2)}, u32[]{:S(2)}) collective-permute-start(bf16[64,1280]{1,0:T(8,128)(2,1)S(1)} %shard_map.88), channel_id=1, source_target_pairs={{0,520},{520,0},{8,512},{512,8},{1,521},{521,1},{9,513},{513,9},{2... | collective-permute-start | bytes 491528 | tf_op jit(solution)/shard_map/ppermute | solution.py:328
  80.7 28.3 %while.33 = (s32[]{:T(128)}, bf16[160,1024]{1,0:T(8,128)(2,1)}, bf16[4,40,1152]{2,1,0:T(8,128)(2,1)}, s32[]{:T(128)}, bf16[1,1024,1024]{2,1,0:T(8,128)(2,1)}, /*...) while((s32[]{:T(128)}, bf16[160,1024]{1,0:T(8,128)(2,1)}, ...), condition=%wide.region_3.4_spmd, body=%wide.region_2.3_spmd.sunk | while | flops 2 | bytes 3973281 | solution.py:299
  80.7 3.7 %body.2 = (bf16[4,40,2176]{2,1,0:T(8,128)(2,1)S(1)}, bf16[160,1024]{1,0:T(8,128)(2,1)}) custom-call(s32[1]{0:T(128)} %bitcast.20.turn_ref, bf16[64,3840]{1,0:T(8,128)(2,1)} %get-tuple-element.275.near_ref, bf16[64,1280]{1,0:T(8,128)(2,1)S(1)} %get-tuple-element.276.far_ref, bf16[1024,128]{1,0:T(8,128)(2,1)S(1)} %get-tuple-element.277.router_ref, ...), custom_call_target="tpu_custom_call" | custom-call | tf_op jit(solution)/shard_map/while/body/pallas_call | solution.py:286
  84.4 13.4 %all_to_all.58.mine_ref = bf16[4,40,2176]{2,1,0:T(8,128)(2,1)S(1)} all-to-all(bf16[4,40,2176]{2,1,0:T(8,128)(2,1)S(1)} %get-tuple-element.233), channel_id=1, replica_groups=mesh['dh'=2,'dl'=8,'ctx'=4,'zh'=2,'y'=4,'core'=2] {'ctx'}, dimensions={0} | all-to-all | bytes 1392640 | tf_op jit(solution)/shard_map/while/body/all_to_all | solution.py:337
  97.8 0.9 body.3
  98.7 3.5 %all-to-all-start.2 = ((bf16[4,40,1152]{2,1,0:T(8,128)(2,1)}), bf16[4,40,1152]{2,1,0:T(8,128)(2,1)S(1)}, u32[]{:S(2)}, u32[]{:S(2)}) async-start(bf16[4,40,1152]{2,1,0:T(8,128)(2,1)} %body.3), calls=%async_computation.2 | async-start | bytes 737280 | tf_op jit(solution)/shard_map/while/body/all_to_all | solution.py:337
  102.2 6.1 %all-to-all-done.2 = bf16[4,40,1152]{2,1,0:T(8,128)(2,1)S(1)} async-done(((bf16[4,40,1152]{2,1,0:T(8,128)(2,1)}), bf16[4,40,1152]{2,1,0:T(8,128)(2,1)S(1)}, u32[]{:S(2)}, u32[]{:S(2)}) %all-to-all-start.2) | async-done | bytes 368672 | tf_op jit(solution)/shard_map/while/body/all_to_all | solution.py:337
  108.2 0.8 copy-done.5
  109.0 2.5 %shard_map.89 = (bf16[64,1280]{1,0:T(8,128)(2,1)S(1)}, bf16[64,1280]{1,0:T(8,128)(2,1)S(1)}, f32[4,8,160]{2,1,0:T(8,128)S(1)}) custom-call(bf16[4,40,1152]{2,1,0:T(8,128)(2,1)} %get-tuple-element.101.full_ref, bf16[64,3840]{1,0:T(8,128)(2,1)} %get-tuple-element.255.near_ref.cot_near_ref, bf16[64,1280]{1,0:T(8,128)(2,1)S(1)} %collective-permute-done.1.cot_far_ref, ...), custom_call_target="tpu_custom_call" | custom-call | tf_op jit(solution)/shard_map/pallas_call | solution.py:286
  111.6 2.5 %collective-permute-start.2 = (bf16[64,1280]{1,0:T(8,128)(2,1)S(1)}, bf16[64,1280]{1,0:T(8,128)(2,1)S(1)}, u32[]{:S(2)}, u32[]{:S(2)}) collective-permute-start(bf16[64,1280]{1,0:T(8,128)(2,1)S(1)} %get-tuple-element.103), channel_id=1, source_target_pairs={{0,520},{520,0},{8,512},{512,8},{1,521},{521,1},{9,513},{513,9},{2... | collective-permute-start | bytes 491528 | tf_op jit(solution)/shard_map/ppermute | solution.py:346
  114.1 6.7 %all_to_all.56.inner_ref = f32[4,8,160]{2,1,0:T(8,128)S(1)} all-to-all(f32[4,8,160]{2,1,0:T(8,128)S(1)} %get-tuple-element.104), channel_id=1, replica_groups=mesh['dh'=2,'dl'=8,'ctx'=4,'zh'=2,'y'=4,'core'=2] {'ctx'}, dimensions={0} | all-to-all | bytes 40960 | tf_op jit(solution)/shard_map/all_to_all | solution.py:347
  120.7 1.0 shard_map.90
  121.7 36.4 %while.34 = (s32[]{:T(128)}, bf16[32,8,128]{2,1,0:T(8,128)(2,1)}, s32[]{:T(128)}, s32[]{:T(128)}) while((s32[]{:T(128)}, bf16[32,8,128]{2,1,0:T(8,128)(2,1)}, s32[]{:T(128)}, s32[]{:T(128)}) %tuple.55), condition=%wide.region_5.6_spmd, body=%wide.region_4.5_spmd.sunk | while | flops 2 | bytes 327765 | solution.py:299
  121.7 12.9 %all-to-all-start.3 = ((bf16[32,8,128]{2,1,0:T(8,128)(2,1)}), bf16[32,8,128]{2,1,0:T(8,128)(2,1)S(1)}, u32[]{:S(2)}, u32[]{:S(2)}) async-start(bf16[32,8,128]{2,1,0:T(8,128)(2,1)} %get-tuple-element.284), calls=%async_computation.3 | async-start | bytes 131072 | tf_op jit(solution)/shard_map/while/body/all_to_all | solution.py:350
  134.6 22.8 %all-to-all-done.3 = bf16[32,8,128]{2,1,0:T(8,128)(2,1)S(1)} async-done(((bf16[32,8,128]{2,1,0:T(8,128)(2,1)}), bf16[32,8,128]{2,1,0:T(8,128)(2,1)S(1)}, u32[]{:S(2)}, u32[]{:S(2)}) %all-to-all-start.3) | async-done | bytes 65568 | tf_op jit(solution)/shard_map/while/body/all_to_all | solution.py:350
  158.1 0.9 shard_map.91
  159.0 16.7 %all_to_all.57 = bf16[8,8,2816]{2,1,0:T(8,128)(2,1)S(1)} all-to-all(bf16[8,8,2816]{2,1,0:T(8,128)(2,1)S(1)} %bitcast.25), channel_id=1, replica_groups=mesh['dh'=2,'dl'=8,'ctx'=4,'zh'=2,'y'=4,'core'=2] {'y','core'}, dimensions={0} | all-to-all | bytes 720896 | tf_op jit(solution)/shard_map/all_to_all | solution.py:351
  175.7 1.5 shard_map.92
  (23 shorter events, 2.3 us)
Async XLA Ops:
  0.6 1.0 copy-start.1
  1.6 0.9 copy-start.2
  2.5 0.7 copy-start.3
  4.9 51.5 %collective-permute-start = (bf16[64,1280]{1,0:T(8,128)(2,1)S(1)}, bf16[64,1280]{1,0:T(8,128)(2,1)}, u32[]{:S(2)}, u32[]{:S(2)}) collective-permute-start(bf16[64,1280]{1,0:T(8,128)(2,1)S(1)} %get-tuple-element.100), channel_id=1, source_target_pairs={{0,520},{520,0},{8,512},{512,8},{1,521},{521,1},{9,513},{513,9},{2... | collective-permute-start | bytes 491528 | tf_op jit(solution)/shard_map/ppermute | solution.py:324
  28.5 14.6 %all-to-all-start = ((bf16[8,8,3840]{2,1,0:T(8,128)(2,1)}), bf16[8,8,3840]{2,1,0:T(8,128)(2,1)S(1)}, u32[]{:S(2)}, u32[]{:S(2)}) async-start(bf16[8,8,3840]{2,1,0:T(8,128)(2,1)} %bitcast.18), calls=%async_computation | async-start | bytes 983040 | tf_op jit(solution)/shard_map/while/body/all_to_all | solution.py:325
  56.5 11.0 %all-to-all-start.4 = ((bf16[8,8,1280]{2,1,0:T(8,128)(2,1)}), bf16[8,8,1280]{2,1,0:T(8,128)(2,1)S(1)}, u32[]{:S(2)}, u32[]{:S(2)}) async-start(bf16[8,8,1280]{2,1,0:T(8,128)(2,1)} %bitcast.7), calls=%async_computation.4 | async-start | bytes 327680 | tf_op jit(solution)/shard_map/all_to_all | solution.py:326
  67.5 41.5 %collective-permute-start.1 = (bf16[64,1280]{1,0:T(8,128)(2,1)S(1)}, bf16[64,1280]{1,0:T(8,128)(2,1)S(1)}, u32[]{:S(2)}, u32[]{:S(2)}) collective-permute-start(bf16[64,1280]{1,0:T(8,128)(2,1)S(1)} %shard_map.88), channel_id=1, source_target_pairs={{0,520},{520,0},{8,512},{512,8},{1,521},{521,1},{9,513},{513,9},{2... | collective-permute-start | bytes 491528 | tf_op jit(solution)/shard_map/ppermute | solution.py:328
  80.7 28.3 %copy-start = (bf16[1,1024,1024]{2,1,0:T(8,128)(2,1)S(1)}, bf16[1,1024,1024]{2,1,0:T(8,128)(2,1)}, u32[]{:S(2)}) copy-start(bf16[1,1024,1024]{2,1,0:T(8,128)(2,1)} %param.18) | copy-start | bytes 6291460
  98.7 9.5 %all-to-all-start.2 = ((bf16[4,40,1152]{2,1,0:T(8,128)(2,1)}), bf16[4,40,1152]{2,1,0:T(8,128)(2,1)S(1)}, u32[]{:S(2)}, u32[]{:S(2)}) async-start(bf16[4,40,1152]{2,1,0:T(8,128)(2,1)} %body.3), calls=%async_computation.2 | async-start | bytes 737280 | tf_op jit(solution)/shard_map/while/body/all_to_all | solution.py:337
  108.2 0.8 copy-start.5
  109.0 11.7 %copy-start.6 = (bf16[4,40,1152]{2,1,0:T(8,128)(2,1)S(1)}, bf16[4,40,1152]{2,1,0:T(8,128)(2,1)}, u32[]{:S(2)}) copy-start(bf16[4,40,1152]{2,1,0:T(8,128)(2,1)} %get-tuple-element.101.full_ref) | copy-start | bytes 1105924
  109.0 11.7 %copy-start.7 = (bf16[160,1024]{1,0:T(8,128)(2,1)S(1)}, bf16[160,1024]{1,0:T(8,128)(2,1)}, u32[]{:S(2)}) copy-start(bf16[160,1024]{1,0:T(8,128)(2,1)} %get-tuple-element.105.x_ref) | copy-start | bytes 983044
  111.6 64.1 %copy-start.4 = (s32[128,1]{0,1:T(1,128)S(1)}, s32[128,1]{0,1:T(1,128)}, u32[]{:S(2)}) copy-start(s32[128,1]{0,1:T(1,128)} %param.14) | copy-start | bytes 1540
  111.6 46.5 %collective-permute-start.2 = (bf16[64,1280]{1,0:T(8,128)(2,1)S(1)}, bf16[64,1280]{1,0:T(8,128)(2,1)S(1)}, u32[]{:S(2)}, u32[]{:S(2)}) collective-permute-start(bf16[64,1280]{1,0:T(8,128)(2,1)S(1)} %get-tuple-element.103), channel_id=1, source_target_pairs={{0,520},{520,0},{8,512},{512,8},{1,521},{521,1},{9,513},{513,9},{2... | collective-permute-start | bytes 491528 | tf_op jit(solution)/shard_map/ppermute | solution.py:346
  121.7 35.8 %all-to-all-start.3 = ((bf16[32,8,128]{2,1,0:T(8,128)(2,1)}), bf16[32,8,128]{2,1,0:T(8,128)(2,1)S(1)}, u32[]{:S(2)}, u32[]{:S(2)}) async-start(bf16[32,8,128]{2,1,0:T(8,128)(2,1)} %get-tuple-element.284), calls=%async_computation.3 | async-start | bytes 131072 | tf_op jit(solution)/shard_map/while/body/all_to_all | solution.py:350
